TPU v7x, 256 devices: a whole 4x4x8 slice. The times are simulated.
256 devices in a mesh: wide: 64 (over z, x, core), rep: 4 (over y).
Axes of the slice: x: 4, y: 4, z: 8, core: 2. Of those that a mesh axis runs over, the one named last changes fastest.
Arguments:
- factor: float32 [32, 1024, 4096], P(None, 'wide'), may hold values from -0.09375 to 0.09375
- inverses: float32 [4, 1, 1024, 1024], P(None, None, 'wide'), as said below
- right_side: float32 [32, 1024, 512], P(None, 'wide', 'rep'), may hold values from -6 to 6
- obs_cells: int32 [4096], replicated, may hold values from 0 to 8388607
- noise: float32 [1024, 4, 8, 1024], P('wide', None, 'rep'), may hold values from -6 to 6
- spectrum: float32 [1024, 8, 1024], P(None, 'rep', 'wide'), may hold values from 0.25 to 4, as said below
Outputs:
- solved: float32 [32, 1024, 512], P(None, 'wide', 'rep')
- correction: float32 [1024, 4, 8, 1024], P('wide', None, 'rep')
Inputs may be any that keep to these rules, and one draw needn't show every extreme that they name: `inverses`: each D_k is lower triangular. spectrum[x, y, z] equals spectrum[(1024 - x) % 1024, y, (1024 - z) % 1024].
All inputs are finite; a program needn't handle non-finite values.
Results may differ from a plain program's by a relative error of at most 0.0001.
Values sent between devices are 32-bit elements; how exact they have to be, the bound alone decides.
No kernel may reach another device: no remote copies, remote signals or barrier semaphores. Data moves between devices by JAX's collectives and lax.ppermute only.
A program may use at most 192 MiB of HBM per device.

v0:
```python
import functools
import math

import jax
import jax.numpy as jnp
import numpy as np
from jax import lax
from jax.experimental import pallas as pl
from jax.experimental.pallas import tpu as pltpu
from jax.sharding import Mesh, PartitionSpec as P

F32 = jnp.float32
BF16 = jnp.bfloat16
WIDE = ("z", "x", "core")
LENGTH = 1024
COLS = 24
NN = (((1,), (0,)), ((), ()))
NT = (((1,), (1,)), ((), ()))
LIMIT = pltpu.CompilerParams(vmem_limit_bytes=56 * 1024 * 1024)


def halves(table):
    high = table.astype(np.float32).astype(jnp.bfloat16)
    low = (table - high.astype(np.float64)).astype(np.float32).astype(jnp.bfloat16)
    return (np.asarray(high), np.asarray(low))


def z_frequencies(owner, xp):
    step = xp.arange(16) % 8
    part = xp.arange(16) // 8
    freq = 16 * owner + step + xp.where(owner >= 32, 1, 0)
    lone = (owner == 0) & (step == 0) & (part == 1)
    return (xp.where(lone, 512, freq), xp.where(lone, 0, 256 * part))


def z_table():
    rows = []
    cells = np.arange(LENGTH)
    for owner in range(64):
        freq, phase = z_frequencies(np.int64(owner), np)
        turn = (freq[:, None] * cells[None, :] + phase[:, None]) % LENGTH
        rows.append(np.cos(2.0 * np.pi * turn / LENGTH))
    return np.concatenate(rows)


def x_table():
    cells = np.arange(LENGTH)
    freq = np.concatenate([np.arange(512), np.arange(512)])
    phase = np.repeat([0, 256], 512)
    freq[512], phase[512] = 512, 0
    turn = (freq[:, None] * cells[None, :] + phase[:, None]) % LENGTH
    return np.cos(2.0 * np.pi * turn / LENGTH)


def split(value):
    high = value.astype(BF16)
    low = (value - high.astype(F32)).astype(BF16)
    return (high, low)


def dot(left, right, dims):
    return lax.dot_general(left, right, dims, preferred_element_type=F32)


def dot_nt(left, right):
    left_high, left_low = split(left)
    right_high, right_low = split(right)
    rows = left.shape[0]
    both = dot(jnp.concatenate([left_high, left_low]), right_high, NT)
    return both[:rows] + both[rows:] + dot(left_high, right_low, NT)


def table_nn(high, low, value):
    value_high, value_low = split(value)
    cols = value.shape[1]
    both = dot(high, jnp.concatenate([value_high, value_low], axis=1), NN)
    return both[:, :cols] + both[:, cols:] + dot(low, value_high, NN)


def swap_groups(value):
    row = lax.broadcasted_iota(jnp.int32, value.shape, 0)
    lane = lax.broadcasted_iota(jnp.int32, value.shape, 1)
    for bit in range(4):
        step = 1 << bit
        row_bit = (row >> bit) & 1
        lane_bit = (lane >> (3 + bit)) & 1
        up = pltpu.roll(pltpu.roll(value, LENGTH - step, 0), 8 * step, 1)
        down = pltpu.roll(pltpu.roll(value, step, 0), 128 - 8 * step, 1)
        value = jnp.where(row_bit == lane_bit, value, jnp.where(lane_bit == 1, up, down))
    return value


def columns_kernel(inverse_ref, right_ref, out_ref, side_ref):
    side_ref[...] = right_ref[...].reshape(64, 128)
    lane = lax.broadcasted_iota(jnp.int32, (64, 128), 1) // 16
    for r in range(8):
        total = jnp.zeros((64, 128), F32)
        for z in range(8):
            piece = inverse_ref[:, 128 * z : 128 * z + 128]
            piece = pltpu.roll(piece, (16 * (z - r)) % 128, 1) if z != r else piece
            total = jnp.where(lane == z, piece, total)
        out_ref[r] = total


def noise_kernel(noise_ref, high_ref, low_ref, out_ref):
    noise_high, noise_low = split(noise_ref[...])
    both = dot(high_ref[...], jnp.concatenate([noise_high, noise_low]), NT)
    slots = both[:, :128] + both[:, 128:] + dot(low_ref[...], noise_high, NT)
    out_ref[...] = slots.reshape(16, 16, 128)


def lower_kernel(one_ref, two_ref, three_ref, out_ref):
    place = 0
    for k, ref in enumerate((one_ref, two_ref, three_ref)):
        for j in range(k + 1):
            out_ref[16 * place : 16 * place + 16] = ref[0, :, LENGTH * j : LENGTH * (j + 1)]
            place += 1


def bundle_kernel(index_ref, columns_ref, *refs):
    side_refs, (near_ref, far_ref) = refs[:4], refs[4:]
    lane = lax.broadcasted_iota(jnp.int32, (64, 128), 1)
    weights = jnp.zeros((64, 128), F32)
    for step, ref in enumerate(side_refs):
        y = lax.rem(index_ref[1] + 4 - step, 4)
        weights = jnp.where(lane == y + 16, ref[:, 0:1], weights)
    side = side_refs[0][...]
    inverses = [columns_ref[:, 16 * k : 16 * k + 16, :].reshape(128, 128) for k in range(4)]
    for z in range(8):
        own = pltpu.roll(side, (128 - 16 * z) % 128, 1) if z else side
        rows = jnp.where(lane < 16, own, weights)
        for k in range(2):
            near_ref[z, 128 * k : 128 * k + 128] = inverses[k]
            far_ref[z, 128 * k : 128 * k + 128] = inverses[2 + k]
        near_ref[z, 256:288] = jnp.transpose(jnp.concatenate([rows, rows]))[:32]


def spread(work, inverse_ref, out_ref):
    high, low = split(work)
    rows_high, rows_low = split(inverse_ref[...].reshape(LENGTH, 128))
    wide = dot(jnp.concatenate([high, low]), rows_high, NT)
    out_ref[...] = wide[:COLS] + wide[COLS:] + dot(high, rows_low, NT)


def first_kernel(near_ref, side_near_ref, out_ref, side_ref):
    lane = lax.broadcasted_iota(jnp.int32, (COLS, 128), 1) // 16
    for k in range(4):
        rows = jnp.zeros((COLS, 128), F32)
        for z in range(8):
            piece = side_near_ref[z, 0:COLS]
            turn = (16 * (z - k)) % 128
            piece = pltpu.roll(piece, turn, 1) if turn else piece
            rows = jnp.where(lane == z, piece, rows)
        side_ref[k] = rows
    spread(side_ref[0], near_ref, out_ref)


def step_kernel(start_ref, a_ref, b_ref, c_ref, d_ref, factor_ref, inverse_ref, out_ref, unknown_ref):
    unknown = (a_ref[...] + b_ref[...]) + (c_ref[...] + d_ref[...])
    unknown_ref[...] = unknown
    work = start_ref[0] - dot_nt(unknown, factor_ref[...].reshape(128, LENGTH))
    spread(work, inverse_ref, out_ref)


def spectrum_kernel(index_ref, spectrum_ref, extra_ref, even_ref, odd_ref):
    owner = index_ref[0]
    row = lax.broadcasted_iota(jnp.int32, (32, 128), 0)
    lane = lax.broadcasted_iota(jnp.int32, (32, 128), 1)
    lone = (owner == 0) & (lane // 8 == 8)
    same_y = row // 16 == lane % 2
    same_z = row % 16 == (lane // 8) % 8 + jnp.where(owner >= 32, 1, 0)
    pick = jnp.where(same_y & same_z & jnp.logical_not(lone), 1.0, 0.0).astype(BF16)
    extra_pick = jnp.where(lone & (row == lane % 2), 1.0, 0.0)[:8].astype(BF16)

    def exact(value, choose):
        high = value.astype(BF16)
        rest = value - high.astype(F32)
        middle = rest.astype(BF16)
        low = (rest - middle.astype(F32)).astype(BF16)
        return choose(high) + (choose(middle) + choose(low))

    wanted = exact(spectrum_ref[...], lambda part: dot(part, pick, NN))
    wanted = wanted + exact(
        jnp.transpose(extra_ref[...]), lambda part: dot(part, extra_pick, NN)
    )
    at_row = lax.broadcasted_iota(jnp.int32, (512, 512), 0)
    at_col = lax.broadcasted_iota(jnp.int32, (512, 512), 1)
    mirror = jnp.where(at_row + at_col == 512, 1.0, 0.0).astype(BF16)
    plus = wanted[:512]
    upper = wanted[512:]
    minus = exact(upper, lambda part: dot(mirror, part, NN))
    first = lax.broadcasted_iota(jnp.int32, (512, 128), 0) == 0
    minus = jnp.where(first, plus, minus)
    lanes = lax.broadcasted_iota(jnp.int32, (512, 128), 1)
    alone = (owner == 0) & ((lanes // 8) % 8 == 0)
    scale = jnp.where(first, 1.0, 2.0) * jnp.where(alone, 1.0, 2.0) / (LENGTH * LENGTH)
    even = (plus + minus) * (0.5 * scale)
    even_ref[0:512] = even
    even_ref[512:1024] = jnp.where(first, upper * scale, even)
    odd = (plus - minus) * (0.5 * scale)
    odd_ref[...] = jnp.where(lanes < 64, -odd, odd)


def add_weights(pencil, cell_ref, wave_ref, plane_ref, weights):
    doubled = jnp.concatenate(
        [weights[g : g + 1] * plane_ref[y : y + 1] for g in range(4) for y in range(2)]
    )
    waves = (wave_ref[...][:, None, :] * doubled[None]).reshape(128, LENGTH)
    cells = lax.broadcasted_iota(jnp.int32, (LENGTH, LENGTH), 0)
    chosen = jnp.where(cells == cell_ref[...], 1.0, 0.0).astype(BF16)
    high, low = split(waves)
    both = dot(chosen, jnp.concatenate([high, low]), NT)
    return pencil + both[:, :128] + both[:, 128:]


def wait_kernel(panel, *refs):
    cell_ref, wave_ref, plane_ref, pencil_ref = refs[:4]
    unknown_refs, refs = refs[4 : 4 + panel], refs[4 + panel :]
    weights = unknown_refs[-1][16:20]
    pencil = 0.0 if panel == 1 else pencil_ref[...]
    if panel == 3:
        pencil = pencil + swap_groups(refs[0][...].reshape(LENGTH, 128))
        refs[1][...] = add_weights(pencil, cell_ref, wave_ref, plane_ref, weights)
        return
    side_ref, factor_refs, (out_ref, work_ref) = refs[0], refs[1:-2], refs[-2:]
    out_ref[...] = add_weights(pencil, cell_ref, wave_ref, plane_ref, weights)
    work = side_ref[0]
    for ref, factor_ref in zip(unknown_refs, factor_refs):
        work = work - dot_nt(ref[...], factor_ref[...].reshape(128, LENGTH))
    work_ref[0] = work


def filter_kernel(
    pencil_ref, cell_ref, wave_ref, plane_ref, a_ref, b_ref, c_ref, d_ref,
    high_hbm, low_hbm, back_high_hbm, back_low_hbm, even_ref, odd_ref, out_ref,
    high_ref, low_ref, back_high_ref, back_low_ref, sems,
):
    sources = (high_hbm, low_hbm, back_high_hbm, back_low_hbm)
    places = (high_ref, low_ref, back_high_ref, back_low_ref)
    copies = [
        pltpu.make_async_copy(source, place, sems.at[number])
        for number, (source, place) in enumerate(zip(sources, places))
    ]
    for copy in copies:
        copy.start()
    weights = (a_ref[16:20] + b_ref[16:20]) + (c_ref[16:20] + d_ref[16:20])
    pencil = add_weights(pencil_ref[...], cell_ref, wave_ref, plane_ref, weights)
    copies[0].wait()
    copies[1].wait()
    freq = table_nn(high_ref[...], low_ref[...], pencil)
    real, imag = freq[:512], freq[512:]
    odd = odd_ref[...]
    real_out = even_ref[0:512] * real + odd * pltpu.roll(imag, 64, 1)
    imag_out = even_ref[512:1024] * imag - odd * pltpu.roll(real, 64, 1)
    copies[2].wait()
    copies[3].wait()
    back = table_nn(
        back_high_ref[...], back_low_ref[...], jnp.concatenate([real_out, imag_out])
    )
    out_ref[...] = swap_groups(back).reshape(64, 16, 128)


def close_kernel(slots_ref, high_ref, low_ref, out_ref, rows_ref):
    @pl.when(pl.program_id(0) == 0)
    def _():
        rows = jnp.transpose(slots_ref[...].reshape(LENGTH, 128))
        rows_high, rows_low = split(rows)
        rows_ref[0:128] = rows_high
        rows_ref[128:256] = rows_low

    both = dot(rows_ref[...], high_ref[...], NN)
    total = both[:128] + both[128:] + dot(rows_ref[0:128], low_ref[...], NN)
    out_ref[...] = total.reshape(out_ref.shape)


def update_kernel(
    first_panel, panels, index_ref, base_ref, factor_ref, unknown_ref, out_ref, high_ref, low_ref
):
    block = pl.program_id(0)

    @pl.when(block == 0)
    def _():
        for k in range(panels):
            high, low = split(unknown_ref[:, 16 * k : 16 * k + 16, :].reshape(128, LENGTH))
            high_ref[k] = high
            low_ref[k] = low

    own = index_ref[0] * 16
    row = lax.broadcasted_iota(jnp.int32, (128, LENGTH), 0) + block * 128
    col = lax.broadcasted_iota(jnp.int32, (128, LENGTH), 1)
    base = base_ref[...].reshape(128, 128)
    if first_panel == 0:
        base_row = lax.broadcasted_iota(jnp.int32, (128, 128), 0) + block * 128
        base = jnp.where(base_row < 64, 0.0, base)
    for step in range(panels):
        panel = first_panel + step
        rows = factor_ref[:, :, LENGTH * step : LENGTH * (step + 1)].reshape(128, LENGTH)
        mine = (row // 16 == panel) & (col == own + row % 16)
        rows = jnp.where(row < 64, jnp.where(mine, -1.0, 0.0), rows)
        rows_high, rows_low = split(rows)
        wide = dot(jnp.concatenate([rows_high, rows_low]), high_ref[step], NT)
        base = base - (wide[:128] + wide[128:] + dot(rows_high, low_ref[step], NT))
    out_ref[...] = base.reshape(8, 16, 128)


def spec(*shape):
    return pl.BlockSpec(shape, lambda *_: (0,) * len(shape))


def block_at(shape, place):
    return pl.BlockSpec(shape, lambda *_: place)


def cost(flops, moved):
    return pl.CostEstimate(flops=flops, bytes_accessed=moved, transcendentals=0)


def shape_of(*shape):
    return jax.ShapeDtypeStruct(shape, F32)


def call(body, name, in_specs, out_specs, out_shape, flops, moved, scratch=(), grid=1):
    return pl.pallas_call(
        body,
        grid=(grid,),
        in_specs=in_specs,
        out_specs=out_specs,
        out_shape=out_shape,
        scratch_shapes=scratch,
        compiler_params=LIMIT,
        cost_estimate=cost(flops, moved),
        name=name,
    )


def ring(size, step):
    return [(place, (place + step) % size) for place in range(size)]


def share(partial):
    total = partial + lax.ppermute(partial, "core", ring(2, 1))
    return [total] + [lax.ppermute(total, "x", ring(4, step)) for step in (1, 2, 3)]


def tie(*groups):
    flat = lax.optimization_barrier(tuple(group[at] for group, ats in groups for at in ats))
    flat = list(flat)
    for group, ats in groups:
        for at in ats:
            group[at] = flat.pop(0)


def update(first_panel, panels, index, base, factor, unknowns):
    return call(
        functools.partial(update_kernel, first_panel, panels),
        "update",
        [
            SMEM,
            pl.BlockSpec((8, 16, 128), lambda i: (i, 0, 0)),
            pl.BlockSpec((8, 16, panels * LENGTH), lambda i: (i, 0, first_panel // panels)),
        ]
        + [spec(8, 16 * panels, LENGTH)],
        pl.BlockSpec((8, 16, 128), lambda i: (i, 0, 0)),
        shape_of(32, 16, 128),
        3 * 2 * 512 * panels * LENGTH * 128,
        2_700_000 * panels,
        [pltpu.VMEM((panels, 128, LENGTH), BF16)] * 2,
        grid=4,
    )(index, base, factor, unknowns)


SMEM = pl.BlockSpec(memory_space=pltpu.SMEM)
ANY = pl.BlockSpec(memory_space=pl.ANY)
TABLE = pltpu.VMEM((LENGTH, LENGTH), BF16)


def per_device(factor, inverses, right_side, obs_cells, noise, spectrum):
    z_high, z_low = (jnp.asarray(t) for t in halves(z_table()))
    x_high, x_low = (jnp.asarray(t) for t in halves(x_table()))
    back_high, back_low = (jnp.asarray(t) for t in halves(x_table().T))
    wide = lax.axis_index(WIDE).astype(jnp.int32)
    index = jnp.stack([wide, lax.axis_index("y").astype(jnp.int32)])

    columns, side = call(
        columns_kernel,
        "columns",
        [spec(64, LENGTH), spec(4, 16, 128)],
        [spec(8, 64, 128), spec(64, 128)],
        [shape_of(8, 64, 128), shape_of(64, 128)],
        0,
        500_000,
    )(inverses.reshape(64, LENGTH), right_side)
    box = [columns, side, spectrum, factor]
    tie((box, (0, 1, 2, 3)))
    columns, side, spectrum, factor = box
    columns = lax.all_to_all(columns, ("x", "core"), 0, 0)

    lower = call(
        lower_kernel,
        "lower",
        [block_at((1, 16, LENGTH * k), (k, 0, 0)) for k in range(1, 4)],
        spec(96, LENGTH),
        shape_of(96, LENGTH),
        0,
        800_000,
    )(factor, factor, factor)
    lower = lax.all_gather(lower, "z")

    sides = [side] + [lax.ppermute(side, "y", ring(4, step)) for step in (1, 2, 3)]
    near, far = call(
        bundle_kernel,
        "bundle",
        [SMEM, spec(8, 64, 128)] + [spec(64, 128)] * 4,
        [spec(8, 288, 128), spec(8, 256, 128)],
        [shape_of(8, 288, 128), shape_of(8, 256, 128)],
        0,
        2_500_000,
    )(index, columns, *sides)
    box = [near, far, noise, spectrum, obs_cells]
    tie((box, (0, 1, 2, 3, 4)))
    near, far, noise, spectrum, obs_cells = box
    near = lax.all_to_all(near, "z", 0, 0)
    extra = lax.ppermute(spectrum[:, :, 0].T, WIDE, [(32, 0)])

    slab = call(
        noise_kernel,
        "noise",
        [spec(128, LENGTH)] + [pl.BlockSpec((256, LENGTH), lambda i: (i, 0))] * 2,
        pl.BlockSpec((16, 16, 128), lambda i: (i, 0, 0)),
        shape_of(64, 16, 128),
        3 * 2 * 128 * LENGTH * LENGTH,
        5_000_000,
        grid=4,
    )(noise.reshape(128, LENGTH), z_high, z_low)

    extra = jnp.concatenate([extra, jnp.zeros((6, LENGTH), F32)])
    even, odd = call(
        spectrum_kernel,
        "spectrum",
        [SMEM, spec(LENGTH, 32), spec(8, LENGTH)],
        [spec(LENGTH, 128), spec(512, 128)],
        [shape_of(LENGTH, 128), shape_of(512, 128)],
        300_000_000,
        1_500_000,
    )(index, spectrum.reshape(LENGTH, 32), extra)

    cell_x = (obs_cells // (8 * LENGTH)).reshape(1, 4096)
    plane = obs_cells // LENGTH % 8 - 2 * lax.axis_index("y")
    planes = jnp.stack([plane == 0, plane == 1]).astype(F32)
    freq, phase = z_frequencies(wide, jnp)
    turn = (freq[:, None] * (obs_cells % LENGTH)[None, :] + phase[:, None]) % LENGTH
    waves = jnp.cos(turn.astype(F32) * (2.0 * math.pi / LENGTH))
    box = [near, slab, even, odd, cell_x, planes, waves]
    tie((box, tuple(range(7))))
    near, slab, even, odd, cell_x, planes, waves = box

    obs_specs = lambda k: [
        block_at((1, LENGTH), (0, k)),
        block_at((16, LENGTH), (0, k)),
        block_at((2, LENGTH), (0, k)),
    ]
    side_spec = lambda k: block_at((1, COLS, 128), (k, 0, 0))
    factor_spec = lambda k, j: block_at((8, 16, LENGTH), (0, k * (k - 1) // 2 + j, 0))
    inverse_spec = lambda k: block_at((8, 128, 128), (0, k % 2, 0))
    panel_spec = spec(COLS, LENGTH)
    panel_shape = shape_of(COLS, LENGTH)
    pencil_spec = spec(LENGTH, 128)

    partial, sides = call(
        first_kernel,
        "first",
        [inverse_spec(0), block_at((8, 32, 128), (0, 8, 0))],
        [panel_spec, spec(4, COLS, 128)],
        [panel_shape, shape_of(4, COLS, 128)],
        20_000_000,
        1_200_000,
    )(near, near)
    parts = share(partial)
    box = [far]
    tie((parts, (1,)), (box, (0,)))
    far = lax.all_to_all(box[0], "z", 0, 0)
    unknowns = []
    work = sides
    pencil = waves
    for panel in range(1, 4):
        partial, unknown = call(
            step_kernel,
            f"step{panel}",
            [side_spec(1 if panel == 1 else 0)]
            + [panel_spec] * 4
            + [factor_spec(panel, panel - 1), inverse_spec(panel)],
            [panel_spec] * 2,
            [panel_shape] * 2,
            40_000_000,
            1_500_000,
        )(work, *parts, lower, near if panel == 1 else far)
        unknowns.append(unknown)
        parts = share(partial)
        if panel == 1:
            box = [slab]
            tie((parts, (1,)), (box, (0,)))
            slab = lax.all_to_all(box[0], WIDE, 0, 0)
        if panel == 2:
            early = lax.all_gather(jnp.concatenate([u[:16] for u in unknowns]), "z")
        later = panel < 3
        box = list(
            call(
                functools.partial(wait_kernel, panel),
                f"wait{panel}",
                obs_specs(panel - 1)
                + [spec(16, 128) if panel == 1 else pencil_spec]
                + [panel_spec] * panel
                + ([side_spec(panel + 1)] if later else [spec(64, 16, 128)])
                + [factor_spec(panel + 1, j) for j in range(panel)] * later,
                [pencil_spec] + [spec(1, COLS, 128)] * later,
                [shape_of(LENGTH, 128)] + [shape_of(1, COLS, 128)] * later,
                2 * 2 * 128 * LENGTH * LENGTH,
                1_500_000,
            )(
                cell_x, waves, planes, pencil, *unknowns, sides if later else slab,
                *[lower] * (panel * later),
            )
        )
        tie((parts, (0, 1, 2, 3)), (box, (0, 1) if later else (0,)))
        pencil, work = box[0], box[-1]

    slots = call(
        filter_kernel,
        "filter",
        [spec(LENGTH, 128)]
        + obs_specs(3)
        + [panel_spec] * 4
        + [ANY] * 4
        + [spec(LENGTH, 128), spec(512, 128)],
        spec(64, 16, 128),
        shape_of(64, 16, 128),
        8 * 2 * 128 * LENGTH * LENGTH,
        11_000_000,
        [TABLE] * 4 + [pltpu.SemaphoreType.DMA((4,))],
    )(pencil, cell_x, waves, planes, *parts, x_high, x_low, back_high, back_low, even, odd)
    late = (parts[0][:16] + parts[1][:16]) + (parts[2][:16] + parts[3][:16])
    late = lax.all_gather(jnp.concatenate([unknowns[2][:16], late]), "z")
    slots = lax.all_to_all(slots, WIDE, 0, 0)
    solved = update(0, 2, index, right_side, factor, early)
    slots, solved = lax.optimization_barrier((slots, solved))
    correction = call(
        close_kernel,
        "close",
        [spec(64, 16, 128)] + [pl.BlockSpec((LENGTH, 256), lambda i: (0, i))] * 2,
        pl.BlockSpec((16, 4, 2, 256), lambda i: (0, 0, 0, i)),
        shape_of(16, 4, 2, LENGTH),
        3 * 2 * 128 * LENGTH * LENGTH,
        5_500_000,
        [pltpu.VMEM((256, LENGTH), BF16)],
        grid=4,
    )(slots, z_high, z_low)
    solved, correction = lax.optimization_barrier((solved, correction))
    solved = update(2, 2, index, solved, factor, late)
    return (solved, correction)


def solution(mesh):
    grid = Mesh(mesh.devices.reshape(8, 4, 2, 4), ("z", "x", "core", "y"))
    return jax.shard_map(
        per_device,
        mesh=grid,
        in_specs=(
            P(None, WIDE, None),
            P(None, None, WIDE, None),
            P(None, WIDE, "y"),
            P(),
            P(WIDE, None, "y", None),
            P(None, "y", WIDE),
        ),
        out_specs=(P(None, WIDE, "y"), P(WIDE, None, "y", None)),
        check_vma=False,
    )
```

profile of v0, /device:TPU:1, one launch (start us, length us, event | category | flops | bytes accessed | tf_op | source)
XLA Modules:
  0.0 228.9 jit_solution(15570448065940726733)
XLA Ops:
  11.2 6.7 %all-to-all-start = ((f32[8,64,128]{2,1,0:T(8,128)}), f32[8,64,128]{2,1,0:T(8,128)S(1)}, u32[]{:S(2)}, u32[]{:S(2)}) async-start(f32[8,64,128]{2,1,0:T(8,128)} %get-tuple-element.63), calls=%async_computation | async-start | bytes 524288 | tf_op jit(solution)/shard_map/all_to_all | solution.py:396
  18.5 2.6 %collective-permute-start.1 = (f32[64,128]{1,0:T(8,128)S(1)}, f32[64,128]{1,0:T(8,128)S(1)}, u32[]{:S(2)}, u32[]{:S(2)}) collective-permute-start(f32[64,128]{1,0:T(8,128)S(1)} %copy-done.24), channel_id=1, source_target_pairs={{0,2},{1,3},{2,0},{3,1},{4,6},{5,7},{6,4},{7,5},{8,10},{9,11},{10,... | collective-permute-start | bytes 98312 | tf_op jit(solution)/shard_map/ppermute | solution.py:409
  25.5 2.6 %bundle.1 = (f32[8,288,128]{2,1,0:T(8,128)}, f32[8,256,128]{2,1,0:T(8,128)}) custom-call(s32[2]{0:T(128)} %pad_add_fusion.index_ref, f32[8,64,128]{2,1,0:T(8,128)} %copy-done.4, f32[64,128]{1,0:T(8,128)} %get-tuple-element.64.refs_0_, f32[64,128]{1,0:T(8,128)} %copy-done.25, f32[64,128]{1,0:T(8,128)} %copy-done.26, f32[64,128]{1,0:T(8,128)} %copy-done.27), custom_call_target="tpu_custom_call" | custom-call | bytes 2500000 | tf_op jit(solution)/shard_map/bundle/pallas_call | solution.py:410
  28.1 8.2 %all-to-all-start.1 = ((f32[8,288,128]{2,1,0:T(8,128)}), f32[8,288,128]{2,1,0:T(8,128)S(1)}, u32[]{:S(2)}, u32[]{:S(2)}) async-start(f32[8,288,128]{2,1,0:T(8,128)} %get-tuple-element.68), calls=%async_computation.1 | async-start | bytes 2359296 | tf_op jit(solution)/shard_map/all_to_all | solution.py:422
  41.4 4.9 %noise.1 = f32[64,16,128]{2,1,0:T(8,128)} custom-call(f32[128,1024]{1,0:T(8,128)} %reshape.53.noise_ref, bf16[1024,1024]{1,0:T(8,128)(2,1)} %constant.131.clone.high_ref, bf16[1024,1024]{1,0:T(8,128)(2,1)} %constant.132.clone.low_ref), custom_call_target="tpu_custom_call" | custom-call | flops 805306368 | bytes 5000000 | tf_op jit(solution)/shard_map/noise/pallas_call | solution.py:425
  48.0 3.8 %spectrum.1 = (f32[1024,128]{1,0:T(8,128)}, f32[512,128]{1,0:T(8,128)}) custom-call(s32[2]{0:T(128)} %pad_add_fusion.index_ref, f32[1024,32]{1,0:T(8,128)} %copy.17.spectrum_ref, f32[8,1024]{1,0:T(8,128)} %concatenate.9.extra_ref), custom_call_target="tpu_custom_call" | custom-call | flops 300000000 | bytes 1500000 | tf_op jit(solution)/shard_map/spectrum/pallas_call | solution.py:437
  51.8 28.4 %all-to-all-done.1.near_ref.side_near_ref.inverse_ref = f32[8,288,128]{2,1,0:T(8,128)S(1)} async-done(((f32[8,288,128]{2,1,0:T(8,128)}), f32[8,288,128]{2,1,0:T(8,128)S(1)}, u32[]{:S(2)}, u32[]{:S(2)}) %all-to-all-start.1) | async-done | bytes 1179680 | tf_op jit(solution)/shard_map/all_to_all | solution.py:422
  83.3 6.8 %collective-permute-start.4 = (f32[24,1024]{1,0:T(8,128)}, f32[24,1024]{1,0:T(8,128)S(1)}, u32[]{:S(2)}, u32[]{:S(2)}) collective-permute-start(f32[24,1024]{1,0:T(8,128)} %get-tuple-element.76), channel_id=1, source_target_pairs={{0,4},{4,0},{1,5},{5,1},{2,6},{6,2},{3,7},{7,3},{8,12},{12,8},{9,1... | collective-permute-start | bytes 294920 | tf_op jit(solution)/shard_map/ppermute | solution.py:341
  92.3 5.2 %collective-permute-done.5.b_ref = f32[24,1024]{1,0:T(8,128)S(1)} collective-permute-done((f32[24,1024]{1,0:T(8,128)S(1)}, f32[24,1024]{1,0:T(8,128)S(1)}, u32[]{:S(2)}, u32[]{:S(2)}) %collective-permute-start.5) | collective-permute-done | bytes 98336 | tf_op jit(solution)/shard_map/ppermute | solution.py:342
  97.5 3.6 %all-to-all-start.2 = ((f32[8,256,128]{2,1,0:T(8,128)}), f32[8,256,128]{2,1,0:T(8,128)S(1)}, u32[]{:S(2)}, u32[]{:S(2)}) async-start(f32[8,256,128]{2,1,0:T(8,128)} %get-tuple-element.94), calls=%async_computation.2 | async-start | bytes 2097152 | tf_op jit(solution)/shard_map/all_to_all | solution.py:481
  102.7 3.5 %collective-permute-done.6.c_ref = f32[24,1024]{1,0:T(8,128)S(1)} collective-permute-done((f32[24,1024]{1,0:T(8,128)S(1)}, f32[24,1024]{1,0:T(8,128)S(1)}, u32[]{:S(2)}, u32[]{:S(2)}) %collective-permute-start.6) | collective-permute-done | bytes 98336 | tf_op jit(solution)/shard_map/ppermute | solution.py:342
  118.5 2.9 %wait1.1 = (f32[1024,128]{1,0:T(8,128)}, f32[1,24,128]{2,1,0:T(8,128)}) custom-call(s32[1,4096]{1,0:T(1,128)} %bitcast.21, f32[16,4096]{1,0:T(8,128)} %fusion.3.refs_1_.refs_3_.wave_ref, f32[2,4096]{1,0:T(2,128)} %add_convert_fusion.refs_2_.plane_ref, f32[16,4096]{1,0:T(8,128)} %fusion.3.refs_1_.refs_3_.wave_ref, f32[24,1024]{1,0:T(8,128)} %get-tuple-element.86.refs_4_, ...), custom_call_target="tpu_custom_call" | custom-call | flops 536870912 | bytes 1500000 | tf_op jit(solution)/shard_map/wait1/pallas_call | solution.py:507
  121.5 6.5 %all-to-all-done.2.inverse_ref = f32[8,256,128]{2,1,0:T(8,128)S(1)} async-done(((f32[8,256,128]{2,1,0:T(8,128)}), f32[8,256,128]{2,1,0:T(8,128)S(1)}, u32[]{:S(2)}, u32[]{:S(2)}) %all-to-all-start.2) | async-done | bytes 1048608 | tf_op jit(solution)/shard_map/all_to_all | solution.py:481
  129.0 2.6 %step2.1 = (f32[24,1024]{1,0:T(8,128)}, f32[24,1024]{1,0:T(8,128)}) custom-call(f32[1,24,128]{2,1,0:T(8,128)} %get-tuple-element.89.start_ref, f32[24,1024]{1,0:T(8,128)} %copy-done.9, f32[24,1024]{1,0:T(8,128)} %copy-done.17, f32[24,1024]{1,0:T(8,128)} %copy-done.18, f32[24,1024]{1,0:T(8,128)} %copy-done.20, f32[8,96,1024]{2,1,0:T(8,128)} %bitcast.14, ...), custom_call_target="tpu_custom_call" | custom-call | flops 40000000 | bytes 1500000 | tf_op jit(solution)/shard_map/step2/pallas_call | solution.py:486
  133.1 6.7 %all-to-all-start.3 = ((f32[64,16,128]{2,1,0:T(8,128)}), f32[64,16,128]{2,1,0:T(8,128)S(1)}, u32[]{:S(2)}, u32[]{:S(2)}) async-start(f32[64,16,128]{2,1,0:T(8,128)} %noise.1), calls=%async_computation.3 | async-start | bytes 1048576 | tf_op jit(solution)/shard_map/all_to_all | solution.py:502
  147.5 3.4 %wait2.1 = (f32[1024,128]{1,0:T(8,128)}, f32[1,24,128]{2,1,0:T(8,128)}) custom-call(s32[1,4096]{1,0:T(1,128)} %bitcast.22, f32[16,4096]{1,0:T(8,128)} %fusion.3.refs_1_.refs_3_.wave_ref, f32[2,4096]{1,0:T(2,128)} %add_convert_fusion.refs_2_.plane_ref, f32[1024,128]{1,0:T(8,128)} %get-tuple-element.96.refs_3_, f32[24,1024]{1,0:T(8,128)} %get-tuple-element.86.refs_4_, ...), custom_call_target="tpu_custom_call" | custom-call | flops 536870912 | bytes 1500000 | tf_op jit(solution)/shard_map/wait2/pallas_call | solution.py:507
  153.6 2.6 %step3.1 = (f32[24,1024]{1,0:T(8,128)}, f32[24,1024]{1,0:T(8,128)}) custom-call(f32[1,24,128]{2,1,0:T(8,128)} %get-tuple-element.100.start_ref, f32[24,1024]{1,0:T(8,128)} %copy-done.10, f32[24,1024]{1,0:T(8,128)} %copy-done.19, f32[24,1024]{1,0:T(8,128)} %copy-done.21, f32[24,1024]{1,0:T(8,128)} %copy-done.22, f32[8,96,1024]{2,1,0:T(8,128)} %bitcast.17, ...), custom_call_target="tpu_custom_call" | custom-call | flops 40000000 | bytes 1500000 | tf_op jit(solution)/shard_map/step3/pallas_call | solution.py:486
  165.3 3.5 %wait3.1.pencil_ref = f32[1024,128]{1,0:T(8,128)} custom-call(s32[1,4096]{1,0:T(1,128)} %bitcast.23, f32[16,4096]{1,0:T(8,128)} %fusion.3.refs_1_.refs_3_.wave_ref, f32[2,4096]{1,0:T(2,128)} %add_convert_fusion.refs_2_.plane_ref, f32[1024,128]{1,0:T(8,128)} %get-tuple-element.106.refs_3_, f32[24,1024]{1,0:T(8,128)} %get-tuple-element.86.refs_4_, ...), custom_call_target="tpu_custom_call" | custom-call | flops 536870912 | bytes 1500000 | tf_op jit(solution)/shard_map/wait3/pallas_call | solution.py:507
  169.7 8.4 %filter.1 = f32[64,16,128]{2,1,0:T(8,128)} custom-call(f32[1024,128]{1,0:T(8,128)} %wait3.1.pencil_ref, s32[1,4096]{1,0:T(1,128)} %bitcast.24, f32[16,4096]{1,0:T(8,128)} %fusion.3.refs_1_.refs_3_.wave_ref, f32[2,4096]{1,0:T(2,128)} %add_convert_fusion.refs_2_.plane_ref, f32[24,1024]{1,0:T(8,128)} %copy-done.5, f32[24,1024]{1,0:T(8,128)} %copy-done.11, ...), custom_call_target="tpu_custom_call" | custom-call | flops 2147483648 | bytes 11000000 | tf_op jit(solution)/shard_map/filter/pallas_call | solution.py:527
  178.1 10.0 %all-to-all-start.4 = ((f32[64,16,128]{2,1,0:T(8,128)}), f32[64,16,128]{2,1,0:T(8,128)S(1)}, u32[]{:S(2)}, u32[]{:S(2)}) async-start(f32[64,16,128]{2,1,0:T(8,128)} %filter.1), calls=%async_computation.4 | async-start | bytes 1048576 | tf_op jit(solution)/shard_map/all_to_all | solution.py:543
  188.1 5.8 %update.2.base_ref = f32[32,16,128]{2,1,0:T(8,128)} custom-call(s32[2]{0:T(128)} %pad_add_fusion.index_ref, f32[32,16,128]{2,1,0:T(8,128)} %base_ref.1, f32[32,16,4096]{2,1,0:T(8,128)} %factor_ref.1, f32[8,32,1024]{2,1,0:T(8,128)} %bitcast.18), custom_call_target="tpu_custom_call" | custom-call | flops 805306368 | bytes 5400000 | tf_op jit(solution)/shard_map/update/pallas_call | solution.py:354
  193.9 16.8 %all-to-all-done.4.slots_ref = f32[64,16,128]{2,1,0:T(8,128)S(1)} async-done(((f32[64,16,128]{2,1,0:T(8,128)}), f32[64,16,128]{2,1,0:T(8,128)S(1)}, u32[]{:S(2)}, u32[]{:S(2)}) %all-to-all-start.4) | async-done | bytes 524320 | tf_op jit(solution)/shard_map/all_to_all | solution.py:543
  211.5 5.1 %close.1 = f32[16,4,2,1024]{3,2,1,0:T(2,128)} custom-call(f32[64,16,128]{2,1,0:T(8,128)} %copy-done.2, bf16[1024,1024]{1,0:T(8,128)(2,1)} %constant.131.clone.high_ref, bf16[1024,1024]{1,0:T(8,128)(2,1)} %constant.132.clone.low_ref), custom_call_target="tpu_custom_call" | custom-call | flops 805306368 | bytes 5500000 | tf_op jit(solution)/shard_map/close/pallas_call | solution.py:546
  216.6 5.8 %update.3 = f32[32,16,128]{2,1,0:T(8,128)} custom-call(s32[2]{0:T(128)} %pad_add_fusion.index_ref, f32[32,16,128]{2,1,0:T(8,128)} %update.2.base_ref, f32[32,16,4096]{2,1,0:T(8,128)} %factor_ref.1, f32[8,32,1024]{2,1,0:T(8,128)} %bitcast.19), custom_call_target="tpu_custom_call" | custom-call | flops 805306368 | bytes 5400000 | tf_op jit(solution)/shard_map/update/pallas_call | solution.py:354
  (131 shorter events, 58.4 us)
Async XLA Ops:
  7.2 99.0 %all-gather.7.cloned.1.call-start = ((), (), s32[]{:S(2)}) async-start(), calls=%async_computation.5 | async-start | bytes 3538944 | tf_op jit(solution)/shard_map/all_gather | solution.py:407
  11.2 13.2 %all-to-all-start = ((f32[8,64,128]{2,1,0:T(8,128)}), f32[8,64,128]{2,1,0:T(8,128)S(1)}, u32[]{:S(2)}, u32[]{:S(2)}) async-start(f32[8,64,128]{2,1,0:T(8,128)} %get-tuple-element.63), calls=%async_computation | async-start | bytes 524288 | tf_op jit(solution)/shard_map/all_to_all | solution.py:396
  17.9 4.9 %collective-permute-start = (f32[64,128]{1,0:T(8,128)S(1)}, f32[64,128]{1,0:T(8,128)S(1)}, u32[]{:S(2)}, u32[]{:S(2)}) collective-permute-start(f32[64,128]{1,0:T(8,128)S(1)} %copy-done.24), channel_id=1, source_target_pairs={{0,1},{1,2},{2,3},{3,0},{4,5},{5,6},{6,7},{7,4},{8,9},{9,10},{10,1... | collective-permute-start | bytes 98312 | tf_op jit(solution)/shard_map/ppermute | solution.py:409
  18.5 4.5 %collective-permute-start.1 = (f32[64,128]{1,0:T(8,128)S(1)}, f32[64,128]{1,0:T(8,128)S(1)}, u32[]{:S(2)}, u32[]{:S(2)}) collective-permute-start(f32[64,128]{1,0:T(8,128)S(1)} %copy-done.24), channel_id=1, source_target_pairs={{0,2},{1,3},{2,0},{3,1},{4,6},{5,7},{6,4},{7,5},{8,10},{9,11},{10,... | collective-permute-start | bytes 98312 | tf_op jit(solution)/shard_map/ppermute | solution.py:409
  28.1 52.1 %all-to-all-start.1 = ((f32[8,288,128]{2,1,0:T(8,128)}), f32[8,288,128]{2,1,0:T(8,128)S(1)}, u32[]{:S(2)}, u32[]{:S(2)}) async-start(f32[8,288,128]{2,1,0:T(8,128)} %get-tuple-element.68), calls=%async_computation.1 | async-start | bytes 2359296 | tf_op jit(solution)/shard_map/all_to_all | solution.py:422
  36.6 10.8 %collective-permute-start.3 = (f32[2,1024]{1,0:T(2,128)S(1)}, f32[2,1024]{1,0:T(2,128)S(1)}, u32[]{:S(2)}, u32[]{:S(2)}) collective-permute-start(f32[2,1024]{1,0:T(2,128)S(1)} %slice_bitcast_fusion), channel_id=1, source_target_pairs={{128,0},{129,1},{130,2},{131,3}} | collective-permute-start | bytes 24584 | tf_op jit(solution)/shard_map/ppermute | solution.py:423
  83.3 8.0 %collective-permute-start.4 = (f32[24,1024]{1,0:T(8,128)}, f32[24,1024]{1,0:T(8,128)S(1)}, u32[]{:S(2)}, u32[]{:S(2)}) collective-permute-start(f32[24,1024]{1,0:T(8,128)} %get-tuple-element.76), channel_id=1, source_target_pairs={{0,4},{4,0},{1,5},{5,1},{2,6},{6,2},{3,7},{7,3},{8,12},{12,8},{9,1... | collective-permute-start | bytes 294920 | tf_op jit(solution)/shard_map/ppermute | solution.py:341
  92.2 5.3 %collective-permute-start.5 = (f32[24,1024]{1,0:T(8,128)S(1)}, f32[24,1024]{1,0:T(8,128)S(1)}, u32[]{:S(2)}, u32[]{:S(2)}) collective-permute-start(f32[24,1024]{1,0:T(8,128)S(1)} %add.110.a_ref), channel_id=1, source_target_pairs={{0,8},{8,16},{16,24},{24,0},{1,9},{9,17},{17,25},{25,1},{2,10},{10... | collective-permute-start | bytes 294920 | tf_op jit(solution)/shard_map/ppermute | solution.py:342
  97.5 30.5 %all-to-all-start.2 = ((f32[8,256,128]{2,1,0:T(8,128)}), f32[8,256,128]{2,1,0:T(8,128)S(1)}, u32[]{:S(2)}, u32[]{:S(2)}) async-start(f32[8,256,128]{2,1,0:T(8,128)} %get-tuple-element.94), calls=%async_computation.2 | async-start | bytes 2097152 | tf_op jit(solution)/shard_map/all_to_all | solution.py:481
  101.1 87.1 %all-gather.9.cloned.1.call-start = ((), (), s32[]{:S(2)}) async-start(), calls=%async_computation.6 | async-start | bytes 1179648 | tf_op jit(solution)/shard_map/all_gather | solution.py:504
  101.1 5.1 %collective-permute-start.6 = (f32[24,1024]{1,0:T(8,128)S(1)}, f32[24,1024]{1,0:T(8,128)S(1)}, u32[]{:S(2)}, u32[]{:S(2)}) collective-permute-start(f32[24,1024]{1,0:T(8,128)S(1)} %add.110.a_ref), channel_id=1, source_target_pairs={{0,16},{8,24},{16,0},{24,8},{1,17},{9,25},{17,1},{25,9},{2,18},{10... | collective-permute-start | bytes 294920 | tf_op jit(solution)/shard_map/ppermute | solution.py:342
  101.2 5.0 %collective-permute-start.7 = (f32[24,1024]{1,0:T(8,128)S(1)}, f32[24,1024]{1,0:T(8,128)S(1)}, u32[]{:S(2)}, u32[]{:S(2)}) collective-permute-start(f32[24,1024]{1,0:T(8,128)S(1)} %add.110.a_ref), channel_id=1, source_target_pairs={{0,24},{8,0},{16,8},{24,16},{1,25},{9,1},{17,9},{25,17},{2,26},{10... | collective-permute-start | bytes 294920 | tf_op jit(solution)/shard_map/ppermute | solution.py:342
  113.8 7.6 %collective-permute-start.9 = (f32[24,1024]{1,0:T(8,128)S(1)}, f32[24,1024]{1,0:T(8,128)S(1)}, u32[]{:S(2)}, u32[]{:S(2)}) collective-permute-start(f32[24,1024]{1,0:T(8,128)S(1)} %add.111.a_ref), channel_id=1, source_target_pairs={{0,8},{8,16},{16,24},{24,0},{1,9},{9,17},{17,25},{25,1},{2,10},{10... | collective-permute-start | bytes 294920 | tf_op jit(solution)/shard_map/ppermute | solution.py:342
  114.5 6.9 %collective-permute-start.10 = (f32[24,1024]{1,0:T(8,128)S(1)}, f32[24,1024]{1,0:T(8,128)S(1)}, u32[]{:S(2)}, u32[]{:S(2)}) collective-permute-start(f32[24,1024]{1,0:T(8,128)S(1)} %add.111.a_ref), channel_id=1, source_target_pairs={{0,16},{8,24},{16,0},{24,8},{1,17},{9,25},{17,1},{25,9},{2,18},{10... | collective-permute-start | bytes 294920 | tf_op jit(solution)/shard_map/ppermute | solution.py:342
  116.5 5.0 %collective-permute-start.11 = (f32[24,1024]{1,0:T(8,128)S(1)}, f32[24,1024]{1,0:T(8,128)S(1)}, u32[]{:S(2)}, u32[]{:S(2)}) collective-permute-start(f32[24,1024]{1,0:T(8,128)S(1)} %add.111.a_ref), channel_id=1, source_target_pairs={{0,24},{8,0},{16,8},{24,16},{1,25},{9,1},{17,9},{25,17},{2,26},{10... | collective-permute-start | bytes 294920 | tf_op jit(solution)/shard_map/ppermute | solution.py:342
  133.1 31.4 %all-to-all-start.3 = ((f32[64,16,128]{2,1,0:T(8,128)}), f32[64,16,128]{2,1,0:T(8,128)S(1)}, u32[]{:S(2)}, u32[]{:S(2)}) async-start(f32[64,16,128]{2,1,0:T(8,128)} %noise.1), calls=%async_computation.3 | async-start | bytes 1048576 | tf_op jit(solution)/shard_map/all_to_all | solution.py:502
  139.9 76.7 %all-gather.11.cloned.1.call-start = ((), (), s32[]{:S(2)}) async-start(), calls=%async_computation.7 | async-start | bytes 1179648 | tf_op jit(solution)/shard_map/all_gather | solution.py:542
  142.7 8.2 %collective-permute-start.13 = (f32[24,1024]{1,0:T(8,128)S(1)}, f32[24,1024]{1,0:T(8,128)S(1)}, u32[]{:S(2)}, u32[]{:S(2)}) collective-permute-start(f32[24,1024]{1,0:T(8,128)S(1)} %add.112.a_ref), channel_id=1, source_target_pairs={{0,8},{8,16},{16,24},{24,0},{1,9},{9,17},{17,25},{25,1},{2,10},{10... | collective-permute-start | bytes 294920 | tf_op jit(solution)/shard_map/ppermute | solution.py:342
  143.9 9.0 %collective-permute-start.14 = (f32[24,1024]{1,0:T(8,128)S(1)}, f32[24,1024]{1,0:T(8,128)S(1)}, u32[]{:S(2)}, u32[]{:S(2)}) collective-permute-start(f32[24,1024]{1,0:T(8,128)S(1)} %add.112.a_ref), channel_id=1, source_target_pairs={{0,16},{8,24},{16,0},{24,8},{1,17},{9,25},{17,1},{25,9},{2,18},{10... | collective-permute-start | bytes 294920 | tf_op jit(solution)/shard_map/ppermute | solution.py:342
  146.3 6.5 %collective-permute-start.15 = (f32[24,1024]{1,0:T(8,128)S(1)}, f32[24,1024]{1,0:T(8,128)S(1)}, u32[]{:S(2)}, u32[]{:S(2)}) collective-permute-start(f32[24,1024]{1,0:T(8,128)S(1)} %add.112.a_ref), channel_id=1, source_target_pairs={{0,24},{8,0},{16,8},{24,16},{1,25},{9,1},{17,9},{25,17},{2,26},{10... | collective-permute-start | bytes 294920 | tf_op jit(solution)/shard_map/ppermute | solution.py:342
  159.7 9.1 %collective-permute-start.17 = (f32[24,1024]{1,0:T(8,128)S(1)}, f32[24,1024]{1,0:T(8,128)S(1)}, u32[]{:S(2)}, u32[]{:S(2)}) collective-permute-start(f32[24,1024]{1,0:T(8,128)S(1)} %add.113.a_ref), channel_id=1, source_target_pairs={{0,8},{8,16},{16,24},{24,0},{1,9},{9,17},{17,25},{25,1},{2,10},{10... | collective-permute-start | bytes 294920 | tf_op jit(solution)/shard_map/ppermute | solution.py:342
  160.6 8.2 %collective-permute-start.18 = (f32[24,1024]{1,0:T(8,128)S(1)}, f32[24,1024]{1,0:T(8,128)S(1)}, u32[]{:S(2)}, u32[]{:S(2)}) collective-permute-start(f32[24,1024]{1,0:T(8,128)S(1)} %add.113.a_ref), channel_id=1, source_target_pairs={{0,16},{8,24},{16,0},{24,8},{1,17},{9,25},{17,1},{25,9},{2,18},{10... | collective-permute-start | bytes 294920 | tf_op jit(solution)/shard_map/ppermute | solution.py:342
  163.0 5.8 %collective-permute-start.19 = (f32[24,1024]{1,0:T(8,128)S(1)}, f32[24,1024]{1,0:T(8,128)S(1)}, u32[]{:S(2)}, u32[]{:S(2)}) collective-permute-start(f32[24,1024]{1,0:T(8,128)S(1)} %add.113.a_ref), channel_id=1, source_target_pairs={{0,24},{8,0},{16,8},{24,16},{1,25},{9,1},{17,9},{25,17},{2,26},{10... | collective-permute-start | bytes 294920 | tf_op jit(solution)/shard_map/ppermute | solution.py:342
  178.1 32.6 %all-to-all-start.4 = ((f32[64,16,128]{2,1,0:T(8,128)}), f32[64,16,128]{2,1,0:T(8,128)S(1)}, u32[]{:S(2)}, u32[]{:S(2)}) async-start(f32[64,16,128]{2,1,0:T(8,128)} %filter.1), calls=%async_computation.4 | async-start | bytes 1048576 | tf_op jit(solution)/shard_map/all_to_all | solution.py:543
  (32 other events, 185.9 us)
Sparse Core Ops, SparseCore 0:
  11.4 73.9 all-gather.6
  133.3 36.2 all-gather.8
  171.3 41.1 all-gather.10
where the time goes:
time: 230 us; the launch traced here: 229 us
  waiting for transfers between devices  68.9 us (30%)
  starting transfers between devices  65.8 us (29%)
  Pallas kernels  60 us (26%)
  between operations  14.1 us (6%)
  local copies, waits for them, and re-layouts  11.5 us (5%)
  other arithmetic  8.66 us (4%)
    all_to_all x1, waiting for transfers between devices, per_device(): near = lax.all_to_all(near, 'z', 0, 0)  28.4 us
    all_to_all x1, waiting for transfers between devices, per_device(): slots = lax.all_to_all(slots, WIDE, 0, 0)  16.8 us
    ppermute x12, starting transfers between devices, share(): lax.ppermute(total, 'x', ring(4, step))  14.4 us
    pallas_call x2, Pallas kernels, update(): call(functools.partial(update_kernel, first_panel, panels), 'update', [SM...  11.5 us
    ppermute x4, starting transfers between devices, share(): total = partial + lax.ppermute(partial, 'core', ring(2, 1))  11.3 us
    ppermute x12, waiting for transfers between devices, share(): lax.ppermute(total, 'x', ring(4, step))  10.8 us
    all_to_all x1, starting transfers between devices, per_device(): slots = lax.all_to_all(slots, WIDE, 0, 0)  9.98 us
    pallas_call x3, Pallas kernels, per_device(): call(functools.partial(wait_kernel, panel), f'wait{panel}', obs_specs(pan...  9.72 us
  transfers between devices with their start and end apart: 28, of which 14 were waited for; matrix products, arithmetic and copies ran while one was open for 6% of the time, Pallas kernels for 21%

commit v1 on v0

--- a/solution.py
+++ b/solution.py
@@ -118,48 +118,57 @@
 
 
 def bundle_kernel(index_ref, columns_ref, *refs):
-    side_refs, (near_ref, far_ref) = refs[:4], refs[4:]
+    side_refs, out_ref = refs[:4], refs[4]
     lane = lax.broadcasted_iota(jnp.int32, (64, 128), 1)
     weights = jnp.zeros((64, 128), F32)
     for step, ref in enumerate(side_refs):
         y = lax.rem(index_ref[1] + 4 - step, 4)
         weights = jnp.where(lane == y + 16, ref[:, 0:1], weights)
     side = side_refs[0][...]
-    inverses = [columns_ref[:, 16 * k : 16 * k + 16, :].reshape(128, 128) for k in range(4)]
+    quarter = columns_ref[pl.ds(2 * index_ref[1], 2)]
+    quarter = [quarter[:, 32 * h : 32 * h + 32].reshape(64, 128) for h in range(2)]
     for z in range(8):
         own = pltpu.roll(side, (128 - 16 * z) % 128, 1) if z else side
         rows = jnp.where(lane < 16, own, weights)
-        for k in range(2):
-            near_ref[z, 128 * k : 128 * k + 128] = inverses[k]
-            far_ref[z, 128 * k : 128 * k + 128] = inverses[2 + k]
-        near_ref[z, 256:288] = jnp.transpose(jnp.concatenate([rows, rows]))[:32]
-
-
-def spread(work, inverse_ref, out_ref):
+        out_ref[z, 0:64] = quarter[0]
+        out_ref[z, 64:128] = quarter[1]
+        out_ref[z, 128:160] = jnp.transpose(jnp.concatenate([rows, rows]))[:32]
+
+
+def spread(work, index_ref, inverse_refs, out_ref, high_ref, low_ref):
+    for number, ref in enumerate(inverse_refs):
+        y = lax.rem(index_ref[1] + 4 - number // 2, 4)
+        start = pl.multiple_of(32 * y + 16 * (number % 2), 16)
+        rows_high, rows_low = split(ref[...])
+        high_ref[:, pl.ds(start, 16), :] = rows_high
+        low_ref[:, pl.ds(start, 16), :] = rows_low
     high, low = split(work)
-    rows_high, rows_low = split(inverse_ref[...].reshape(LENGTH, 128))
+    rows_high = high_ref[...].reshape(LENGTH, 128)
     wide = dot(jnp.concatenate([high, low]), rows_high, NT)
+    rows_low = low_ref[...].reshape(LENGTH, 128)
     out_ref[...] = wide[:COLS] + wide[COLS:] + dot(high, rows_low, NT)
 
 
-def first_kernel(near_ref, side_near_ref, out_ref, side_ref):
+def first_kernel(index_ref, slab_ref, *refs):
+    inverse_refs, (out_ref, side_ref, high_ref, low_ref) = refs[:8], refs[8:]
     lane = lax.broadcasted_iota(jnp.int32, (COLS, 128), 1) // 16
     for k in range(4):
         rows = jnp.zeros((COLS, 128), F32)
         for z in range(8):
-            piece = side_near_ref[z, 0:COLS]
+            piece = slab_ref[z, 0:COLS]
             turn = (16 * (z - k)) % 128
             piece = pltpu.roll(piece, turn, 1) if turn else piece
             rows = jnp.where(lane == z, piece, rows)
         side_ref[k] = rows
-    spread(side_ref[0], near_ref, out_ref)
-
-
-def step_kernel(start_ref, a_ref, b_ref, c_ref, d_ref, factor_ref, inverse_ref, out_ref, unknown_ref):
+    spread(side_ref[0], index_ref, inverse_refs, out_ref, high_ref, low_ref)
+
+
+def step_kernel(index_ref, start_ref, a_ref, b_ref, c_ref, d_ref, factor_ref, *refs):
+    inverse_refs, (out_ref, unknown_ref, high_ref, low_ref) = refs[:8], refs[8:]
     unknown = (a_ref[...] + b_ref[...]) + (c_ref[...] + d_ref[...])
     unknown_ref[...] = unknown
     work = start_ref[0] - dot_nt(unknown, factor_ref[...].reshape(128, LENGTH))
-    spread(work, inverse_ref, out_ref)
+    spread(work, index_ref, inverse_refs, out_ref, high_ref, low_ref)
 
 
 def spectrum_kernel(index_ref, spectrum_ref, extra_ref, even_ref, odd_ref):
@@ -390,10 +399,14 @@
         0,
         500_000,
     )(inverses.reshape(64, LENGTH), right_side)
-    box = [columns, side, spectrum, factor]
-    tie((box, (0, 1, 2, 3)))
-    columns, side, spectrum, factor = box
+    box = [columns, side, factor]
+    tie((box, (0, 1, 2)))
+    columns, side, factor = box
     columns = lax.all_to_all(columns, ("x", "core"), 0, 0)
+    extra = lax.ppermute(spectrum[:, :, 0].T, WIDE, [(32, 0)])
+    box = [columns, extra]
+    tie((box, (0, 1)))
+    columns, extra = box
 
     lower = call(
         lower_kernel,
@@ -407,20 +420,19 @@
     lower = lax.all_gather(lower, "z")
 
     sides = [side] + [lax.ppermute(side, "y", ring(4, step)) for step in (1, 2, 3)]
-    near, far = call(
+    quarter = call(
         bundle_kernel,
         "bundle",
         [SMEM, spec(8, 64, 128)] + [spec(64, 128)] * 4,
-        [spec(8, 288, 128), spec(8, 256, 128)],
-        [shape_of(8, 288, 128), shape_of(8, 256, 128)],
+        spec(8, 160, 128),
+        shape_of(8, 160, 128),
         0,
-        2_500_000,
+        1_500_000,
     )(index, columns, *sides)
-    box = [near, far, noise, spectrum, obs_cells]
-    tie((box, (0, 1, 2, 3, 4)))
-    near, far, noise, spectrum, obs_cells = box
-    near = lax.all_to_all(near, "z", 0, 0)
-    extra = lax.ppermute(spectrum[:, :, 0].T, WIDE, [(32, 0)])
+    box = [quarter, noise, spectrum, obs_cells]
+    tie((box, (0, 1, 2, 3)))
+    quarter, noise, spectrum, obs_cells = box
+    quarter = lax.all_to_all(quarter, "z", 0, 0)
 
     slab = call(
         noise_kernel,
@@ -450,9 +462,12 @@
     freq, phase = z_frequencies(wide, jnp)
     turn = (freq[:, None] * (obs_cells % LENGTH)[None, :] + phase[:, None]) % LENGTH
     waves = jnp.cos(turn.astype(F32) * (2.0 * math.pi / LENGTH))
-    box = [near, slab, even, odd, cell_x, planes, waves]
+    box = [quarter, slab, even, odd, cell_x, planes, waves]
     tie((box, tuple(range(7))))
-    near, slab, even, odd, cell_x, planes, waves = box
+    quarter, slab, even, odd, cell_x, planes, waves = box
+    own = [quarter[:, 0:64], quarter[:, 64:128]]
+    own = [[one] + [lax.ppermute(one, "y", ring(4, step)) for step in (1, 2, 3)] for one in own]
+    slab = lax.all_to_all(slab, WIDE, 0, 0)
 
     obs_specs = lambda k: [
         block_at((1, LENGTH), (0, k)),
@@ -461,7 +476,9 @@
     ]
     side_spec = lambda k: block_at((1, COLS, 128), (k, 0, 0))
     factor_spec = lambda k, j: block_at((8, 16, LENGTH), (0, k * (k - 1) // 2 + j, 0))
-    inverse_spec = lambda k: block_at((8, 128, 128), (0, k % 2, 0))
+    inverse_specs = lambda k: [block_at((8, 16, 128), (0, k % 2 + a, 0)) for a in (0, 2)] * 4
+    inverses = [[one for one in own[k // 2] for _ in range(2)] for k in range(4)]
+    inverse_scratch = [pltpu.VMEM((8, 128, 128), BF16)] * 2
     panel_spec = spec(COLS, LENGTH)
     panel_shape = shape_of(COLS, LENGTH)
     pencil_spec = spec(LENGTH, 128)
@@ -469,16 +486,14 @@
     partial, sides = call(
         first_kernel,
         "first",
-        [inverse_spec(0), block_at((8, 32, 128), (0, 8, 0))],
+        [SMEM, block_at((8, 32, 128), (0, 4, 0))] + inverse_specs(0),
         [panel_spec, spec(4, COLS, 128)],
         [panel_shape, shape_of(4, COLS, 128)],
         20_000_000,
         1_200_000,
-    )(near, near)
+        inverse_scratch,
+    )(index, quarter, *inverses[0])
     parts = share(partial)
-    box = [far]
-    tie((parts, (1,)), (box, (0,)))
-    far = lax.all_to_all(box[0], "z", 0, 0)
     unknowns = []
     work = sides
     pencil = waves
@@ -486,21 +501,19 @@
         partial, unknown = call(
             step_kernel,
             f"step{panel}",
-            [side_spec(1 if panel == 1 else 0)]
+            [SMEM, side_spec(1 if panel == 1 else 0)]
             + [panel_spec] * 4
-            + [factor_spec(panel, panel - 1), inverse_spec(panel)],
+            + [factor_spec(panel, panel - 1)]
+            + inverse_specs(panel),
             [panel_spec] * 2,
             [panel_shape] * 2,
             40_000_000,
             1_500_000,
-        )(work, *parts, lower, near if panel == 1 else far)
+            inverse_scratch,
+        )(index, work, *parts, lower, *inverses[panel])
         unknowns.append(unknown)
         parts = share(partial)
-        if panel == 1:
-            box = [slab]
-            tie((parts, (1,)), (box, (0,)))
-            slab = lax.all_to_all(box[0], WIDE, 0, 0)
-        if panel == 2:
+        if panel == 3:
             early = lax.all_gather(jnp.concatenate([u[:16] for u in unknowns]), "z")
         later = panel < 3
         box = list(
@@ -539,9 +552,9 @@
         [TABLE] * 4 + [pltpu.SemaphoreType.DMA((4,))],
     )(pencil, cell_x, waves, planes, *parts, x_high, x_low, back_high, back_low, even, odd)
     late = (parts[0][:16] + parts[1][:16]) + (parts[2][:16] + parts[3][:16])
-    late = lax.all_gather(jnp.concatenate([unknowns[2][:16], late]), "z")
+    late = lax.all_gather(jnp.concatenate([late, jnp.zeros((16, LENGTH), F32)]), "z")
     slots = lax.all_to_all(slots, WIDE, 0, 0)
-    solved = update(0, 2, index, right_side, factor, early)
+    solved = update(0, 3, index, right_side, factor, early)
     slots, solved = lax.optimization_barrier((slots, solved))
     correction = call(
         close_kernel,
@@ -555,7 +568,7 @@
         grid=4,
     )(slots, z_high, z_low)
     solved, correction = lax.optimization_barrier((solved, correction))
-    solved = update(2, 2, index, solved, factor, late)
+    solved = update(3, 1, index, solved, factor, late)
     return (solved, correction)
 
 

time: 230 us -> 232 us (level); the launches traced: 229 us -> 228 us
  starting transfers between devices: 65.8 us -> 61.3 us
  waiting for transfers between devices: 68.9 us -> 72.8 us
    ppermute x0 -> x6, starting transfers between devices: none -> 9.88 us  [per_device(): lax.ppermute(one, 'y', ring(4, step))]
    ppermute x0 -> x6, waiting for transfers between devices: none -> 9.74 us  [per_device(): lax.ppermute(one, 'y', ring(4, step))]
    all_to_all x3 -> x2, waiting for transfers between devices: 34.9 us -> 28.5 us  [the longest x1 15.2 us: per_device(): slab = lax.all_to_all(slab, WIDE, 0, 0)]
    all_gather x1, waiting for transfers between devices: 0.01 us -> 5.71 us  [per_device(): lax.all_gather(jnp.concatenate([late, jnp.zeros((16, LENGTH), F32)]), 'z')]
    all_to_all x3 -> x2, starting transfers between devices: 18.5 us -> 13.2 us  [the longest x1 7.59 us: per_device(): quarter = lax.all_to_all(quarter, 'z', 0, 0)]
    all_to_all x1, starting transfers between devices: 9.98 us -> 5.55 us  [per_device(): slots = lax.all_to_all(slots, WIDE, 0, 0)]
    ppermute x4, starting transfers between devices: 11.3 us -> 7.59 us  [share(): total = partial + lax.ppermute(partial, 'core', ring(2, 1))]
    all_to_all x1, waiting for transfers between devices: 16.8 us -> 13.5 us  [per_device(): slots = lax.all_to_all(slots, WIDE, 0, 0)]
  transfers between devices with their start and end apart: 28 -> 33, of which waited for: 14 -> 16; matrix products, arithmetic and copies ran while one was open for 6% -> 5% of each run, Pallas kernels for 21% -> 19%
where the time goes in v1:
time: 232 us; the launch traced here: 228 us
  waiting for transfers between devices  72.8 us (31%)
  starting transfers between devices  61.3 us (26%)
  Pallas kernels  59.7 us (26%)
  between operations  14.2 us (6%)
  local copies, waits for them, and re-layouts  12.3 us (5%)
  other arithmetic  7.99 us (3%)
    all_to_all x1, waiting for transfers between devices, per_device(): slab = lax.all_to_all(slab, WIDE, 0, 0)  15.2 us
    all_to_all x1, waiting for transfers between devices, per_device(): slots = lax.all_to_all(slots, WIDE, 0, 0)  13.5 us
    ppermute x12, starting transfers between devices, share(): lax.ppermute(total, 'x', ring(4, step))  13.3 us
    all_to_all x1, waiting for transfers between devices, per_device(): quarter = lax.all_to_all(quarter, 'z', 0, 0)  13.2 us
    pallas_call x2, Pallas kernels, update(): call(functools.partial(update_kernel, first_panel, panels), 'update', [SM...  11.7 us
    ppermute x12, waiting for transfers between devices, share(): lax.ppermute(total, 'x', ring(4, step))  10.9 us
    ppermute x6, starting transfers between devices, per_device(): lax.ppermute(one, 'y', ring(4, step))  9.88 us
    pallas_call x3, Pallas kernels, per_device(): call(functools.partial(wait_kernel, panel), f'wait{panel}', obs_specs(pan...  9.76 us
  transfers between devices with their start and end apart: 33, of which 16 were waited for; matrix products, arithmetic and copies ran while one was open for 5% of the time, Pallas kernels for 19%

profile of v1, /device:TPU:1, one launch (start us, length us, event | category | flops | bytes accessed | tf_op | source)
XLA Modules:
  0.0 228.3 jit_solution(327269714747621589)
XLA Ops:
  11.3 6.7 %all-to-all-start = ((f32[8,64,128]{2,1,0:T(8,128)}), f32[8,64,128]{2,1,0:T(8,128)S(1)}, u32[]{:S(2)}, u32[]{:S(2)}) async-start(f32[8,64,128]{2,1,0:T(8,128)} %get-tuple-element.57), calls=%async_computation | async-start | bytes 524288 | tf_op jit(solution)/shard_map/all_to_all | solution.py:405
  18.5 2.6 %collective-permute-start.2 = (f32[64,128]{1,0:T(8,128)S(1)}, f32[64,128]{1,0:T(8,128)S(1)}, u32[]{:S(2)}, u32[]{:S(2)}) collective-permute-start(f32[64,128]{1,0:T(8,128)S(1)} %copy-done.32), channel_id=1, source_target_pairs={{0,2},{1,3},{2,0},{3,1},{4,6},{5,7},{6,4},{7,5},{8,10},{9,11},{10,... | collective-permute-start | bytes 98312 | tf_op jit(solution)/shard_map/ppermute | solution.py:422
  30.3 7.6 %all-to-all-start.1 = ((f32[8,160,128]{2,1,0:T(8,128)}), f32[8,160,128]{2,1,0:T(8,128)S(1)}, u32[]{:S(2)}, u32[]{:S(2)}) async-start(f32[8,160,128]{2,1,0:T(8,128)} %bundle.1), calls=%async_computation.1 | async-start | bytes 1310720 | tf_op jit(solution)/shard_map/all_to_all | solution.py:435
  38.5 4.9 %noise.1 = f32[64,16,128]{2,1,0:T(8,128)} custom-call(f32[128,1024]{1,0:T(8,128)} %reshape.53.noise_ref, bf16[1024,1024]{1,0:T(8,128)(2,1)} %constant.132.clone.high_ref, bf16[1024,1024]{1,0:T(8,128)(2,1)} %constant.133.clone.low_ref), custom_call_target="tpu_custom_call" | custom-call | flops 805306368 | bytes 5000000 | tf_op jit(solution)/shard_map/noise/pallas_call | solution.py:437
  44.1 3.8 %spectrum.1 = (f32[1024,128]{1,0:T(8,128)}, f32[512,128]{1,0:T(8,128)}) custom-call(s32[2]{0:T(128)} %pad_add_fusion.index_ref, f32[1024,32]{1,0:T(8,128)} %copy.17.spectrum_ref, f32[8,1024]{1,0:T(8,128)} %concatenate.9.extra_ref), custom_call_target="tpu_custom_call" | custom-call | flops 300000000 | bytes 1500000 | tf_op jit(solution)/shard_map/spectrum/pallas_call | solution.py:449
  50.3 13.2 %all-to-all-done.1.slab_ref = f32[8,160,128]{2,1,0:T(8,128)S(1)} async-done(((f32[8,160,128]{2,1,0:T(8,128)}), f32[8,160,128]{2,1,0:T(8,128)S(1)}, u32[]{:S(2)}, u32[]{:S(2)}) %all-to-all-start.1) | async-done | bytes 655392 | tf_op jit(solution)/shard_map/all_to_all | solution.py:435
  65.3 3.5 %collective-permute-start.5 = (f32[8,64,128]{2,1,0:T(8,128)S(1)}, f32[8,64,128]{2,1,0:T(8,128)S(1)}, u32[]{:S(2)}, u32[]{:S(2)}) collective-permute-start(f32[8,64,128]{2,1,0:T(8,128)S(1)} %get-tuple-element.111.refs_0_.refs_1_), channel_id=1, source_target_pairs={{0,2},{1,3},{2,0},{3,1},{4,6},{5,7},{6,4},{7,5},{8,10},{9,11},{10,... | collective-permute-start | bytes 786440 | tf_op jit(solution)/shard_map/ppermute | solution.py:469
  71.8 6.9 %collective-permute-done.5.refs_4_.refs_5_ = f32[8,64,128]{2,1,0:T(8,128)S(1)} collective-permute-done((f32[8,64,128]{2,1,0:T(8,128)S(1)}, f32[8,64,128]{2,1,0:T(8,128)S(1)}, u32[]{:S(2)}, u32[]{:S(2)}) %collective-permute-start.5) | collective-permute-done | bytes 262176 | tf_op jit(solution)/shard_map/ppermute | solution.py:469
  82.2 3.0 %collective-permute-start.7 = (f32[24,1024]{1,0:T(8,128)}, f32[24,1024]{1,0:T(8,128)S(1)}, u32[]{:S(2)}, u32[]{:S(2)}) collective-permute-start(f32[24,1024]{1,0:T(8,128)} %get-tuple-element.69), channel_id=1, source_target_pairs={{0,4},{4,0},{1,5},{5,1},{2,6},{6,2},{3,7},{7,3},{8,12},{12,8},{9,1... | collective-permute-start | bytes 294920 | tf_op jit(solution)/shard_map/ppermute | solution.py:350
  91.4 4.8 %collective-permute-done.8.b_ref = f32[24,1024]{1,0:T(8,128)S(1)} collective-permute-done((f32[24,1024]{1,0:T(8,128)S(1)}, f32[24,1024]{1,0:T(8,128)S(1)}, u32[]{:S(2)}, u32[]{:S(2)}) %collective-permute-start.8) | collective-permute-done | bytes 98336 | tf_op jit(solution)/shard_map/ppermute | solution.py:351
  107.5 3.7 %collective-permute-done.12.b_ref = f32[24,1024]{1,0:T(8,128)S(1)} collective-permute-done((f32[24,1024]{1,0:T(8,128)S(1)}, f32[24,1024]{1,0:T(8,128)S(1)}, u32[]{:S(2)}, u32[]{:S(2)}) %collective-permute-start.12) | collective-permute-done | bytes 98336 | tf_op jit(solution)/shard_map/ppermute | solution.py:351
  111.2 2.9 %wait1.1 = (f32[1024,128]{1,0:T(8,128)}, f32[1,24,128]{2,1,0:T(8,128)}) custom-call(s32[1,4096]{1,0:T(1,128)} %bitcast.21, f32[16,4096]{1,0:T(8,128)} %fusion.3.refs_1_.refs_3_.wave_ref, f32[2,4096]{1,0:T(2,128)} %add_convert_fusion.refs_2_.plane_ref, f32[16,4096]{1,0:T(8,128)} %fusion.3.refs_1_.refs_3_.wave_ref, f32[24,1024]{1,0:T(8,128)} %get-tuple-element.75.refs_4_, ...), custom_call_target="tpu_custom_call" | custom-call | flops 536870912 | bytes 1500000 | tf_op jit(solution)/shard_map/wait1/pallas_call | solution.py:520
  119.7 2.7 %collective-permute-start.18 = (f32[24,1024]{1,0:T(8,128)}, f32[24,1024]{1,0:T(8,128)S(1)}, u32[]{:S(2)}, u32[]{:S(2)}) collective-permute-start(f32[24,1024]{1,0:T(8,128)} %get-tuple-element.83), channel_id=1, source_target_pairs={{0,4},{4,0},{1,5},{5,1},{2,6},{6,2},{3,7},{7,3},{8,12},{12,8},{9,1... | collective-permute-start | bytes 294920 | tf_op jit(solution)/shard_map/ppermute | solution.py:350
  128.1 3.4 %wait2.1 = (f32[1024,128]{1,0:T(8,128)}, f32[1,24,128]{2,1,0:T(8,128)}) custom-call(s32[1,4096]{1,0:T(1,128)} %bitcast.22, f32[16,4096]{1,0:T(8,128)} %fusion.3.refs_1_.refs_3_.wave_ref, f32[2,4096]{1,0:T(2,128)} %add_convert_fusion.refs_2_.plane_ref, f32[1024,128]{1,0:T(8,128)} %get-tuple-element.84.refs_3_, f32[24,1024]{1,0:T(8,128)} %get-tuple-element.75.refs_4_, ...), custom_call_target="tpu_custom_call" | custom-call | flops 536870912 | bytes 1500000 | tf_op jit(solution)/shard_map/wait2/pallas_call | solution.py:520
  137.0 5.6 %all-to-all-start.2 = ((f32[64,16,128]{2,1,0:T(8,128)}), f32[64,16,128]{2,1,0:T(8,128)S(1)}, u32[]{:S(2)}, u32[]{:S(2)}) async-start(f32[64,16,128]{2,1,0:T(8,128)} %noise.1), calls=%async_computation.2 | async-start | bytes 1048576 | tf_op jit(solution)/shard_map/all_to_all | solution.py:470
  150.5 15.2 %all-to-all-done.2.refs_7_ = f32[64,16,128]{2,1,0:T(8,128)S(1)} async-done(((f32[64,16,128]{2,1,0:T(8,128)}), f32[64,16,128]{2,1,0:T(8,128)S(1)}, u32[]{:S(2)}, u32[]{:S(2)}) %all-to-all-start.2) | async-done | bytes 524320 | tf_op jit(solution)/shard_map/all_to_all | solution.py:470
  166.5 3.5 %wait3.1.pencil_ref = f32[1024,128]{1,0:T(8,128)} custom-call(s32[1,4096]{1,0:T(1,128)} %bitcast.23, f32[16,4096]{1,0:T(8,128)} %fusion.3.refs_1_.refs_3_.wave_ref, f32[2,4096]{1,0:T(2,128)} %add_convert_fusion.refs_2_.plane_ref, f32[1024,128]{1,0:T(8,128)} %get-tuple-element.94.refs_3_, f32[24,1024]{1,0:T(8,128)} %get-tuple-element.75.refs_4_, ...), custom_call_target="tpu_custom_call" | custom-call | flops 536870912 | bytes 1500000 | tf_op jit(solution)/shard_map/wait3/pallas_call | solution.py:520
  170.9 8.5 %filter.1 = f32[64,16,128]{2,1,0:T(8,128)} custom-call(f32[1024,128]{1,0:T(8,128)} %wait3.1.pencil_ref, s32[1,4096]{1,0:T(1,128)} %bitcast.24, f32[16,4096]{1,0:T(8,128)} %fusion.3.refs_1_.refs_3_.wave_ref, f32[2,4096]{1,0:T(2,128)} %add_convert_fusion.refs_2_.plane_ref, f32[24,1024]{1,0:T(8,128)} %copy-done.13, f32[24,1024]{1,0:T(8,128)} %copy-done.18, ...), custom_call_target="tpu_custom_call" | custom-call | flops 2147483648 | bytes 11000000 | tf_op jit(solution)/shard_map/filter/pallas_call | solution.py:540
  179.4 5.5 %all-to-all-start.3 = ((f32[64,16,128]{2,1,0:T(8,128)}), f32[64,16,128]{2,1,0:T(8,128)S(1)}, u32[]{:S(2)}, u32[]{:S(2)}) async-start(f32[64,16,128]{2,1,0:T(8,128)} %filter.1), calls=%async_computation.3 | async-start | bytes 1048576 | tf_op jit(solution)/shard_map/all_to_all | solution.py:556
  184.9 7.1 %update.2.base_ref = f32[32,16,128]{2,1,0:T(8,128)} custom-call(s32[2]{0:T(128)} %pad_add_fusion.index_ref, f32[32,16,128]{2,1,0:T(8,128)} %base_ref.1, f32[32,16,4096]{2,1,0:T(8,128)} %factor_ref.1, f32[8,48,1024]{2,1,0:T(8,128)} %bitcast.19), custom_call_target="tpu_custom_call" | custom-call | flops 1207959552 | bytes 8100000 | tf_op jit(solution)/shard_map/update/pallas_call | solution.py:363
  192.0 13.5 %all-to-all-done.3.slots_ref = f32[64,16,128]{2,1,0:T(8,128)S(1)} async-done(((f32[64,16,128]{2,1,0:T(8,128)}), f32[64,16,128]{2,1,0:T(8,128)S(1)}, u32[]{:S(2)}, u32[]{:S(2)}) %all-to-all-start.3) | async-done | bytes 524320 | tf_op jit(solution)/shard_map/all_to_all | solution.py:556
  206.4 5.1 %close.1 = f32[16,4,2,1024]{3,2,1,0:T(2,128)} custom-call(f32[64,16,128]{2,1,0:T(8,128)} %copy-done.9, bf16[1024,1024]{1,0:T(8,128)(2,1)} %constant.132.clone.high_ref, bf16[1024,1024]{1,0:T(8,128)(2,1)} %constant.133.clone.low_ref), custom_call_target="tpu_custom_call" | custom-call | flops 805306368 | bytes 5500000 | tf_op jit(solution)/shard_map/close/pallas_call | solution.py:559
  211.5 5.7 %all-gather.11.cloned.1.call-done = f32[256,1024]{1,0:T(8,128)} async-done(((f32[32,1024]{1,0:T(8,128)}), f32[256,1024]{1,0:T(8,128)}) %all-gather.11.cloned.1.call-update) | async-done | bytes 1048592 | tf_op jit(solution)/shard_map/all_gather | solution.py:555
  217.2 4.6 %update.3 = f32[32,16,128]{2,1,0:T(8,128)} custom-call(s32[2]{0:T(128)} %pad_add_fusion.index_ref, f32[32,16,128]{2,1,0:T(8,128)} %update.2.base_ref, f32[32,16,4096]{2,1,0:T(8,128)} %factor_ref.1, f32[8,32,1024]{2,1,0:T(8,128)} %bitcast.20), custom_call_target="tpu_custom_call" | custom-call | flops 402653184 | bytes 2700000 | tf_op jit(solution)/shard_map/update/pallas_call | solution.py:363
  (158 shorter events, 70.1 us)
Async XLA Ops:
  7.2 89.0 %all-gather.7.cloned.1.call-start = ((), (), s32[]{:S(2)}) async-start(), calls=%async_computation.4 | async-start | bytes 3538944 | tf_op jit(solution)/shard_map/all_gather | solution.py:420
  11.3 13.2 %all-to-all-start = ((f32[8,64,128]{2,1,0:T(8,128)}), f32[8,64,128]{2,1,0:T(8,128)S(1)}, u32[]{:S(2)}, u32[]{:S(2)}) async-start(f32[8,64,128]{2,1,0:T(8,128)} %get-tuple-element.57), calls=%async_computation | async-start | bytes 524288 | tf_op jit(solution)/shard_map/all_to_all | solution.py:405
  18.0 6.5 %collective-permute-start.1 = (f32[64,128]{1,0:T(8,128)S(1)}, f32[64,128]{1,0:T(8,128)S(1)}, u32[]{:S(2)}, u32[]{:S(2)}) collective-permute-start(f32[64,128]{1,0:T(8,128)S(1)} %copy-done.32), channel_id=1, source_target_pairs={{0,1},{1,2},{2,3},{3,0},{4,5},{5,6},{6,7},{7,4},{8,9},{9,10},{10,1... | collective-permute-start | bytes 98312 | tf_op jit(solution)/shard_map/ppermute | solution.py:422
  18.5 6.0 %collective-permute-start.2 = (f32[64,128]{1,0:T(8,128)S(1)}, f32[64,128]{1,0:T(8,128)S(1)}, u32[]{:S(2)}, u32[]{:S(2)}) collective-permute-start(f32[64,128]{1,0:T(8,128)S(1)} %copy-done.32), channel_id=1, source_target_pairs={{0,2},{1,3},{2,0},{3,1},{4,6},{5,7},{6,4},{7,5},{8,10},{9,11},{10,... | collective-permute-start | bytes 98312 | tf_op jit(solution)/shard_map/ppermute | solution.py:422
  30.3 33.2 %all-to-all-start.1 = ((f32[8,160,128]{2,1,0:T(8,128)}), f32[8,160,128]{2,1,0:T(8,128)S(1)}, u32[]{:S(2)}, u32[]{:S(2)}) async-start(f32[8,160,128]{2,1,0:T(8,128)} %bundle.1), calls=%async_computation.1 | async-start | bytes 1310720 | tf_op jit(solution)/shard_map/all_to_all | solution.py:435
  37.9 147.1 %all-gather.9.cloned.1.call-start = ((), (), s32[]{:S(2)}) async-start(), calls=%async_computation.5 | async-start | bytes 1769472 | tf_op jit(solution)/shard_map/all_gather | solution.py:517
  63.6 8.2 %collective-permute-start.4 = (f32[8,64,128]{2,1,0:T(8,128)S(1)}, f32[8,64,128]{2,1,0:T(8,128)S(1)}, u32[]{:S(2)}, u32[]{:S(2)}) collective-permute-start(f32[8,64,128]{2,1,0:T(8,128)S(1)} %get-tuple-element.111.refs_0_.refs_1_), channel_id=1, source_target_pairs={{0,1},{1,2},{2,3},{3,0},{4,5},{5,6},{6,7},{7,4},{8,9},{9,10},{10,1... | collective-permute-start | bytes 786440 | tf_op jit(solution)/shard_map/ppermute | solution.py:469
  65.3 13.4 %collective-permute-start.5 = (f32[8,64,128]{2,1,0:T(8,128)S(1)}, f32[8,64,128]{2,1,0:T(8,128)S(1)}, u32[]{:S(2)}, u32[]{:S(2)}) collective-permute-start(f32[8,64,128]{2,1,0:T(8,128)S(1)} %get-tuple-element.111.refs_0_.refs_1_), channel_id=1, source_target_pairs={{0,2},{1,3},{2,0},{3,1},{4,6},{5,7},{6,4},{7,5},{8,10},{9,11},{10,... | collective-permute-start | bytes 786440 | tf_op jit(solution)/shard_map/ppermute | solution.py:469
  68.8 9.9 %collective-permute-start.6 = (f32[8,64,128]{2,1,0:T(8,128)S(1)}, f32[8,64,128]{2,1,0:T(8,128)S(1)}, u32[]{:S(2)}, u32[]{:S(2)}) collective-permute-start(f32[8,64,128]{2,1,0:T(8,128)S(1)} %get-tuple-element.111.refs_0_.refs_1_), channel_id=1, source_target_pairs={{0,3},{1,0},{2,1},{3,2},{4,7},{5,4},{6,5},{7,6},{8,11},{9,8},{10,9... | collective-permute-start | bytes 786440 | tf_op jit(solution)/shard_map/ppermute | solution.py:469
  88.8 7.4 %collective-permute-start.8 = (f32[24,1024]{1,0:T(8,128)S(1)}, f32[24,1024]{1,0:T(8,128)S(1)}, u32[]{:S(2)}, u32[]{:S(2)}) collective-permute-start(f32[24,1024]{1,0:T(8,128)S(1)} %add.112.a_ref), channel_id=1, source_target_pairs={{0,8},{8,16},{16,24},{24,0},{1,9},{9,17},{17,25},{25,1},{2,10},{10... | collective-permute-start | bytes 294920 | tf_op jit(solution)/shard_map/ppermute | solution.py:351
  88.8 7.3 %collective-permute-start.9 = (f32[24,1024]{1,0:T(8,128)S(1)}, f32[24,1024]{1,0:T(8,128)S(1)}, u32[]{:S(2)}, u32[]{:S(2)}) collective-permute-start(f32[24,1024]{1,0:T(8,128)S(1)} %add.112.a_ref), channel_id=1, source_target_pairs={{0,16},{8,24},{16,0},{24,8},{1,17},{9,25},{17,1},{25,9},{2,18},{10... | collective-permute-start | bytes 294920 | tf_op jit(solution)/shard_map/ppermute | solution.py:351
  100.5 14.5 %collective-permute-start.15 = (f32[8,64,128]{2,1,0:T(8,128)S(1)}, f32[8,64,128]{2,1,0:T(8,128)S(1)}, u32[]{:S(2)}, u32[]{:S(2)}) collective-permute-start(f32[8,64,128]{2,1,0:T(8,128)S(1)} %get-tuple-element.110.refs_0_.refs_1_), channel_id=1, source_target_pairs={{0,1},{1,2},{2,3},{3,0},{4,5},{5,6},{6,7},{7,4},{8,9},{9,10},{10,1... | collective-permute-start | bytes 786440 | tf_op jit(solution)/shard_map/ppermute | solution.py:469
  101.5 14.3 %collective-permute-start.16 = (f32[8,64,128]{2,1,0:T(8,128)S(1)}, f32[8,64,128]{2,1,0:T(8,128)S(1)}, u32[]{:S(2)}, u32[]{:S(2)}) collective-permute-start(f32[8,64,128]{2,1,0:T(8,128)S(1)} %get-tuple-element.110.refs_0_.refs_1_), channel_id=1, source_target_pairs={{0,2},{1,3},{2,0},{3,1},{4,6},{5,7},{6,4},{7,5},{8,10},{9,11},{10,... | collective-permute-start | bytes 786440 | tf_op jit(solution)/shard_map/ppermute | solution.py:469
  103.8 12.0 %collective-permute-start.17 = (f32[8,64,128]{2,1,0:T(8,128)S(1)}, f32[8,64,128]{2,1,0:T(8,128)S(1)}, u32[]{:S(2)}, u32[]{:S(2)}) collective-permute-start(f32[8,64,128]{2,1,0:T(8,128)S(1)} %get-tuple-element.110.refs_0_.refs_1_), channel_id=1, source_target_pairs={{0,3},{1,0},{2,1},{3,2},{4,7},{5,4},{6,5},{7,6},{8,11},{9,8},{10,9... | collective-permute-start | bytes 786440 | tf_op jit(solution)/shard_map/ppermute | solution.py:469
  105.1 6.1 %collective-permute-start.12 = (f32[24,1024]{1,0:T(8,128)S(1)}, f32[24,1024]{1,0:T(8,128)S(1)}, u32[]{:S(2)}, u32[]{:S(2)}) collective-permute-start(f32[24,1024]{1,0:T(8,128)S(1)} %add.113.a_ref), channel_id=1, source_target_pairs={{0,8},{8,16},{16,24},{24,0},{1,9},{9,17},{17,25},{25,1},{2,10},{10... | collective-permute-start | bytes 294920 | tf_op jit(solution)/shard_map/ppermute | solution.py:351
  105.2 8.9 %collective-permute-start.13 = (f32[24,1024]{1,0:T(8,128)S(1)}, f32[24,1024]{1,0:T(8,128)S(1)}, u32[]{:S(2)}, u32[]{:S(2)}) collective-permute-start(f32[24,1024]{1,0:T(8,128)S(1)} %add.113.a_ref), channel_id=1, source_target_pairs={{0,16},{8,24},{16,0},{24,8},{1,17},{9,25},{17,1},{25,9},{2,18},{10... | collective-permute-start | bytes 294920 | tf_op jit(solution)/shard_map/ppermute | solution.py:351
  124.5 7.0 %collective-permute-start.19 = (f32[24,1024]{1,0:T(8,128)S(1)}, f32[24,1024]{1,0:T(8,128)S(1)}, u32[]{:S(2)}, u32[]{:S(2)}) collective-permute-start(f32[24,1024]{1,0:T(8,128)S(1)} %add.114.a_ref), channel_id=1, source_target_pairs={{0,8},{8,16},{16,24},{24,0},{1,9},{9,17},{17,25},{25,1},{2,10},{10... | collective-permute-start | bytes 294920 | tf_op jit(solution)/shard_map/ppermute | solution.py:351
  124.6 6.9 %collective-permute-start.20 = (f32[24,1024]{1,0:T(8,128)S(1)}, f32[24,1024]{1,0:T(8,128)S(1)}, u32[]{:S(2)}, u32[]{:S(2)}) collective-permute-start(f32[24,1024]{1,0:T(8,128)S(1)} %add.114.a_ref), channel_id=1, source_target_pairs={{0,16},{8,24},{16,0},{24,8},{1,17},{9,25},{17,1},{25,9},{2,18},{10... | collective-permute-start | bytes 294920 | tf_op jit(solution)/shard_map/ppermute | solution.py:351
  137.0 28.7 %all-to-all-start.2 = ((f32[64,16,128]{2,1,0:T(8,128)}), f32[64,16,128]{2,1,0:T(8,128)S(1)}, u32[]{:S(2)}, u32[]{:S(2)}) async-start(f32[64,16,128]{2,1,0:T(8,128)} %noise.1), calls=%async_computation.2 | async-start | bytes 1048576 | tf_op jit(solution)/shard_map/all_to_all | solution.py:470
  142.7 74.5 %all-gather.11.cloned.1.call-start = ((), (), s32[]{:S(2)}) async-start(), calls=%async_computation.6 | async-start | bytes 1179648 | tf_op jit(solution)/shard_map/all_gather | solution.py:555
  145.6 24.4 %collective-permute-start.23 = (f32[24,1024]{1,0:T(8,128)S(1)}, f32[24,1024]{1,0:T(8,128)S(1)}, u32[]{:S(2)}, u32[]{:S(2)}) collective-permute-start(f32[24,1024]{1,0:T(8,128)S(1)} %add.115.a_ref), channel_id=1, source_target_pairs={{0,8},{8,16},{16,24},{24,0},{1,9},{9,17},{17,25},{25,1},{2,10},{10... | collective-permute-start | bytes 294920 | tf_op jit(solution)/shard_map/ppermute | solution.py:351
  146.9 23.1 %collective-permute-start.24 = (f32[24,1024]{1,0:T(8,128)S(1)}, f32[24,1024]{1,0:T(8,128)S(1)}, u32[]{:S(2)}, u32[]{:S(2)}) collective-permute-start(f32[24,1024]{1,0:T(8,128)S(1)} %add.115.a_ref), channel_id=1, source_target_pairs={{0,16},{8,24},{16,0},{24,8},{1,17},{9,25},{17,1},{25,9},{2,18},{10... | collective-permute-start | bytes 294920 | tf_op jit(solution)/shard_map/ppermute | solution.py:351
  149.3 20.7 %collective-permute-start.25 = (f32[24,1024]{1,0:T(8,128)S(1)}, f32[24,1024]{1,0:T(8,128)S(1)}, u32[]{:S(2)}, u32[]{:S(2)}) collective-permute-start(f32[24,1024]{1,0:T(8,128)S(1)} %add.115.a_ref), channel_id=1, source_target_pairs={{0,24},{8,0},{16,8},{24,16},{1,25},{9,1},{17,9},{25,17},{2,26},{10... | collective-permute-start | bytes 294920 | tf_op jit(solution)/shard_map/ppermute | solution.py:351
  179.4 26.2 %all-to-all-start.3 = ((f32[64,16,128]{2,1,0:T(8,128)}), f32[64,16,128]{2,1,0:T(8,128)S(1)}, u32[]{:S(2)}, u32[]{:S(2)}) async-start(f32[64,16,128]{2,1,0:T(8,128)} %filter.1), calls=%async_computation.3 | async-start | bytes 1048576 | tf_op jit(solution)/shard_map/all_to_all | solution.py:556
  (45 other events, 258.3 us)
Sparse Core Ops, SparseCore 0:
  11.4 62.7 all-gather.6
  137.1 39.3 all-gather.8
  178.4 38.7 all-gather.10

commit v2 on v1

--- a/solution.py
+++ b/solution.py
@@ -118,7 +118,7 @@
 
 
 def bundle_kernel(index_ref, columns_ref, *refs):
-    side_refs, out_ref = refs[:4], refs[4]
+    side_refs, extra_ref, out_ref = refs[:4], refs[4], refs[5]
     lane = lax.broadcasted_iota(jnp.int32, (64, 128), 1)
     weights = jnp.zeros((64, 128), F32)
     for step, ref in enumerate(side_refs):
@@ -133,6 +133,7 @@
         out_ref[z, 0:64] = quarter[0]
         out_ref[z, 64:128] = quarter[1]
         out_ref[z, 128:160] = jnp.transpose(jnp.concatenate([rows, rows]))[:32]
+        out_ref[z, 160:176] = extra_ref[...]
 
 
 def spread(work, index_ref, inverse_refs, out_ref, high_ref, low_ref):
@@ -163,9 +164,14 @@
     spread(side_ref[0], index_ref, inverse_refs, out_ref, high_ref, low_ref)
 
 
-def step_kernel(index_ref, start_ref, a_ref, b_ref, c_ref, d_ref, factor_ref, *refs):
-    inverse_refs, (out_ref, unknown_ref, high_ref, low_ref) = refs[:8], refs[8:]
+def step_kernel(panel, index_ref, start_ref, a_ref, b_ref, c_ref, d_ref, factor_ref, *refs):
+    inverse_refs, refs = refs[:8], refs[8:]
     unknown = (a_ref[...] + b_ref[...]) + (c_ref[...] + d_ref[...])
+    if panel == 2:
+        older_ref, refs = refs[0], refs[1:]
+        refs[2][0:16] = older_ref[0:16]
+        refs[2][16:32] = unknown[0:16]
+    out_ref, unknown_ref, high_ref, low_ref = refs[0], refs[1], refs[-2], refs[-1]
     unknown_ref[...] = unknown
     work = start_ref[0] - dot_nt(unknown, factor_ref[...].reshape(128, LENGTH))
     spread(work, index_ref, inverse_refs, out_ref, high_ref, low_ref)
@@ -189,9 +195,12 @@
         return choose(high) + (choose(middle) + choose(low))
 
     wanted = exact(spectrum_ref[...], lambda part: dot(part, pick, NN))
-    wanted = wanted + exact(
-        jnp.transpose(extra_ref[...]), lambda part: dot(part, extra_pick, NN)
-    )
+    extra = [
+        jnp.concatenate([extra_ref[0, 8 * y + t : 8 * y + t + 1] for t in range(8)], axis=1)
+        for y in range(2)
+    ]
+    extra = jnp.concatenate(extra + [jnp.zeros((6, LENGTH), F32)])
+    wanted = wanted + exact(jnp.transpose(extra), lambda part: dot(part, extra_pick, NN))
     at_row = lax.broadcasted_iota(jnp.int32, (512, 512), 0)
     at_col = lax.broadcasted_iota(jnp.int32, (512, 512), 1)
     mirror = jnp.where(at_row + at_col == 512, 1.0, 0.0).astype(BF16)
@@ -226,13 +235,14 @@
     cell_ref, wave_ref, plane_ref, pencil_ref = refs[:4]
     unknown_refs, refs = refs[4 : 4 + panel], refs[4 + panel :]
     weights = unknown_refs[-1][16:20]
-    pencil = 0.0 if panel == 1 else pencil_ref[...]
+    pencil = pencil_ref[...].reshape(LENGTH, 128)
+    pencil = swap_groups(pencil) if panel == 1 else pencil
+    pencil = add_weights(pencil, cell_ref, wave_ref, plane_ref, weights)
     if panel == 3:
-        pencil = pencil + swap_groups(refs[0][...].reshape(LENGTH, 128))
-        refs[1][...] = add_weights(pencil, cell_ref, wave_ref, plane_ref, weights)
+        refs[0][...] = pencil
         return
     side_ref, factor_refs, (out_ref, work_ref) = refs[0], refs[1:-2], refs[-2:]
-    out_ref[...] = add_weights(pencil, cell_ref, wave_ref, plane_ref, weights)
+    out_ref[...] = pencil
     work = side_ref[0]
     for ref, factor_ref in zip(unknown_refs, factor_refs):
         work = work - dot_nt(ref[...], factor_ref[...].reshape(128, LENGTH))
@@ -403,10 +413,7 @@
     tie((box, (0, 1, 2)))
     columns, side, factor = box
     columns = lax.all_to_all(columns, ("x", "core"), 0, 0)
-    extra = lax.ppermute(spectrum[:, :, 0].T, WIDE, [(32, 0)])
-    box = [columns, extra]
-    tie((box, (0, 1)))
-    columns, extra = box
+    extra = spectrum[:, :, 0].T.reshape(16, 128)
 
     lower = call(
         lower_kernel,
@@ -423,12 +430,12 @@
     quarter = call(
         bundle_kernel,
         "bundle",
-        [SMEM, spec(8, 64, 128)] + [spec(64, 128)] * 4,
-        spec(8, 160, 128),
-        shape_of(8, 160, 128),
+        [SMEM, spec(8, 64, 128)] + [spec(64, 128)] * 4 + [spec(16, 128)],
+        spec(8, 176, 128),
+        shape_of(8, 176, 128),
         0,
         1_500_000,
-    )(index, columns, *sides)
+    )(index, columns, *sides, extra)
     box = [quarter, noise, spectrum, obs_cells]
     tie((box, (0, 1, 2, 3)))
     quarter, noise, spectrum, obs_cells = box
@@ -445,26 +452,15 @@
         grid=4,
     )(noise.reshape(128, LENGTH), z_high, z_low)
 
-    extra = jnp.concatenate([extra, jnp.zeros((6, LENGTH), F32)])
-    even, odd = call(
-        spectrum_kernel,
-        "spectrum",
-        [SMEM, spec(LENGTH, 32), spec(8, LENGTH)],
-        [spec(LENGTH, 128), spec(512, 128)],
-        [shape_of(LENGTH, 128), shape_of(512, 128)],
-        300_000_000,
-        1_500_000,
-    )(index, spectrum.reshape(LENGTH, 32), extra)
-
     cell_x = (obs_cells // (8 * LENGTH)).reshape(1, 4096)
     plane = obs_cells // LENGTH % 8 - 2 * lax.axis_index("y")
     planes = jnp.stack([plane == 0, plane == 1]).astype(F32)
     freq, phase = z_frequencies(wide, jnp)
     turn = (freq[:, None] * (obs_cells % LENGTH)[None, :] + phase[:, None]) % LENGTH
     waves = jnp.cos(turn.astype(F32) * (2.0 * math.pi / LENGTH))
-    box = [quarter, slab, even, odd, cell_x, planes, waves]
-    tie((box, tuple(range(7))))
-    quarter, slab, even, odd, cell_x, planes, waves = box
+    box = [quarter, slab, spectrum, cell_x, planes, waves]
+    tie((box, tuple(range(6))))
+    quarter, slab, spectrum, cell_x, planes, waves = box
     own = [quarter[:, 0:64], quarter[:, 64:128]]
     own = [[one] + [lax.ppermute(one, "y", ring(4, step)) for step in (1, 2, 3)] for one in own]
     slab = lax.all_to_all(slab, WIDE, 0, 0)
@@ -477,7 +473,7 @@
     side_spec = lambda k: block_at((1, COLS, 128), (k, 0, 0))
     factor_spec = lambda k, j: block_at((8, 16, LENGTH), (0, k * (k - 1) // 2 + j, 0))
     inverse_specs = lambda k: [block_at((8, 16, 128), (0, k % 2 + a, 0)) for a in (0, 2)] * 4
-    inverses = [[one for one in own[k // 2] for _ in range(2)] for k in range(4)]
+    inverses = lambda k: [one for one in own[k // 2] for _ in range(2)]
     inverse_scratch = [pltpu.VMEM((8, 128, 128), BF16)] * 2
     panel_spec = spec(COLS, LENGTH)
     panel_shape = shape_of(COLS, LENGTH)
@@ -492,45 +488,61 @@
         20_000_000,
         1_200_000,
         inverse_scratch,
-    )(index, quarter, *inverses[0])
+    )(index, quarter, *inverses(0))
+    box = [partial, spectrum]
+    tie((box, (0, 1)))
+    partial, spectrum = box
     parts = share(partial)
+    even, odd = call(
+        spectrum_kernel,
+        "spectrum",
+        [SMEM, spec(LENGTH, 32), block_at((1, 16, 128), (4, 10, 0))],
+        [spec(LENGTH, 128), spec(512, 128)],
+        [shape_of(LENGTH, 128), shape_of(512, 128)],
+        300_000_000,
+        1_500_000,
+    )(index, spectrum.reshape(LENGTH, 32), quarter)
+    box = [even, odd]
+    tie((parts, (0, 1, 2, 3)), (own[1], (1, 2, 3)), (box, (0, 1)))
+    even, odd = box
     unknowns = []
     work = sides
-    pencil = waves
+    pencil = slab
     for panel in range(1, 4):
-        partial, unknown = call(
-            step_kernel,
+        partial, unknown, *pair = call(
+            functools.partial(step_kernel, panel),
             f"step{panel}",
             [SMEM, side_spec(1 if panel == 1 else 0)]
             + [panel_spec] * 4
             + [factor_spec(panel, panel - 1)]
-            + inverse_specs(panel),
-            [panel_spec] * 2,
-            [panel_shape] * 2,
+            + inverse_specs(panel)
+            + [panel_spec] * (panel == 2),
+            [panel_spec] * 2 + [spec(32, LENGTH)] * (panel == 2),
+            [panel_shape] * 2 + [shape_of(32, LENGTH)] * (panel == 2),
             40_000_000,
             1_500_000,
             inverse_scratch,
-        )(index, work, *parts, lower, *inverses[panel])
+        )(index, work, *parts, lower, *inverses(panel), *unknowns[:1] * (panel == 2))
         unknowns.append(unknown)
         parts = share(partial)
-        if panel == 3:
-            early = lax.all_gather(jnp.concatenate([u[:16] for u in unknowns]), "z")
+        if panel == 2:
+            early = lax.all_gather(pair[0], "z")
         later = panel < 3
         box = list(
             call(
                 functools.partial(wait_kernel, panel),
                 f"wait{panel}",
                 obs_specs(panel - 1)
-                + [spec(16, 128) if panel == 1 else pencil_spec]
+                + [spec(64, 16, 128) if panel == 1 else pencil_spec]
                 + [panel_spec] * panel
-                + ([side_spec(panel + 1)] if later else [spec(64, 16, 128)])
+                + [side_spec(panel + 1)] * later
                 + [factor_spec(panel + 1, j) for j in range(panel)] * later,
                 [pencil_spec] + [spec(1, COLS, 128)] * later,
                 [shape_of(LENGTH, 128)] + [shape_of(1, COLS, 128)] * later,
                 2 * 2 * 128 * LENGTH * LENGTH,
                 1_500_000,
             )(
-                cell_x, waves, planes, pencil, *unknowns, sides if later else slab,
+                cell_x, waves, planes, pencil, *unknowns, *[sides] * later,
                 *[lower] * (panel * later),
             )
         )
@@ -552,9 +564,9 @@
         [TABLE] * 4 + [pltpu.SemaphoreType.DMA((4,))],
     )(pencil, cell_x, waves, planes, *parts, x_high, x_low, back_high, back_low, even, odd)
     late = (parts[0][:16] + parts[1][:16]) + (parts[2][:16] + parts[3][:16])
-    late = lax.all_gather(jnp.concatenate([late, jnp.zeros((16, LENGTH), F32)]), "z")
+    late = lax.all_gather(jnp.concatenate([unknowns[2][:16], late]), "z")
     slots = lax.all_to_all(slots, WIDE, 0, 0)
-    solved = update(0, 3, index, right_side, factor, early)
+    solved = update(0, 2, index, right_side, factor, early)
     slots, solved = lax.optimization_barrier((slots, solved))
     correction = call(
         close_kernel,
@@ -568,7 +580,7 @@
         grid=4,
     )(slots, z_high, z_low)
     solved, correction = lax.optimization_barrier((solved, correction))
-    solved = update(3, 1, index, solved, factor, late)
+    solved = update(2, 2, index, solved, factor, late)
     return (solved, correction)
 
 

time: 232 us -> 219 us (0.944)
  waiting for transfers between devices: 72.8 us -> 60.3 us
  starting transfers between devices: 61.3 us -> 64.8 us
  local copies, waits for them, and re-layouts: 12.3 us -> 9.66 us
    all_to_all x1, waiting for transfers between devices: 15.2 us -> 0.01 us  [per_device(): slab = lax.all_to_all(slab, WIDE, 0, 0)]
    all_to_all x1, waiting for transfers between devices: 13.2 us -> 21.3 us  [per_device(): quarter = lax.all_to_all(quarter, 'z', 0, 0)]
    ppermute x12, waiting for transfers between devices: 10.9 us -> 3.02 us  [share(): lax.ppermute(total, 'x', ring(4, step))]
    all_to_all x1, starting transfers between devices: 5.55 us -> 10.5 us  [per_device(): slots = lax.all_to_all(slots, WIDE, 0, 0)]
    ppermute x6, starting transfers between devices: 9.88 us -> 6.12 us  [per_device(): lax.ppermute(one, 'y', ring(4, step))]
    unnamed x73 -> x71, local copies, waits for them, and re-layouts: 7 us -> 5.97 us
  transfers between devices with their start and end apart: 33 -> 32, of which waited for: 16 -> 17; matrix products, arithmetic and copies ran while one was open for 5% -> 5% of each run, Pallas kernels for 19% -> 22%
where the time goes in v2:
time: 219 us; the launch traced here: 216 us
  starting transfers between devices  64.8 us (30%)
  waiting for transfers between devices  60.3 us (28%)
  Pallas kernels  59.4 us (27%)
  between operations  14.1 us (6%)
  local copies, waits for them, and re-layouts  9.66 us (4%)
  other arithmetic  8 us (4%)
    all_to_all x1, waiting for transfers between devices, per_device(): quarter = lax.all_to_all(quarter, 'z', 0, 0)  21.3 us
    ppermute x12, starting transfers between devices, share(): lax.ppermute(total, 'x', ring(4, step))  15.1 us
    all_to_all x1, waiting for transfers between devices, per_device(): slots = lax.all_to_all(slots, WIDE, 0, 0)  14.8 us
    pallas_call x2, Pallas kernels, update(): call(functools.partial(update_kernel, first_panel, panels), 'update', [SM...  11.5 us
    all_to_all x1, starting transfers between devices, per_device(): slots = lax.all_to_all(slots, WIDE, 0, 0)  10.5 us
    pallas_call x3, Pallas kernels, per_device(): call(functools.partial(wait_kernel, panel), f'wait{panel}', obs_specs(pan...  9.55 us
    ppermute x6, waiting for transfers between devices, per_device(): lax.ppermute(one, 'y', ring(4, step))  9.15 us
    pallas_call x1, Pallas kernels, per_device(): call(filter_kernel, 'filter', [spec(LENGTH, 128)] + obs_specs(3) + [panel...  8.44 us
  transfers between devices with their start and end apart: 32, of which 17 were waited for; matrix products, arithmetic and copies ran while one was open for 5% of the time, Pallas kernels for 22%

profile of v2, /device:TPU:1, one launch (start us, length us, event | category | flops | bytes accessed | tf_op | source)
XLA Modules:
  0.0 216.3 jit_solution(974388690836789164)
XLA Ops:
  11.3 6.7 %all-to-all-start = ((f32[8,64,128]{2,1,0:T(8,128)}), f32[8,64,128]{2,1,0:T(8,128)S(1)}, u32[]{:S(2)}, u32[]{:S(2)}) async-start(f32[8,64,128]{2,1,0:T(8,128)} %get-tuple-element.66), calls=%async_computation | async-start | bytes 524288 | tf_op jit(solution)/shard_map/all_to_all | solution.py:415
  18.5 2.6 %collective-permute-start.1 = (f32[64,128]{1,0:T(8,128)S(1)}, f32[64,128]{1,0:T(8,128)S(1)}, u32[]{:S(2)}, u32[]{:S(2)}) collective-permute-start(f32[64,128]{1,0:T(8,128)S(1)} %copy-done.31), channel_id=1, source_target_pairs={{0,2},{1,3},{2,0},{3,1},{4,6},{5,7},{6,4},{7,5},{8,10},{9,11},{10,... | collective-permute-start | bytes 98312 | tf_op jit(solution)/shard_map/ppermute | solution.py:429
  29.0 8.2 %all-to-all-start.1 = ((f32[8,176,128]{2,1,0:T(8,128)}), f32[8,176,128]{2,1,0:T(8,128)S(1)}, u32[]{:S(2)}, u32[]{:S(2)}) async-start(f32[8,176,128]{2,1,0:T(8,128)} %bundle.1), calls=%async_computation.1 | async-start | bytes 1441792 | tf_op jit(solution)/shard_map/all_to_all | solution.py:442
  37.2 4.9 %noise.1 = f32[64,16,128]{2,1,0:T(8,128)} custom-call(f32[128,1024]{1,0:T(8,128)} %reshape.57.noise_ref, bf16[1024,1024]{1,0:T(8,128)(2,1)} %constant.129.clone.high_ref, bf16[1024,1024]{1,0:T(8,128)(2,1)} %constant.130.clone.low_ref), custom_call_target="tpu_custom_call" | custom-call | flops 805306368 | bytes 5000000 | tf_op jit(solution)/shard_map/noise/pallas_call | solution.py:444
  45.0 21.3 %all-to-all-done.1.slab_ref.extra_ref = f32[8,176,128]{2,1,0:T(8,128)S(1)} async-done(((f32[8,176,128]{2,1,0:T(8,128)}), f32[8,176,128]{2,1,0:T(8,128)S(1)}, u32[]{:S(2)}, u32[]{:S(2)}) %all-to-all-start.1) | async-done | bytes 720928 | tf_op jit(solution)/shard_map/all_to_all | solution.py:442
  66.4 7.7 %all-to-all-start.2 = ((f32[64,16,128]{2,1,0:T(8,128)}), f32[64,16,128]{2,1,0:T(8,128)S(1)}, u32[]{:S(2)}, u32[]{:S(2)}) async-start(f32[64,16,128]{2,1,0:T(8,128)} %noise.1), calls=%async_computation.2 | async-start | bytes 1048576 | tf_op jit(solution)/shard_map/all_to_all | solution.py:466
  74.3 3.4 %collective-permute-start.4 = (f32[8,64,128]{2,1,0:T(8,128)S(1)}, f32[8,64,128]{2,1,0:T(8,128)S(1)}, u32[]{:S(2)}, u32[]{:S(2)}) collective-permute-start(f32[8,64,128]{2,1,0:T(8,128)S(1)} %get-tuple-element.129.refs_0_.refs_1_), channel_id=1, source_target_pairs={{0,2},{1,3},{2,0},{3,1},{4,6},{5,7},{6,4},{7,5},{8,10},{9,11},{10,... | collective-permute-start | bytes 786440 | tf_op jit(solution)/shard_map/ppermute | solution.py:465
  79.3 3.6 %collective-permute-done.3.refs_2_.refs_3_ = f32[8,64,128]{2,1,0:T(8,128)S(1)} collective-permute-done((f32[8,64,128]{2,1,0:T(8,128)S(1)}, f32[8,64,128]{2,1,0:T(8,128)S(1)}, u32[]{:S(2)}, u32[]{:S(2)}) %collective-permute-start.3) | collective-permute-done | bytes 262176 | tf_op jit(solution)/shard_map/ppermute | solution.py:465
  83.9 5.4 %collective-permute-done.4.refs_4_.refs_5_ = f32[8,64,128]{2,1,0:T(8,128)S(1)} collective-permute-done((f32[8,64,128]{2,1,0:T(8,128)S(1)}, f32[8,64,128]{2,1,0:T(8,128)S(1)}, u32[]{:S(2)}, u32[]{:S(2)}) %collective-permute-start.4) | collective-permute-done | bytes 262176 | tf_op jit(solution)/shard_map/ppermute | solution.py:465
  103.2 3.8 %spectrum.1 = (f32[1024,128]{1,0:T(8,128)}, f32[512,128]{1,0:T(8,128)}) custom-call(s32[2]{0:T(128)} %pad_add_fusion.index_ref, f32[1024,32]{1,0:T(8,128)} %copy.15.spectrum_ref, f32[8,176,128]{2,1,0:T(8,128)} %copy-done), custom_call_target="tpu_custom_call" | custom-call | flops 300000000 | bytes 1500000 | tf_op jit(solution)/shard_map/spectrum/pallas_call | solution.py:496
  107.9 2.5 %step1.1 = (f32[24,1024]{1,0:T(8,128)}, f32[24,1024]{1,0:T(8,128)}) custom-call(s32[2]{0:T(128)} %pad_add_fusion.index_ref, f32[4,24,128]{2,1,0:T(8,128)} %get-tuple-element.73.start_ref.refs_5_.refs_6_, f32[24,1024]{1,0:T(8,128)} %copy-done.14, f32[24,1024]{1,0:T(8,128)} %copy-done.21, f32[24,1024]{1,0:T(8,128)} %copy-done.22, f32[24,1024]{1,0:T(8,128)} %copy-done.23, ...), custom_call_target="tpu_custom_call" | custom-call | flops 40000000 | bytes 1500000 | tf_op jit(solution)/shard_map/step1/pallas_call | solution.py:512
  117.6 3.5 %wait1.1 = (f32[1024,128]{1,0:T(8,128)}, f32[1,24,128]{2,1,0:T(8,128)}) custom-call(s32[1,4096]{1,0:T(1,128)} %bitcast.21, f32[16,4096]{1,0:T(8,128)} %fusion.3.refs_1_.wave_ref, f32[2,4096]{1,0:T(2,128)} %add_convert_fusion.refs_2_.plane_ref, f32[64,16,128]{2,1,0:T(8,128)} %copy-done.10, f32[24,1024]{1,0:T(8,128)} %get-tuple-element.90.refs_4_.refs_8_, ...), custom_call_target="tpu_custom_call" | custom-call | flops 536870912 | bytes 1500000 | tf_op jit(solution)/shard_map/wait1/pallas_call | solution.py:532
  122.2 2.6 %step2.1 = (f32[24,1024]{1,0:T(8,128)}, f32[24,1024]{1,0:T(8,128)}, f32[32,1024]{1,0:T(8,128)}) custom-call(s32[2]{0:T(128)} %pad_add_fusion.index_ref, f32[1,24,128]{2,1,0:T(8,128)} %get-tuple-element.93.start_ref, f32[24,1024]{1,0:T(8,128)} %copy-done.15, f32[24,1024]{1,0:T(8,128)} %copy-done.24, f32[24,1024]{1,0:T(8,128)} %copy-done.26, ...), custom_call_target="tpu_custom_call" | custom-call | flops 40000000 | bytes 1500000 | tf_op jit(solution)/shard_map/step2/pallas_call | solution.py:512
  129.0 3.2 %collective-permute-start.19 = (f32[24,1024]{1,0:T(8,128)S(1)}, f32[24,1024]{1,0:T(8,128)S(1)}, u32[]{:S(2)}, u32[]{:S(2)}) collective-permute-start(f32[24,1024]{1,0:T(8,128)S(1)} %add.110.a_ref), channel_id=1, source_target_pairs={{0,16},{8,24},{16,0},{24,8},{1,17},{9,25},{17,1},{25,9},{2,18},{10... | collective-permute-start | bytes 294920 | tf_op jit(solution)/shard_map/ppermute | solution.py:361
  132.1 3.3 %wait2.1 = (f32[1024,128]{1,0:T(8,128)}, f32[1,24,128]{2,1,0:T(8,128)}) custom-call(s32[1,4096]{1,0:T(1,128)} %bitcast.22, f32[16,4096]{1,0:T(8,128)} %fusion.3.refs_1_.wave_ref, f32[2,4096]{1,0:T(2,128)} %add_convert_fusion.refs_2_.plane_ref, f32[1024,128]{1,0:T(8,128)} %get-tuple-element.102.refs_3_, f32[24,1024]{1,0:T(8,128)} %get-tuple-element.90.refs_4_.refs_8_, ...), custom_call_target="tpu_custom_call" | custom-call | flops 536870912 | bytes 1500000 | tf_op jit(solution)/shard_map/wait2/pallas_call | solution.py:532
  143.9 2.8 %collective-permute-start.23 = (f32[24,1024]{1,0:T(8,128)S(1)}, f32[24,1024]{1,0:T(8,128)S(1)}, u32[]{:S(2)}, u32[]{:S(2)}) collective-permute-start(f32[24,1024]{1,0:T(8,128)S(1)} %add.111.a_ref), channel_id=1, source_target_pairs={{0,16},{8,24},{16,0},{24,8},{1,17},{9,25},{17,1},{25,9},{2,18},{10... | collective-permute-start | bytes 294920 | tf_op jit(solution)/shard_map/ppermute | solution.py:361
  147.5 2.7 %wait3.1.pencil_ref = f32[1024,128]{1,0:T(8,128)} custom-call(s32[1,4096]{1,0:T(1,128)} %bitcast.23, f32[16,4096]{1,0:T(8,128)} %fusion.3.refs_1_.wave_ref, f32[2,4096]{1,0:T(2,128)} %add_convert_fusion.refs_2_.plane_ref, f32[1024,128]{1,0:T(8,128)} %get-tuple-element.112.refs_3_, f32[24,1024]{1,0:T(8,128)} %get-tuple-element.90.refs_4_.refs_8_, ...), custom_call_target="tpu_custom_call" | custom-call | flops 536870912 | bytes 1500000 | tf_op jit(solution)/shard_map/wait3/pallas_call | solution.py:532
  152.3 8.4 %filter.1 = f32[64,16,128]{2,1,0:T(8,128)} custom-call(f32[1024,128]{1,0:T(8,128)} %wait3.1.pencil_ref, s32[1,4096]{1,0:T(1,128)} %bitcast.24, f32[16,4096]{1,0:T(8,128)} %fusion.3.refs_1_.wave_ref, f32[2,4096]{1,0:T(2,128)} %add_convert_fusion.refs_2_.plane_ref, f32[24,1024]{1,0:T(8,128)} %copy-done.12, f32[24,1024]{1,0:T(8,128)} %copy-done.17, ...), custom_call_target="tpu_custom_call" | custom-call | flops 2147483648 | bytes 11000000 | tf_op jit(solution)/shard_map/filter/pallas_call | solution.py:552
  160.7 10.5 %all-to-all-start.3 = ((f32[64,16,128]{2,1,0:T(8,128)}), f32[64,16,128]{2,1,0:T(8,128)S(1)}, u32[]{:S(2)}, u32[]{:S(2)}) async-start(f32[64,16,128]{2,1,0:T(8,128)} %filter.1), calls=%async_computation.3 | async-start | bytes 1048576 | tf_op jit(solution)/shard_map/all_to_all | solution.py:568
  171.2 5.8 %update.2.base_ref = f32[32,16,128]{2,1,0:T(8,128)} custom-call(s32[2]{0:T(128)} %pad_add_fusion.index_ref, f32[32,16,128]{2,1,0:T(8,128)} %base_ref.1, f32[32,16,4096]{2,1,0:T(8,128)} %factor_ref.1, f32[8,32,1024]{2,1,0:T(8,128)} %bitcast.19), custom_call_target="tpu_custom_call" | custom-call | flops 805306368 | bytes 5400000 | tf_op jit(solution)/shard_map/update/pallas_call | solution.py:373
  177.0 14.8 %all-to-all-done.3.slots_ref = f32[64,16,128]{2,1,0:T(8,128)S(1)} async-done(((f32[64,16,128]{2,1,0:T(8,128)}), f32[64,16,128]{2,1,0:T(8,128)S(1)}, u32[]{:S(2)}, u32[]{:S(2)}) %all-to-all-start.3) | async-done | bytes 524320 | tf_op jit(solution)/shard_map/all_to_all | solution.py:568
  192.6 5.1 %close.1 = f32[16,4,2,1024]{3,2,1,0:T(2,128)} custom-call(f32[64,16,128]{2,1,0:T(8,128)} %copy-done.9, bf16[1024,1024]{1,0:T(8,128)(2,1)} %constant.129.clone.high_ref, bf16[1024,1024]{1,0:T(8,128)(2,1)} %constant.130.clone.low_ref), custom_call_target="tpu_custom_call" | custom-call | flops 805306368 | bytes 5500000 | tf_op jit(solution)/shard_map/close/pallas_call | solution.py:571
  197.7 6.4 %all-gather.11.cloned.1.call-done = f32[256,1024]{1,0:T(8,128)} async-done(((f32[32,1024]{1,0:T(8,128)}), f32[256,1024]{1,0:T(8,128)}) %all-gather.11.cloned.1.call-update) | async-done | bytes 1048592 | tf_op jit(solution)/shard_map/all_gather | solution.py:567
  204.0 5.8 %update.3 = f32[32,16,128]{2,1,0:T(8,128)} custom-call(s32[2]{0:T(128)} %pad_add_fusion.index_ref, f32[32,16,128]{2,1,0:T(8,128)} %update.2.base_ref, f32[32,16,4096]{2,1,0:T(8,128)} %factor_ref.1, f32[8,32,1024]{2,1,0:T(8,128)} %bitcast.20), custom_call_target="tpu_custom_call" | custom-call | flops 805306368 | bytes 5400000 | tf_op jit(solution)/shard_map/update/pallas_call | solution.py:373
  (151 shorter events, 57.3 us)
Async XLA Ops:
  7.2 100.0 %all-gather.7.cloned.1.call-start = ((), (), s32[]{:S(2)}) async-start(), calls=%async_computation.4 | async-start | bytes 3538944 | tf_op jit(solution)/shard_map/all_gather | solution.py:427
  11.3 13.2 %all-to-all-start = ((f32[8,64,128]{2,1,0:T(8,128)}), f32[8,64,128]{2,1,0:T(8,128)S(1)}, u32[]{:S(2)}, u32[]{:S(2)}) async-start(f32[8,64,128]{2,1,0:T(8,128)} %get-tuple-element.66), calls=%async_computation | async-start | bytes 524288 | tf_op jit(solution)/shard_map/all_to_all | solution.py:415
  18.0 5.5 %collective-permute-start = (f32[64,128]{1,0:T(8,128)S(1)}, f32[64,128]{1,0:T(8,128)S(1)}, u32[]{:S(2)}, u32[]{:S(2)}) collective-permute-start(f32[64,128]{1,0:T(8,128)S(1)} %copy-done.31), channel_id=1, source_target_pairs={{0,1},{1,2},{2,3},{3,0},{4,5},{5,6},{6,7},{7,4},{8,9},{9,10},{10,1... | collective-permute-start | bytes 98312 | tf_op jit(solution)/shard_map/ppermute | solution.py:429
  29.0 37.4 %all-to-all-start.1 = ((f32[8,176,128]{2,1,0:T(8,128)}), f32[8,176,128]{2,1,0:T(8,128)S(1)}, u32[]{:S(2)}, u32[]{:S(2)}) async-start(f32[8,176,128]{2,1,0:T(8,128)} %bundle.1), calls=%async_computation.1 | async-start | bytes 1441792 | tf_op jit(solution)/shard_map/all_to_all | solution.py:442
  66.4 50.5 %all-to-all-start.2 = ((f32[64,16,128]{2,1,0:T(8,128)}), f32[64,16,128]{2,1,0:T(8,128)S(1)}, u32[]{:S(2)}, u32[]{:S(2)}) async-start(f32[64,16,128]{2,1,0:T(8,128)} %noise.1), calls=%async_computation.2 | async-start | bytes 1048576 | tf_op jit(solution)/shard_map/all_to_all | solution.py:466
  74.1 97.1 %all-gather.9.cloned.1.call-start = ((), (), s32[]{:S(2)}) async-start(), calls=%async_computation.5 | async-start | bytes 1179648 | tf_op jit(solution)/shard_map/all_gather | solution.py:529
  74.2 8.7 %collective-permute-start.3 = (f32[8,64,128]{2,1,0:T(8,128)S(1)}, f32[8,64,128]{2,1,0:T(8,128)S(1)}, u32[]{:S(2)}, u32[]{:S(2)}) collective-permute-start(f32[8,64,128]{2,1,0:T(8,128)S(1)} %get-tuple-element.129.refs_0_.refs_1_), channel_id=1, source_target_pairs={{0,1},{1,2},{2,3},{3,0},{4,5},{5,6},{6,7},{7,4},{8,9},{9,10},{10,1... | collective-permute-start | bytes 786440 | tf_op jit(solution)/shard_map/ppermute | solution.py:465
  74.3 15.0 %collective-permute-start.4 = (f32[8,64,128]{2,1,0:T(8,128)S(1)}, f32[8,64,128]{2,1,0:T(8,128)S(1)}, u32[]{:S(2)}, u32[]{:S(2)}) collective-permute-start(f32[8,64,128]{2,1,0:T(8,128)S(1)} %get-tuple-element.129.refs_0_.refs_1_), channel_id=1, source_target_pairs={{0,2},{1,3},{2,0},{3,1},{4,6},{5,7},{6,4},{7,5},{8,10},{9,11},{10,... | collective-permute-start | bytes 786440 | tf_op jit(solution)/shard_map/ppermute | solution.py:465
  77.7 11.8 %collective-permute-start.5 = (f32[8,64,128]{2,1,0:T(8,128)S(1)}, f32[8,64,128]{2,1,0:T(8,128)S(1)}, u32[]{:S(2)}, u32[]{:S(2)}) collective-permute-start(f32[8,64,128]{2,1,0:T(8,128)S(1)} %get-tuple-element.129.refs_0_.refs_1_), channel_id=1, source_target_pairs={{0,3},{1,0},{2,1},{3,2},{4,7},{5,4},{6,5},{7,6},{8,11},{9,8},{10,9... | collective-permute-start | bytes 786440 | tf_op jit(solution)/shard_map/ppermute | solution.py:465
  77.7 23.4 %collective-permute-start.10 = (f32[8,64,128]{2,1,0:T(8,128)S(1)}, f32[8,64,128]{2,1,0:T(8,128)S(1)}, u32[]{:S(2)}, u32[]{:S(2)}) collective-permute-start(f32[8,64,128]{2,1,0:T(8,128)S(1)} %get-tuple-element.128.refs_0_.refs_1_), channel_id=1, source_target_pairs={{0,1},{1,2},{2,3},{3,0},{4,5},{5,6},{6,7},{7,4},{8,9},{9,10},{10,1... | collective-permute-start | bytes 786440 | tf_op jit(solution)/shard_map/ppermute | solution.py:465
  79.1 27.9 %collective-permute-start.11 = (f32[8,64,128]{2,1,0:T(8,128)S(1)}, f32[8,64,128]{2,1,0:T(8,128)S(1)}, u32[]{:S(2)}, u32[]{:S(2)}) collective-permute-start(f32[8,64,128]{2,1,0:T(8,128)S(1)} %get-tuple-element.128.refs_0_.refs_1_), channel_id=1, source_target_pairs={{0,2},{1,3},{2,0},{3,1},{4,6},{5,7},{6,4},{7,5},{8,10},{9,11},{10,... | collective-permute-start | bytes 786440 | tf_op jit(solution)/shard_map/ppermute | solution.py:465
  82.9 24.1 %collective-permute-start.12 = (f32[8,64,128]{2,1,0:T(8,128)S(1)}, f32[8,64,128]{2,1,0:T(8,128)S(1)}, u32[]{:S(2)}, u32[]{:S(2)}) collective-permute-start(f32[8,64,128]{2,1,0:T(8,128)S(1)} %get-tuple-element.128.refs_0_.refs_1_), channel_id=1, source_target_pairs={{0,3},{1,0},{2,1},{3,2},{4,7},{5,4},{6,5},{7,6},{8,11},{9,8},{10,9... | collective-permute-start | bytes 786440 | tf_op jit(solution)/shard_map/ppermute | solution.py:465
  97.1 10.0 %collective-permute-start.7 = (f32[24,1024]{1,0:T(8,128)S(1)}, f32[24,1024]{1,0:T(8,128)S(1)}, u32[]{:S(2)}, u32[]{:S(2)}) collective-permute-start(f32[24,1024]{1,0:T(8,128)S(1)} %add.108.a_ref), channel_id=1, source_target_pairs={{0,8},{8,16},{16,24},{24,0},{1,9},{9,17},{17,25},{25,1},{2,10},{10... | collective-permute-start | bytes 294920 | tf_op jit(solution)/shard_map/ppermute | solution.py:361
  98.7 8.4 %collective-permute-start.8 = (f32[24,1024]{1,0:T(8,128)S(1)}, f32[24,1024]{1,0:T(8,128)S(1)}, u32[]{:S(2)}, u32[]{:S(2)}) collective-permute-start(f32[24,1024]{1,0:T(8,128)S(1)} %add.108.a_ref), channel_id=1, source_target_pairs={{0,16},{8,24},{16,0},{24,8},{1,17},{9,25},{17,1},{25,9},{2,18},{10... | collective-permute-start | bytes 294920 | tf_op jit(solution)/shard_map/ppermute | solution.py:361
  101.1 6.1 %collective-permute-start.9 = (f32[24,1024]{1,0:T(8,128)S(1)}, f32[24,1024]{1,0:T(8,128)S(1)}, u32[]{:S(2)}, u32[]{:S(2)}) collective-permute-start(f32[24,1024]{1,0:T(8,128)S(1)} %add.108.a_ref), channel_id=1, source_target_pairs={{0,24},{8,0},{16,8},{24,16},{1,25},{9,1},{17,9},{25,17},{2,26},{10... | collective-permute-start | bytes 294920 | tf_op jit(solution)/shard_map/ppermute | solution.py:361
  113.8 7.6 %collective-permute-start.14 = (f32[24,1024]{1,0:T(8,128)S(1)}, f32[24,1024]{1,0:T(8,128)S(1)}, u32[]{:S(2)}, u32[]{:S(2)}) collective-permute-start(f32[24,1024]{1,0:T(8,128)S(1)} %add.109.a_ref), channel_id=1, source_target_pairs={{0,8},{8,16},{16,24},{24,0},{1,9},{9,17},{17,25},{25,1},{2,10},{10... | collective-permute-start | bytes 294920 | tf_op jit(solution)/shard_map/ppermute | solution.py:361
  114.2 7.2 %collective-permute-start.15 = (f32[24,1024]{1,0:T(8,128)S(1)}, f32[24,1024]{1,0:T(8,128)S(1)}, u32[]{:S(2)}, u32[]{:S(2)}) collective-permute-start(f32[24,1024]{1,0:T(8,128)S(1)} %add.109.a_ref), channel_id=1, source_target_pairs={{0,16},{8,24},{16,0},{24,8},{1,17},{9,25},{17,1},{25,9},{2,18},{10... | collective-permute-start | bytes 294920 | tf_op jit(solution)/shard_map/ppermute | solution.py:361
  115.6 6.0 %collective-permute-start.16 = (f32[24,1024]{1,0:T(8,128)S(1)}, f32[24,1024]{1,0:T(8,128)S(1)}, u32[]{:S(2)}, u32[]{:S(2)}) collective-permute-start(f32[24,1024]{1,0:T(8,128)S(1)} %add.109.a_ref), channel_id=1, source_target_pairs={{0,24},{8,0},{16,8},{24,16},{1,25},{9,1},{17,9},{25,17},{2,26},{10... | collective-permute-start | bytes 294920 | tf_op jit(solution)/shard_map/ppermute | solution.py:361
  124.9 79.1 %all-gather.11.cloned.1.call-start = ((), (), s32[]{:S(2)}) async-start(), calls=%async_computation.6 | async-start | bytes 1179648 | tf_op jit(solution)/shard_map/all_gather | solution.py:567
  128.6 6.9 %collective-permute-start.18 = (f32[24,1024]{1,0:T(8,128)S(1)}, f32[24,1024]{1,0:T(8,128)S(1)}, u32[]{:S(2)}, u32[]{:S(2)}) collective-permute-start(f32[24,1024]{1,0:T(8,128)S(1)} %add.110.a_ref), channel_id=1, source_target_pairs={{0,8},{8,16},{16,24},{24,0},{1,9},{9,17},{17,25},{25,1},{2,10},{10... | collective-permute-start | bytes 294920 | tf_op jit(solution)/shard_map/ppermute | solution.py:361
  129.0 7.9 %collective-permute-start.19 = (f32[24,1024]{1,0:T(8,128)S(1)}, f32[24,1024]{1,0:T(8,128)S(1)}, u32[]{:S(2)}, u32[]{:S(2)}) collective-permute-start(f32[24,1024]{1,0:T(8,128)S(1)} %add.110.a_ref), channel_id=1, source_target_pairs={{0,16},{8,24},{16,0},{24,8},{1,17},{9,25},{17,1},{25,9},{2,18},{10... | collective-permute-start | bytes 294920 | tf_op jit(solution)/shard_map/ppermute | solution.py:361
  143.3 7.0 %collective-permute-start.22 = (f32[24,1024]{1,0:T(8,128)S(1)}, f32[24,1024]{1,0:T(8,128)S(1)}, u32[]{:S(2)}, u32[]{:S(2)}) collective-permute-start(f32[24,1024]{1,0:T(8,128)S(1)} %add.111.a_ref), channel_id=1, source_target_pairs={{0,8},{8,16},{16,24},{24,0},{1,9},{9,17},{17,25},{25,1},{2,10},{10... | collective-permute-start | bytes 294920 | tf_op jit(solution)/shard_map/ppermute | solution.py:361
  143.9 7.4 %collective-permute-start.23 = (f32[24,1024]{1,0:T(8,128)S(1)}, f32[24,1024]{1,0:T(8,128)S(1)}, u32[]{:S(2)}, u32[]{:S(2)}) collective-permute-start(f32[24,1024]{1,0:T(8,128)S(1)} %add.111.a_ref), channel_id=1, source_target_pairs={{0,16},{8,24},{16,0},{24,8},{1,17},{9,25},{17,1},{25,9},{2,18},{10... | collective-permute-start | bytes 294920 | tf_op jit(solution)/shard_map/ppermute | solution.py:361
  160.7 31.1 %all-to-all-start.3 = ((f32[64,16,128]{2,1,0:T(8,128)}), f32[64,16,128]{2,1,0:T(8,128)S(1)}, u32[]{:S(2)}, u32[]{:S(2)}) async-start(f32[64,16,128]{2,1,0:T(8,128)} %filter.1), calls=%async_computation.3 | async-start | bytes 1048576 | tf_op jit(solution)/shard_map/all_to_all | solution.py:568
  (43 other events, 227.9 us)
Sparse Core Ops, SparseCore 0:
  11.4 63.9 all-gather.6
  125.0 34.2 all-gather.8
  161.1 42.8 all-gather.10

commit v3 on v2

--- a/solution.py
+++ b/solution.py
@@ -109,12 +109,12 @@
     out_ref[...] = slots.reshape(16, 16, 128)
 
 
-def lower_kernel(one_ref, two_ref, three_ref, out_ref):
-    place = 0
-    for k, ref in enumerate((one_ref, two_ref, three_ref)):
-        for j in range(k + 1):
-            out_ref[16 * place : 16 * place + 16] = ref[0, :, LENGTH * j : LENGTH * (j + 1)]
-            place += 1
+def lower_kernel(one_ref, two_ref, three_ref, near_ref, far_ref):
+    near_ref[0:16] = one_ref[0]
+    for j in range(2):
+        near_ref[16 * j + 16 : 16 * j + 32] = two_ref[0, :, LENGTH * j : LENGTH * (j + 1)]
+    for j in range(3):
+        far_ref[16 * j : 16 * j + 16] = three_ref[0, :, LENGTH * j : LENGTH * (j + 1)]
 
 
 def bundle_kernel(index_ref, columns_ref, *refs):
@@ -126,14 +126,23 @@
         weights = jnp.where(lane == y + 16, ref[:, 0:1], weights)
     side = side_refs[0][...]
     quarter = columns_ref[pl.ds(2 * index_ref[1], 2)]
-    quarter = [quarter[:, 32 * h : 32 * h + 32].reshape(64, 128) for h in range(2)]
+    second = quarter[:, 16:32].reshape(32, 128)
+    others = quarter[:, 32:64].reshape(64, 128)
+    whole = columns_ref[:, 0:16, :].reshape(128, 128)
     for z in range(8):
         own = pltpu.roll(side, (128 - 16 * z) % 128, 1) if z else side
         rows = jnp.where(lane < 16, own, weights)
-        out_ref[z, 0:64] = quarter[0]
-        out_ref[z, 64:128] = quarter[1]
-        out_ref[z, 128:160] = jnp.transpose(jnp.concatenate([rows, rows]))[:32]
-        out_ref[z, 160:176] = extra_ref[...]
+        out_ref[z, 0:128] = whole
+        out_ref[z, 128:160] = second
+        out_ref[z, 160:224] = others
+        out_ref[z, 224:256] = jnp.transpose(jnp.concatenate([rows, rows]))[:32]
+        out_ref[z, 256:272] = extra_ref[...]
+
+
+def product(work, rows_high, rows_low):
+    high, low = split(work)
+    wide = dot(jnp.concatenate([high, low]), rows_high, NT)
+    return wide[:COLS] + wide[COLS:] + dot(high, rows_low, NT)
 
 
 def spread(work, index_ref, inverse_refs, out_ref, high_ref, low_ref):
@@ -143,15 +152,11 @@
         rows_high, rows_low = split(ref[...])
         high_ref[:, pl.ds(start, 16), :] = rows_high
         low_ref[:, pl.ds(start, 16), :] = rows_low
-    high, low = split(work)
     rows_high = high_ref[...].reshape(LENGTH, 128)
-    wide = dot(jnp.concatenate([high, low]), rows_high, NT)
-    rows_low = low_ref[...].reshape(LENGTH, 128)
-    out_ref[...] = wide[:COLS] + wide[COLS:] + dot(high, rows_low, NT)
-
-
-def first_kernel(index_ref, slab_ref, *refs):
-    inverse_refs, (out_ref, side_ref, high_ref, low_ref) = refs[:8], refs[8:]
+    out_ref[...] = product(work, rows_high, low_ref[...].reshape(LENGTH, 128))
+
+
+def first_kernel(slab_ref, inverse_ref, out_ref, side_ref):
     lane = lax.broadcasted_iota(jnp.int32, (COLS, 128), 1) // 16
     for k in range(4):
         rows = jnp.zeros((COLS, 128), F32)
@@ -161,13 +166,16 @@
             piece = pltpu.roll(piece, turn, 1) if turn else piece
             rows = jnp.where(lane == z, piece, rows)
         side_ref[k] = rows
-    spread(side_ref[0], index_ref, inverse_refs, out_ref, high_ref, low_ref)
+    out_ref[...] = product(side_ref[0], *split(inverse_ref[...].reshape(LENGTH, 128)))
 
 
 def step_kernel(panel, index_ref, start_ref, a_ref, b_ref, c_ref, d_ref, factor_ref, *refs):
     inverse_refs, refs = refs[:8], refs[8:]
     unknown = (a_ref[...] + b_ref[...]) + (c_ref[...] + d_ref[...])
-    if panel == 2:
+    if panel == 1:
+        refs[2][0:16] = unknown[0:16]
+        refs[2][16:32] = jnp.zeros((16, LENGTH), F32)
+    if panel == 3:
         older_ref, refs = refs[0], refs[1:]
         refs[2][0:16] = older_ref[0:16]
         refs[2][16:32] = unknown[0:16]
@@ -293,8 +301,9 @@
 
 
 def update_kernel(
-    first_panel, panels, index_ref, base_ref, factor_ref, unknown_ref, out_ref, high_ref, low_ref
+    first_panel, panels, index_ref, base_ref, unknown_ref, *refs
 ):
+    factor_refs, (out_ref, high_ref, low_ref) = refs[:panels], refs[panels:]
     block = pl.program_id(0)
 
     @pl.when(block == 0)
@@ -313,7 +322,7 @@
         base = jnp.where(base_row < 64, 0.0, base)
     for step in range(panels):
         panel = first_panel + step
-        rows = factor_ref[:, :, LENGTH * step : LENGTH * (step + 1)].reshape(128, LENGTH)
+        rows = factor_refs[step][...].reshape(128, LENGTH)
         mine = (row // 16 == panel) & (col == own + row % 16)
         rows = jnp.where(row < 64, jnp.where(mine, -1.0, 0.0), rows)
         rows_high, rows_low = split(rows)
@@ -376,16 +385,19 @@
         [
             SMEM,
             pl.BlockSpec((8, 16, 128), lambda i: (i, 0, 0)),
-            pl.BlockSpec((8, 16, panels * LENGTH), lambda i: (i, 0, first_panel // panels)),
+            spec(8, 16 * panels, LENGTH),
         ]
-        + [spec(8, 16 * panels, LENGTH)],
+        + [
+            pl.BlockSpec((8, 16, LENGTH), lambda i, place=first_panel + k: (i, 0, place))
+            for k in range(panels)
+        ],
         pl.BlockSpec((8, 16, 128), lambda i: (i, 0, 0)),
         shape_of(32, 16, 128),
         3 * 2 * 512 * panels * LENGTH * 128,
         2_700_000 * panels,
         [pltpu.VMEM((panels, 128, LENGTH), BF16)] * 2,
         grid=4,
-    )(index, base, factor, unknowns)
+    )(index, base, unknowns, *[factor] * panels)
 
 
 SMEM = pl.BlockSpec(memory_space=pltpu.SMEM)
@@ -415,12 +427,12 @@
     columns = lax.all_to_all(columns, ("x", "core"), 0, 0)
     extra = spectrum[:, :, 0].T.reshape(16, 128)
 
-    lower = call(
+    lower, lower_far = call(
         lower_kernel,
         "lower",
         [block_at((1, 16, LENGTH * k), (k, 0, 0)) for k in range(1, 4)],
-        spec(96, LENGTH),
-        shape_of(96, LENGTH),
+        [spec(48, LENGTH)] * 2,
+        [shape_of(48, LENGTH)] * 2,
         0,
         800_000,
     )(factor, factor, factor)
@@ -431,14 +443,15 @@
         bundle_kernel,
         "bundle",
         [SMEM, spec(8, 64, 128)] + [spec(64, 128)] * 4 + [spec(16, 128)],
-        spec(8, 176, 128),
-        shape_of(8, 176, 128),
+        spec(8, 272, 128),
+        shape_of(8, 272, 128),
         0,
         1_500_000,
     )(index, columns, *sides, extra)
-    box = [quarter, noise, spectrum, obs_cells]
-    tie((box, (0, 1, 2, 3)))
-    quarter, noise, spectrum, obs_cells = box
+    box = [quarter, noise, spectrum, obs_cells, lower_far]
+    tie((box, (0, 1, 2, 3, 4)))
+    quarter, noise, spectrum, obs_cells, lower_far = box
+    lower_far = lax.all_gather(lower_far, "z")
     quarter = lax.all_to_all(quarter, "z", 0, 0)
 
     slab = call(
@@ -461,8 +474,8 @@
     box = [quarter, slab, spectrum, cell_x, planes, waves]
     tie((box, tuple(range(6))))
     quarter, slab, spectrum, cell_x, planes, waves = box
-    own = [quarter[:, 0:64], quarter[:, 64:128]]
-    own = [[one] + [lax.ppermute(one, "y", ring(4, step)) for step in (1, 2, 3)] for one in own]
+    own = quarter[:, 128:224]
+    own = [own] + [lax.ppermute(own, "y", ring(4, step)) for step in (1, 2, 3)]
     slab = lax.all_to_all(slab, WIDE, 0, 0)
 
     obs_specs = lambda k: [
@@ -471,9 +484,12 @@
         block_at((2, LENGTH), (0, k)),
     ]
     side_spec = lambda k: block_at((1, COLS, 128), (k, 0, 0))
-    factor_spec = lambda k, j: block_at((8, 16, LENGTH), (0, k * (k - 1) // 2 + j, 0))
-    inverse_specs = lambda k: [block_at((8, 16, 128), (0, k % 2 + a, 0)) for a in (0, 2)] * 4
-    inverses = lambda k: [one for one in own[k // 2] for _ in range(2)]
+    factor_spec = lambda k, j: block_at((8, 16, LENGTH), (0, j + (k == 2), 0))
+    factor_rows = lambda k: lower_far if k == 3 else lower
+    inverse_specs = lambda k: [
+        block_at((8, 16, 128), (0, a if k == 1 else k + 2 * a, 0)) for a in range(2)
+    ] * 4
+    inverses = [one for one in range(4) for _ in range(2)]
     inverse_scratch = [pltpu.VMEM((8, 128, 128), BF16)] * 2
     panel_spec = spec(COLS, LENGTH)
     panel_shape = shape_of(COLS, LENGTH)
@@ -482,13 +498,12 @@
     partial, sides = call(
         first_kernel,
         "first",
-        [SMEM, block_at((8, 32, 128), (0, 4, 0))] + inverse_specs(0),
+        [block_at((8, 32, 128), (0, 7, 0)), block_at((8, 128, 128), (0, 0, 0))],
         [panel_spec, spec(4, COLS, 128)],
         [panel_shape, shape_of(4, COLS, 128)],
         20_000_000,
         1_200_000,
-        inverse_scratch,
-    )(index, quarter, *inverses(0))
+    )(quarter, quarter)
     box = [partial, spectrum]
     tie((box, (0, 1)))
     partial, spectrum = box
@@ -496,14 +511,14 @@
     even, odd = call(
         spectrum_kernel,
         "spectrum",
-        [SMEM, spec(LENGTH, 32), block_at((1, 16, 128), (4, 10, 0))],
+        [SMEM, spec(LENGTH, 32), block_at((1, 16, 128), (4, 16, 0))],
         [spec(LENGTH, 128), spec(512, 128)],
         [shape_of(LENGTH, 128), shape_of(512, 128)],
         300_000_000,
         1_500_000,
     )(index, spectrum.reshape(LENGTH, 32), quarter)
     box = [even, odd]
-    tie((parts, (0, 1, 2, 3)), (own[1], (1, 2, 3)), (box, (0, 1)))
+    tie((parts, (0, 1, 2, 3)), (own, (0, 1, 2, 3)), (box, (0, 1)))
     even, odd = box
     unknowns = []
     work = sides
@@ -516,16 +531,16 @@
             + [panel_spec] * 4
             + [factor_spec(panel, panel - 1)]
             + inverse_specs(panel)
-            + [panel_spec] * (panel == 2),
-            [panel_spec] * 2 + [spec(32, LENGTH)] * (panel == 2),
-            [panel_shape] * 2 + [shape_of(32, LENGTH)] * (panel == 2),
+            + [panel_spec] * (panel == 3),
+            [panel_spec] * 2 + [spec(32, LENGTH)] * (panel != 2),
+            [panel_shape] * 2 + [shape_of(32, LENGTH)] * (panel != 2),
             40_000_000,
             1_500_000,
             inverse_scratch,
-        )(index, work, *parts, lower, *inverses(panel), *unknowns[:1] * (panel == 2))
+        )(index, work, *parts, factor_rows(panel), *[own[at] for at in inverses], *unknowns[1:2] * (panel == 3))
         unknowns.append(unknown)
         parts = share(partial)
-        if panel == 2:
+        if panel == 1:
             early = lax.all_gather(pair[0], "z")
         later = panel < 3
         box = list(
@@ -543,7 +558,7 @@
                 1_500_000,
             )(
                 cell_x, waves, planes, pencil, *unknowns, *[sides] * later,
-                *[lower] * (panel * later),
+                *[factor_rows(panel + 1)] * (panel * later),
             )
         )
         tie((parts, (0, 1, 2, 3)), (box, (0, 1) if later else (0,)))
@@ -564,9 +579,9 @@
         [TABLE] * 4 + [pltpu.SemaphoreType.DMA((4,))],
     )(pencil, cell_x, waves, planes, *parts, x_high, x_low, back_high, back_low, even, odd)
     late = (parts[0][:16] + parts[1][:16]) + (parts[2][:16] + parts[3][:16])
-    late = lax.all_gather(jnp.concatenate([unknowns[2][:16], late]), "z")
+    late = lax.all_gather(jnp.concatenate([pair[0], late]), "z")
     slots = lax.all_to_all(slots, WIDE, 0, 0)
-    solved = update(0, 2, index, right_side, factor, early)
+    solved = update(0, 1, index, right_side, factor, early)
     slots, solved = lax.optimization_barrier((slots, solved))
     correction = call(
         close_kernel,
@@ -580,7 +595,7 @@
         grid=4,
     )(slots, z_high, z_low)
     solved, correction = lax.optimization_barrier((solved, correction))
-    solved = update(2, 2, index, solved, factor, late)
+    solved = update(1, 3, index, solved, factor, late)
     return (solved, correction)
 
 

time: 219 us -> 219 us (level)
  waiting for transfers between devices: 60.3 us -> 63.8 us
  starting transfers between devices: 64.8 us -> 62.2 us
    all_to_all x1, waiting for transfers between devices: 0.01 us -> 10.2 us  [per_device(): slab = lax.all_to_all(slab, WIDE, 0, 0)]
    ppermute x6 -> x3, waiting for transfers between devices: 9.15 us -> 0.01 us  [per_device(): own = [own] + [lax.ppermute(own, 'y', ring(4, step)) for step in (1, 2, 3)]]
    all_gather x1 -> x2, waiting for transfers between devices: 6.35 us -> 0.43 us  [the longest x1 0.43 us: per_device(): late = lax.all_gather(jnp.concatenate([pair[0], late]), 'z')]
    all_to_all x1, waiting for transfers between devices: 21.3 us -> 26.6 us  [per_device(): quarter = lax.all_to_all(quarter, 'z', 0, 0)]
    ppermute x12, starting transfers between devices: 15.1 us -> 17.7 us  [share(): lax.ppermute(total, 'x', ring(4, step))]
    all_to_all x1, waiting for transfers between devices: 14.8 us -> 17.4 us  [per_device(): slots = lax.all_to_all(slots, WIDE, 0, 0)]
    all_to_all x1, starting transfers between devices: 10.5 us -> 7.94 us  [per_device(): slots = lax.all_to_all(slots, WIDE, 0, 0)]
    ppermute x6 -> x3, starting transfers between devices: 6.12 us -> 4.95 us  [per_device(): own = [own] + [lax.ppermute(own, 'y', ring(4, step)) for step in (1, 2, 3)]]
  transfers between devices with their start and end apart: 32 -> 30, of which waited for: 17 -> 12; matrix products, arithmetic and copies ran while one was open for 5% -> 5% of each run, Pallas kernels for 22% -> 22%
where the time goes in v3:
time: 219 us; the launch traced here: 216 us
  waiting for transfers between devices  63.8 us (29%)
  starting transfers between devices  62.2 us (28%)
  Pallas kernels  59.7 us (27%)
  between operations  14.2 us (6%)
  other arithmetic  7.98 us (4%)
  local copies, waits for them, and re-layouts  7.96 us (4%)
    all_to_all x1, waiting for transfers between devices, per_device(): quarter = lax.all_to_all(quarter, 'z', 0, 0)  26.6 us
    ppermute x12, starting transfers between devices, share(): lax.ppermute(total, 'x', ring(4, step))  17.7 us
    all_to_all x1, waiting for transfers between devices, per_device(): slots = lax.all_to_all(slots, WIDE, 0, 0)  17.4 us
    pallas_call x2, Pallas kernels, update(): call(functools.partial(update_kernel, first_panel, panels), 'update', [SM...  11.8 us
    all_to_all x1, waiting for transfers between devices, per_device(): slab = lax.all_to_all(slab, WIDE, 0, 0)  10.2 us
    pallas_call x3, Pallas kernels, per_device(): call(functools.partial(wait_kernel, panel), f'wait{panel}', obs_specs(pan...  9.53 us
    pallas_call x1, Pallas kernels, per_device(): call(filter_kernel, 'filter', [spec(LENGTH, 128)] + obs_specs(3) + [panel...  8.43 us
    all_to_all x1, starting transfers between devices, per_device(): quarter = lax.all_to_all(quarter, 'z', 0, 0)  8.2 us
  transfers between devices with their start and end apart: 30, of which 12 were waited for; matrix products, arithmetic and copies ran while one was open for 5% of the time, Pallas kernels for 22%

profile of v3, /device:TPU:1, one launch (start us, length us, event | category | flops | bytes accessed | tf_op | source)
XLA Modules:
  0.0 215.8 jit_solution(9839627981231469558)
XLA Ops:
  11.3 6.6 %all-to-all-start = ((f32[8,64,128]{2,1,0:T(8,128)}), f32[8,64,128]{2,1,0:T(8,128)S(1)}, u32[]{:S(2)}, u32[]{:S(2)}) async-start(f32[8,64,128]{2,1,0:T(8,128)} %get-tuple-element.71), calls=%async_computation | async-start | bytes 524288 | tf_op jit(solution)/shard_map/all_to_all | solution.py:427
  18.5 2.6 %collective-permute-start.1 = (f32[64,128]{1,0:T(8,128)S(1)}, f32[64,128]{1,0:T(8,128)S(1)}, u32[]{:S(2)}, u32[]{:S(2)}) collective-permute-start(f32[64,128]{1,0:T(8,128)S(1)} %copy-done.28), channel_id=1, source_target_pairs={{0,2},{1,3},{2,0},{3,1},{4,6},{5,7},{6,4},{7,5},{8,10},{9,11},{10,... | collective-permute-start | bytes 98312 | tf_op jit(solution)/shard_map/ppermute | solution.py:441
  27.8 8.2 %all-to-all-start.1 = ((f32[8,272,128]{2,1,0:T(8,128)}), f32[8,272,128]{2,1,0:T(8,128)S(1)}, u32[]{:S(2)}, u32[]{:S(2)}) async-start(f32[8,272,128]{2,1,0:T(8,128)} %bundle.1), calls=%async_computation.1 | async-start | bytes 2228224 | tf_op jit(solution)/shard_map/all_to_all | solution.py:455
  37.3 4.9 %noise.1 = f32[64,16,128]{2,1,0:T(8,128)} custom-call(f32[128,1024]{1,0:T(8,128)} %reshape.57.noise_ref, bf16[1024,1024]{1,0:T(8,128)(2,1)} %constant.129.clone.high_ref, bf16[1024,1024]{1,0:T(8,128)(2,1)} %constant.130.clone.low_ref), custom_call_target="tpu_custom_call" | custom-call | flops 805306368 | bytes 5000000 | tf_op jit(solution)/shard_map/noise/pallas_call | solution.py:457
  45.2 26.6 %all-to-all-done.1.slab_ref.inverse_ref.extra_ref = f32[8,272,128]{2,1,0:T(8,128)S(1)} async-done(((f32[8,272,128]{2,1,0:T(8,128)}), f32[8,272,128]{2,1,0:T(8,128)S(1)}, u32[]{:S(2)}, u32[]{:S(2)}) %all-to-all-start.1) | async-done | bytes 1114144 | tf_op jit(solution)/shard_map/all_to_all | solution.py:455
  72.8 2.5 %collective-permute-start.8 = (f32[8,96,128]{2,1,0:T(8,128)S(1)}, f32[8,96,128]{2,1,0:T(8,128)S(1)}, u32[]{:S(2)}, u32[]{:S(2)}) collective-permute-start(f32[8,96,128]{2,1,0:T(8,128)S(1)} %slice.19.refs_0_.refs_1_), channel_id=1, source_target_pairs={{0,2},{1,3},{2,0},{3,1},{4,6},{5,7},{6,4},{7,5},{8,10},{9,11},{10,... | collective-permute-start | bytes 1179656 | tf_op jit(solution)/shard_map/ppermute | solution.py:478
  78.9 2.9 %collective-permute-start.3 = (f32[24,1024]{1,0:T(8,128)}, f32[24,1024]{1,0:T(8,128)S(1)}, u32[]{:S(2)}, u32[]{:S(2)}) collective-permute-start(f32[24,1024]{1,0:T(8,128)} %get-tuple-element.83), channel_id=1, source_target_pairs={{0,4},{4,0},{1,5},{5,1},{2,6},{6,2},{3,7},{7,3},{8,12},{12,8},{9,1... | collective-permute-start | bytes 294920 | tf_op jit(solution)/shard_map/ppermute | solution.py:369
  86.6 2.7 %collective-permute-done.4.b_ref = f32[24,1024]{1,0:T(8,128)S(1)} collective-permute-done((f32[24,1024]{1,0:T(8,128)S(1)}, f32[24,1024]{1,0:T(8,128)S(1)}, u32[]{:S(2)}, u32[]{:S(2)}) %collective-permute-start.4) | collective-permute-done | bytes 98336 | tf_op jit(solution)/shard_map/ppermute | solution.py:370
  90.6 3.8 %spectrum.1 = (f32[1024,128]{1,0:T(8,128)}, f32[512,128]{1,0:T(8,128)}) custom-call(s32[2]{0:T(128)} %pad_add_fusion.index_ref, f32[1024,32]{1,0:T(8,128)} %copy.15.spectrum_ref, f32[8,272,128]{2,1,0:T(8,128)} %copy-done), custom_call_target="tpu_custom_call" | custom-call | flops 300000000 | bytes 1500000 | tf_op jit(solution)/shard_map/spectrum/pallas_call | solution.py:511
  95.5 2.6 %step1.1 = (f32[24,1024]{1,0:T(8,128)}, f32[24,1024]{1,0:T(8,128)}, f32[32,1024]{1,0:T(8,128)}) custom-call(s32[2]{0:T(128)} %pad_add_fusion.index_ref, f32[4,24,128]{2,1,0:T(8,128)} %get-tuple-element.80.start_ref.refs_5_.refs_6_, f32[24,1024]{1,0:T(8,128)} %copy-done.10, f32[24,1024]{1,0:T(8,128)} %copy-done.18, f32[24,1024]{1,0:T(8,128)} %copy-done.19, ...), custom_call_target="tpu_custom_call" | custom-call | flops 40000000 | bytes 1500000 | tf_op jit(solution)/shard_map/step1/pallas_call | solution.py:527
  98.1 7.1 %all-to-all-start.2 = ((f32[64,16,128]{2,1,0:T(8,128)}), f32[64,16,128]{2,1,0:T(8,128)S(1)}, u32[]{:S(2)}, u32[]{:S(2)}) async-start(f32[64,16,128]{2,1,0:T(8,128)} %noise.1), calls=%async_computation.2 | async-start | bytes 1048576 | tf_op jit(solution)/shard_map/all_to_all | solution.py:479
  112.8 10.2 %all-to-all-done.2.refs_3_ = f32[64,16,128]{2,1,0:T(8,128)S(1)} async-done(((f32[64,16,128]{2,1,0:T(8,128)}), f32[64,16,128]{2,1,0:T(8,128)S(1)}, u32[]{:S(2)}, u32[]{:S(2)}) %all-to-all-start.2) | async-done | bytes 524320 | tf_op jit(solution)/shard_map/all_to_all | solution.py:479
  123.7 3.5 %wait1.1 = (f32[1024,128]{1,0:T(8,128)}, f32[1,24,128]{2,1,0:T(8,128)}) custom-call(s32[1,4096]{1,0:T(1,128)} %bitcast.22, f32[16,4096]{1,0:T(8,128)} %fusion.3.refs_1_.wave_ref, f32[2,4096]{1,0:T(2,128)} %add_convert_fusion.refs_2_.plane_ref, f32[64,16,128]{2,1,0:T(8,128)} %copy-done.5, f32[24,1024]{1,0:T(8,128)} %get-tuple-element.101.refs_4_, ...), custom_call_target="tpu_custom_call" | custom-call | flops 536870912 | bytes 1500000 | tf_op jit(solution)/shard_map/wait1/pallas_call | solution.py:547
  127.9 2.5 %step2.1 = (f32[24,1024]{1,0:T(8,128)}, f32[24,1024]{1,0:T(8,128)}) custom-call(s32[2]{0:T(128)} %pad_add_fusion.index_ref, f32[1,24,128]{2,1,0:T(8,128)} %get-tuple-element.104.start_ref, f32[24,1024]{1,0:T(8,128)} %copy-done.12, f32[24,1024]{1,0:T(8,128)} %copy-done.23, f32[24,1024]{1,0:T(8,128)} %copy-done.25, f32[24,1024]{1,0:T(8,128)} %copy-done.26, ...), custom_call_target="tpu_custom_call" | custom-call | flops 40000000 | bytes 1500000 | tf_op jit(solution)/shard_map/step2/pallas_call | solution.py:527
  138.1 3.3 %wait2.1 = (f32[1024,128]{1,0:T(8,128)}, f32[1,24,128]{2,1,0:T(8,128)}) custom-call(s32[1,4096]{1,0:T(1,128)} %bitcast.23, f32[16,4096]{1,0:T(8,128)} %fusion.3.refs_1_.wave_ref, f32[2,4096]{1,0:T(2,128)} %add_convert_fusion.refs_2_.plane_ref, f32[1024,128]{1,0:T(8,128)} %get-tuple-element.110.refs_3_, f32[24,1024]{1,0:T(8,128)} %get-tuple-element.101.refs_4_, ...), custom_call_target="tpu_custom_call" | custom-call | flops 536870912 | bytes 1500000 | tf_op jit(solution)/shard_map/wait2/pallas_call | solution.py:547
  142.1 2.6 %step3.1 = (f32[24,1024]{1,0:T(8,128)}, f32[24,1024]{1,0:T(8,128)}, f32[32,1024]{1,0:T(8,128)}) custom-call(s32[2]{0:T(128)} %pad_add_fusion.index_ref, f32[1,24,128]{2,1,0:T(8,128)} %get-tuple-element.115.start_ref, f32[24,1024]{1,0:T(8,128)} %copy-done.11, f32[24,1024]{1,0:T(8,128)} %copy-done.20, f32[24,1024]{1,0:T(8,128)} %copy-done.21, ...), custom_call_target="tpu_custom_call" | custom-call | flops 40000000 | bytes 1500000 | tf_op jit(solution)/shard_map/step3/pallas_call | solution.py:527
  149.5 2.4 %collective-permute-start.20 = (f32[24,1024]{1,0:T(8,128)S(1)}, f32[24,1024]{1,0:T(8,128)S(1)}, u32[]{:S(2)}, u32[]{:S(2)}) collective-permute-start(f32[24,1024]{1,0:T(8,128)S(1)} %add.111.a_ref), channel_id=1, source_target_pairs={{0,16},{8,24},{16,0},{24,8},{1,17},{9,25},{17,1},{25,9},{2,18},{10... | collective-permute-start | bytes 294920 | tf_op jit(solution)/shard_map/ppermute | solution.py:370
  152.9 2.7 %wait3.1.pencil_ref = f32[1024,128]{1,0:T(8,128)} custom-call(s32[1,4096]{1,0:T(1,128)} %bitcast.24, f32[16,4096]{1,0:T(8,128)} %fusion.3.refs_1_.wave_ref, f32[2,4096]{1,0:T(2,128)} %add_convert_fusion.refs_2_.plane_ref, f32[1024,128]{1,0:T(8,128)} %get-tuple-element.121.refs_3_, f32[24,1024]{1,0:T(8,128)} %get-tuple-element.101.refs_4_, ...), custom_call_target="tpu_custom_call" | custom-call | flops 536870912 | bytes 1500000 | tf_op jit(solution)/shard_map/wait3/pallas_call | solution.py:547
  157.4 8.4 %filter.1 = f32[64,16,128]{2,1,0:T(8,128)} custom-call(f32[1024,128]{1,0:T(8,128)} %wait3.1.pencil_ref, s32[1,4096]{1,0:T(1,128)} %bitcast.25, f32[16,4096]{1,0:T(8,128)} %fusion.3.refs_1_.wave_ref, f32[2,4096]{1,0:T(2,128)} %add_convert_fusion.refs_2_.plane_ref, f32[24,1024]{1,0:T(8,128)} %copy-done.8, f32[24,1024]{1,0:T(8,128)} %copy-done.13, ...), custom_call_target="tpu_custom_call" | custom-call | flops 2147483648 | bytes 11000000 | tf_op jit(solution)/shard_map/filter/pallas_call | solution.py:567
  165.8 7.9 %all-to-all-start.3 = ((f32[64,16,128]{2,1,0:T(8,128)}), f32[64,16,128]{2,1,0:T(8,128)S(1)}, u32[]{:S(2)}, u32[]{:S(2)}) async-start(f32[64,16,128]{2,1,0:T(8,128)} %filter.1), calls=%async_computation.3 | async-start | bytes 1048576 | tf_op jit(solution)/shard_map/all_to_all | solution.py:583
  173.8 4.6 %update.2.base_ref = f32[32,16,128]{2,1,0:T(8,128)} custom-call(s32[2]{0:T(128)} %pad_add_fusion.index_ref, f32[32,16,128]{2,1,0:T(8,128)} %base_ref.1, f32[8,32,1024]{2,1,0:T(8,128)} %bitcast.21, f32[32,16,4096]{2,1,0:T(8,128)} %refs_2_), custom_call_target="tpu_custom_call" | custom-call | flops 402653184 | bytes 2700000 | tf_op jit(solution)/shard_map/update/pallas_call | solution.py:382
  178.4 17.4 %all-to-all-done.3.slots_ref = f32[64,16,128]{2,1,0:T(8,128)S(1)} async-done(((f32[64,16,128]{2,1,0:T(8,128)}), f32[64,16,128]{2,1,0:T(8,128)S(1)}, u32[]{:S(2)}, u32[]{:S(2)}) %all-to-all-start.3) | async-done | bytes 524320 | tf_op jit(solution)/shard_map/all_to_all | solution.py:583
  196.6 5.1 %close.1 = f32[16,4,2,1024]{3,2,1,0:T(2,128)} custom-call(f32[64,16,128]{2,1,0:T(8,128)} %copy-done.6, bf16[1024,1024]{1,0:T(8,128)(2,1)} %constant.129.clone.high_ref, bf16[1024,1024]{1,0:T(8,128)(2,1)} %constant.130.clone.low_ref), custom_call_target="tpu_custom_call" | custom-call | flops 805306368 | bytes 5500000 | tf_op jit(solution)/shard_map/close/pallas_call | solution.py:586
  202.1 7.2 %update.3 = f32[32,16,128]{2,1,0:T(8,128)} custom-call(s32[2]{0:T(128)} %pad_add_fusion.index_ref, f32[32,16,128]{2,1,0:T(8,128)} %update.2.base_ref, f32[8,48,1024]{2,1,0:T(8,128)} %bitcast.20, f32[32,16,4096]{2,1,0:T(8,128)} %refs_2_, f32[32,16,4096]{2,1,0:T(8,128)} %refs_2_, f32[32,16,4096]{2,1,0:T(8,128)} %refs_2_), custom_call_target="tpu_custom_call" | custom-call | flops 1207959552 | bytes 8100000 | tf_op jit(solution)/shard_map/update/pallas_call | solution.py:382
  (141 shorter events, 53.4 us)
Async XLA Ops:
  7.2 87.3 %all-gather.9.cloned.1.call-start = ((), (), s32[]{:S(2)}) async-start(), calls=%async_computation.4 | async-start | bytes 1769472 | tf_op jit(solution)/shard_map/all_gather | solution.py:439
  11.3 13.1 %all-to-all-start = ((f32[8,64,128]{2,1,0:T(8,128)}), f32[8,64,128]{2,1,0:T(8,128)S(1)}, u32[]{:S(2)}, u32[]{:S(2)}) async-start(f32[8,64,128]{2,1,0:T(8,128)} %get-tuple-element.71), calls=%async_computation | async-start | bytes 524288 | tf_op jit(solution)/shard_map/all_to_all | solution.py:427
  17.8 120.2 %all-gather.11.cloned.1.call-start = ((), (), s32[]{:S(2)}) async-start(), calls=%async_computation.5 | async-start | bytes 1769472 | tf_op jit(solution)/shard_map/all_gather | solution.py:454
  17.9 5.5 %collective-permute-start = (f32[64,128]{1,0:T(8,128)S(1)}, f32[64,128]{1,0:T(8,128)S(1)}, u32[]{:S(2)}, u32[]{:S(2)}) collective-permute-start(f32[64,128]{1,0:T(8,128)S(1)} %copy-done.28), channel_id=1, source_target_pairs={{0,1},{1,2},{2,3},{3,0},{4,5},{5,6},{6,7},{7,4},{8,9},{9,10},{10,1... | collective-permute-start | bytes 98312 | tf_op jit(solution)/shard_map/ppermute | solution.py:441
  18.5 4.9 %collective-permute-start.1 = (f32[64,128]{1,0:T(8,128)S(1)}, f32[64,128]{1,0:T(8,128)S(1)}, u32[]{:S(2)}, u32[]{:S(2)}) collective-permute-start(f32[64,128]{1,0:T(8,128)S(1)} %copy-done.28), channel_id=1, source_target_pairs={{0,2},{1,3},{2,0},{3,1},{4,6},{5,7},{6,4},{7,5},{8,10},{9,11},{10,... | collective-permute-start | bytes 98312 | tf_op jit(solution)/shard_map/ppermute | solution.py:441
  27.8 44.0 %all-to-all-start.1 = ((f32[8,272,128]{2,1,0:T(8,128)}), f32[8,272,128]{2,1,0:T(8,128)S(1)}, u32[]{:S(2)}, u32[]{:S(2)}) async-start(f32[8,272,128]{2,1,0:T(8,128)} %bundle.1), calls=%async_computation.1 | async-start | bytes 2228224 | tf_op jit(solution)/shard_map/all_to_all | solution.py:455
  36.0 137.8 %all-gather.13.cloned.1.call-start = ((), (), s32[]{:S(2)}) async-start(), calls=%async_computation.6 | async-start | bytes 1179648 | tf_op jit(solution)/shard_map/all_gather | solution.py:544
  71.8 22.6 %collective-permute-start.7 = (f32[8,96,128]{2,1,0:T(8,128)S(1)}, f32[8,96,128]{2,1,0:T(8,128)S(1)}, u32[]{:S(2)}, u32[]{:S(2)}) collective-permute-start(f32[8,96,128]{2,1,0:T(8,128)S(1)} %slice.19.refs_0_.refs_1_), channel_id=1, source_target_pairs={{0,1},{1,2},{2,3},{3,0},{4,5},{5,6},{6,7},{7,4},{8,9},{9,10},{10,1... | collective-permute-start | bytes 1179656 | tf_op jit(solution)/shard_map/ppermute | solution.py:478
  72.8 21.6 %collective-permute-start.8 = (f32[8,96,128]{2,1,0:T(8,128)S(1)}, f32[8,96,128]{2,1,0:T(8,128)S(1)}, u32[]{:S(2)}, u32[]{:S(2)}) collective-permute-start(f32[8,96,128]{2,1,0:T(8,128)S(1)} %slice.19.refs_0_.refs_1_), channel_id=1, source_target_pairs={{0,2},{1,3},{2,0},{3,1},{4,6},{5,7},{6,4},{7,5},{8,10},{9,11},{10,... | collective-permute-start | bytes 1179656 | tf_op jit(solution)/shard_map/ppermute | solution.py:478
  75.3 19.1 %collective-permute-start.9 = (f32[8,96,128]{2,1,0:T(8,128)S(1)}, f32[8,96,128]{2,1,0:T(8,128)S(1)}, u32[]{:S(2)}, u32[]{:S(2)}) collective-permute-start(f32[8,96,128]{2,1,0:T(8,128)S(1)} %slice.19.refs_0_.refs_1_), channel_id=1, source_target_pairs={{0,3},{1,0},{2,1},{3,2},{4,7},{5,4},{6,5},{7,6},{8,11},{9,8},{10,9... | collective-permute-start | bytes 1179656 | tf_op jit(solution)/shard_map/ppermute | solution.py:478
  83.9 5.4 %collective-permute-start.4 = (f32[24,1024]{1,0:T(8,128)S(1)}, f32[24,1024]{1,0:T(8,128)S(1)}, u32[]{:S(2)}, u32[]{:S(2)}) collective-permute-start(f32[24,1024]{1,0:T(8,128)S(1)} %add.108.a_ref), channel_id=1, source_target_pairs={{0,8},{8,16},{16,24},{24,0},{1,9},{9,17},{17,25},{25,1},{2,10},{10... | collective-permute-start | bytes 294920 | tf_op jit(solution)/shard_map/ppermute | solution.py:370
  85.1 9.3 %collective-permute-start.5 = (f32[24,1024]{1,0:T(8,128)S(1)}, f32[24,1024]{1,0:T(8,128)S(1)}, u32[]{:S(2)}, u32[]{:S(2)}) collective-permute-start(f32[24,1024]{1,0:T(8,128)S(1)} %add.108.a_ref), channel_id=1, source_target_pairs={{0,16},{8,24},{16,0},{24,8},{1,17},{9,25},{17,1},{25,9},{2,18},{10... | collective-permute-start | bytes 294920 | tf_op jit(solution)/shard_map/ppermute | solution.py:370
  89.3 5.1 %collective-permute-start.6 = (f32[24,1024]{1,0:T(8,128)S(1)}, f32[24,1024]{1,0:T(8,128)S(1)}, u32[]{:S(2)}, u32[]{:S(2)}) collective-permute-start(f32[24,1024]{1,0:T(8,128)S(1)} %add.108.a_ref), channel_id=1, source_target_pairs={{0,24},{8,0},{16,8},{24,16},{1,25},{9,1},{17,9},{25,17},{2,26},{10... | collective-permute-start | bytes 294920 | tf_op jit(solution)/shard_map/ppermute | solution.py:370
  98.1 24.9 %all-to-all-start.2 = ((f32[64,16,128]{2,1,0:T(8,128)}), f32[64,16,128]{2,1,0:T(8,128)S(1)}, u32[]{:S(2)}, u32[]{:S(2)}) async-start(f32[64,16,128]{2,1,0:T(8,128)} %noise.1), calls=%async_computation.2 | async-start | bytes 1048576 | tf_op jit(solution)/shard_map/all_to_all | solution.py:479
  105.2 97.0 %all-gather.15.cloned.1.call-start = ((), (), s32[]{:S(2)}) async-start(), calls=%async_computation.7 | async-start | bytes 1769472 | tf_op jit(solution)/shard_map/all_gather | solution.py:582
  107.8 19.4 %collective-permute-start.11 = (f32[24,1024]{1,0:T(8,128)S(1)}, f32[24,1024]{1,0:T(8,128)S(1)}, u32[]{:S(2)}, u32[]{:S(2)}) collective-permute-start(f32[24,1024]{1,0:T(8,128)S(1)} %add.109.a_ref), channel_id=1, source_target_pairs={{0,8},{8,16},{16,24},{24,0},{1,9},{9,17},{17,25},{25,1},{2,10},{10... | collective-permute-start | bytes 294920 | tf_op jit(solution)/shard_map/ppermute | solution.py:370
  109.2 18.0 %collective-permute-start.12 = (f32[24,1024]{1,0:T(8,128)S(1)}, f32[24,1024]{1,0:T(8,128)S(1)}, u32[]{:S(2)}, u32[]{:S(2)}) collective-permute-start(f32[24,1024]{1,0:T(8,128)S(1)} %add.109.a_ref), channel_id=1, source_target_pairs={{0,16},{8,24},{16,0},{24,8},{1,17},{9,25},{17,1},{25,9},{2,18},{10... | collective-permute-start | bytes 294920 | tf_op jit(solution)/shard_map/ppermute | solution.py:370
  111.6 15.6 %collective-permute-start.13 = (f32[24,1024]{1,0:T(8,128)S(1)}, f32[24,1024]{1,0:T(8,128)S(1)}, u32[]{:S(2)}, u32[]{:S(2)}) collective-permute-start(f32[24,1024]{1,0:T(8,128)S(1)} %add.109.a_ref), channel_id=1, source_target_pairs={{0,24},{8,0},{16,8},{24,16},{1,25},{9,1},{17,9},{25,17},{2,26},{10... | collective-permute-start | bytes 294920 | tf_op jit(solution)/shard_map/ppermute | solution.py:370
  133.1 8.3 %collective-permute-start.15 = (f32[24,1024]{1,0:T(8,128)S(1)}, f32[24,1024]{1,0:T(8,128)S(1)}, u32[]{:S(2)}, u32[]{:S(2)}) collective-permute-start(f32[24,1024]{1,0:T(8,128)S(1)} %add.110.a_ref), channel_id=1, source_target_pairs={{0,8},{8,16},{16,24},{24,0},{1,9},{9,17},{17,25},{25,1},{2,10},{10... | collective-permute-start | bytes 294920 | tf_op jit(solution)/shard_map/ppermute | solution.py:370
  134.1 7.3 %collective-permute-start.16 = (f32[24,1024]{1,0:T(8,128)S(1)}, f32[24,1024]{1,0:T(8,128)S(1)}, u32[]{:S(2)}, u32[]{:S(2)}) collective-permute-start(f32[24,1024]{1,0:T(8,128)S(1)} %add.110.a_ref), channel_id=1, source_target_pairs={{0,16},{8,24},{16,0},{24,8},{1,17},{9,25},{17,1},{25,9},{2,18},{10... | collective-permute-start | bytes 294920 | tf_op jit(solution)/shard_map/ppermute | solution.py:370
  136.5 5.0 %collective-permute-start.17 = (f32[24,1024]{1,0:T(8,128)S(1)}, f32[24,1024]{1,0:T(8,128)S(1)}, u32[]{:S(2)}, u32[]{:S(2)}) collective-permute-start(f32[24,1024]{1,0:T(8,128)S(1)} %add.110.a_ref), channel_id=1, source_target_pairs={{0,24},{8,0},{16,8},{24,16},{1,25},{9,1},{17,9},{25,17},{2,26},{10... | collective-permute-start | bytes 294920 | tf_op jit(solution)/shard_map/ppermute | solution.py:370
  148.1 7.5 %collective-permute-start.19 = (f32[24,1024]{1,0:T(8,128)S(1)}, f32[24,1024]{1,0:T(8,128)S(1)}, u32[]{:S(2)}, u32[]{:S(2)}) collective-permute-start(f32[24,1024]{1,0:T(8,128)S(1)} %add.111.a_ref), channel_id=1, source_target_pairs={{0,8},{8,16},{16,24},{24,0},{1,9},{9,17},{17,25},{25,1},{2,10},{10... | collective-permute-start | bytes 294920 | tf_op jit(solution)/shard_map/ppermute | solution.py:370
  149.5 7.1 %collective-permute-start.20 = (f32[24,1024]{1,0:T(8,128)S(1)}, f32[24,1024]{1,0:T(8,128)S(1)}, u32[]{:S(2)}, u32[]{:S(2)}) collective-permute-start(f32[24,1024]{1,0:T(8,128)S(1)} %add.111.a_ref), channel_id=1, source_target_pairs={{0,16},{8,24},{16,0},{24,8},{1,17},{9,25},{17,1},{25,9},{2,18},{10... | collective-permute-start | bytes 294920 | tf_op jit(solution)/shard_map/ppermute | solution.py:370
  165.8 30.0 %all-to-all-start.3 = ((f32[64,16,128]{2,1,0:T(8,128)}), f32[64,16,128]{2,1,0:T(8,128)S(1)}, u32[]{:S(2)}, u32[]{:S(2)}) async-start(f32[64,16,128]{2,1,0:T(8,128)} %filter.1), calls=%async_computation.3 | async-start | bytes 1048576 | tf_op jit(solution)/shard_map/all_to_all | solution.py:583
  (38 other events, 184.4 us)
Sparse Core Ops, SparseCore 0:
  11.4 55.0 all-gather.8
  68.3 39.5 all-gather.10
  109.7 42.9 all-gather.12
  157.5 44.6 all-gather.14

commit v4 on v3

--- a/solution.py
+++ b/solution.py
@@ -111,10 +111,10 @@
 
 def lower_kernel(one_ref, two_ref, three_ref, near_ref, far_ref):
     near_ref[0:16] = one_ref[0]
-    for j in range(2):
-        near_ref[16 * j + 16 : 16 * j + 32] = two_ref[0, :, LENGTH * j : LENGTH * (j + 1)]
+    near_ref[16:32] = two_ref[0, :, 0:LENGTH]
+    far_ref[0:16] = two_ref[0, :, LENGTH : 2 * LENGTH]
     for j in range(3):
-        far_ref[16 * j : 16 * j + 16] = three_ref[0, :, LENGTH * j : LENGTH * (j + 1)]
+        far_ref[16 * j + 16 : 16 * j + 32] = three_ref[0, :, LENGTH * j : LENGTH * (j + 1)]
 
 
 def bundle_kernel(index_ref, columns_ref, *refs):
@@ -313,22 +313,33 @@
             high_ref[k] = high
             low_ref[k] = low
 
-    own = index_ref[0] * 16
-    row = lax.broadcasted_iota(jnp.int32, (128, LENGTH), 0) + block * 128
-    col = lax.broadcasted_iota(jnp.int32, (128, LENGTH), 1)
+    def subtract(base, first):
+        for step in range(panels):
+            panel = first_panel + step
+            rows = factor_refs[step][...].reshape(128, LENGTH)
+            if first:
+                own = index_ref[0] * 16
+                row = lax.broadcasted_iota(jnp.int32, (64, LENGTH), 0)
+                col = lax.broadcasted_iota(jnp.int32, (64, LENGTH), 1)
+                mine = (row // 16 == panel) & (col == own + row % 16)
+                rows = jnp.concatenate([jnp.where(mine, -1.0, 0.0), rows[64:]])
+            rows_high, rows_low = split(rows)
+            wide = dot(jnp.concatenate([rows_high, rows_low]), high_ref[step], NT)
+            base = base - (wide[:128] + wide[128:] + dot(rows_high, low_ref[step], NT))
+        out_ref[...] = base.reshape(8, 16, 128)
+
     base = base_ref[...].reshape(128, 128)
-    if first_panel == 0:
-        base_row = lax.broadcasted_iota(jnp.int32, (128, 128), 0) + block * 128
-        base = jnp.where(base_row < 64, 0.0, base)
-    for step in range(panels):
-        panel = first_panel + step
-        rows = factor_refs[step][...].reshape(128, LENGTH)
-        mine = (row // 16 == panel) & (col == own + row % 16)
-        rows = jnp.where(row < 64, jnp.where(mine, -1.0, 0.0), rows)
-        rows_high, rows_low = split(rows)
-        wide = dot(jnp.concatenate([rows_high, rows_low]), high_ref[step], NT)
-        base = base - (wide[:128] + wide[128:] + dot(rows_high, low_ref[step], NT))
-    out_ref[...] = base.reshape(8, 16, 128)
+
+    @pl.when(block == 0)
+    def _():
+        if first_panel == 0:
+            subtract(jnp.concatenate([jnp.zeros((64, 128), F32), base[64:]]), True)
+        else:
+            subtract(base, True)
+
+    @pl.when(block > 0)
+    def _():
+        subtract(base, False)
 
 
 def spec(*shape):
@@ -431,8 +442,8 @@
         lower_kernel,
         "lower",
         [block_at((1, 16, LENGTH * k), (k, 0, 0)) for k in range(1, 4)],
-        [spec(48, LENGTH)] * 2,
-        [shape_of(48, LENGTH)] * 2,
+        [spec(32, LENGTH), spec(64, LENGTH)],
+        [shape_of(32, LENGTH), shape_of(64, LENGTH)],
         0,
         800_000,
     )(factor, factor, factor)
@@ -484,8 +495,9 @@
         block_at((2, LENGTH), (0, k)),
     ]
     side_spec = lambda k: block_at((1, COLS, 128), (k, 0, 0))
-    factor_spec = lambda k, j: block_at((8, 16, LENGTH), (0, j + (k == 2), 0))
-    factor_rows = lambda k: lower_far if k == 3 else lower
+    factor_at = {(1, 0): 0, (2, 0): 1, (2, 1): 0, (3, 0): 1, (3, 1): 2, (3, 2): 3}
+    factor_spec = lambda k, j: block_at((8, 16, LENGTH), (0, factor_at[k, j], 0))
+    factor_rows = lambda k, j: lower_far if k + j > 2 else lower
     inverse_specs = lambda k: [
         block_at((8, 16, 128), (0, a if k == 1 else k + 2 * a, 0)) for a in range(2)
     ] * 4
@@ -517,9 +529,9 @@
         300_000_000,
         1_500_000,
     )(index, spectrum.reshape(LENGTH, 32), quarter)
-    box = [even, odd]
-    tie((parts, (0, 1, 2, 3)), (own, (0, 1, 2, 3)), (box, (0, 1)))
-    even, odd = box
+    box = [even, odd, slab]
+    tie((parts, (0, 1, 2, 3)), (own, (0, 1, 2, 3)), (box, (0, 1, 2)))
+    even, odd, slab = box
     unknowns = []
     work = sides
     pencil = slab
@@ -537,7 +549,7 @@
             40_000_000,
             1_500_000,
             inverse_scratch,
-        )(index, work, *parts, factor_rows(panel), *[own[at] for at in inverses], *unknowns[1:2] * (panel == 3))
+        )(index, work, *parts, factor_rows(panel, panel - 1), *[own[at] for at in inverses], *unknowns[1:2] * (panel == 3))
         unknowns.append(unknown)
         parts = share(partial)
         if panel == 1:
@@ -551,14 +563,14 @@
                 + [spec(64, 16, 128) if panel == 1 else pencil_spec]
                 + [panel_spec] * panel
                 + [side_spec(panel + 1)] * later
-                + [factor_spec(panel + 1, j) for j in range(panel)] * later,
+                + [factor_spec(panel + 1, j) for j in range(panel * later)],
                 [pencil_spec] + [spec(1, COLS, 128)] * later,
                 [shape_of(LENGTH, 128)] + [shape_of(1, COLS, 128)] * later,
                 2 * 2 * 128 * LENGTH * LENGTH,
                 1_500_000,
             )(
                 cell_x, waves, planes, pencil, *unknowns, *[sides] * later,
-                *[factor_rows(panel + 1)] * (panel * later),
+                *[factor_rows(panel + 1, j) for j in range(panel * later)],
             )
         )
         tie((parts, (0, 1, 2, 3)), (box, (0, 1) if later else (0,)))

time: 219 us -> 214 us (0.977)
  waiting for transfers between devices: 63.8 us -> 59.8 us
    all_to_all x1, waiting for transfers between devices: 10.2 us -> 0.94 us  [per_device(): slab = lax.all_to_all(slab, WIDE, 0, 0)]
    all_gather x1, waiting for transfers between devices: 0.43 us -> 4.31 us  [per_device(): late = lax.all_gather(jnp.concatenate([pair[0], late]), 'z')]
    ppermute x12, waiting for transfers between devices: 3.61 us -> 6.8 us  [share(): lax.ppermute(total, 'x', ring(4, step))]
    all_to_all x1, waiting for transfers between devices: 26.6 us -> 23.8 us  [per_device(): quarter = lax.all_to_all(quarter, 'z', 0, 0)]
    all_to_all x1, starting transfers between devices: 7.94 us -> 10.4 us  [per_device(): slots = lax.all_to_all(slots, WIDE, 0, 0)]
  transfers between devices with their start and end apart: 30 -> 30, of which waited for: 12 -> 14; matrix products, arithmetic and copies ran while one was open for 5% -> 5% of each run, Pallas kernels for 22% -> 23%
where the time goes in v4:
time: 214 us; the launch traced here: 211 us
  starting transfers between devices  63.6 us (30%)
  waiting for transfers between devices  59.8 us (28%)
  Pallas kernels  59.6 us (28%)
  between operations  14.2 us (7%)
  other arithmetic  7.98 us (4%)
  local copies, waits for them, and re-layouts  6.14 us (3%)
    all_to_all x1, waiting for transfers between devices, per_device(): quarter = lax.all_to_all(quarter, 'z', 0, 0)  23.8 us
    all_to_all x1, waiting for transfers between devices, per_device(): slots = lax.all_to_all(slots, WIDE, 0, 0)  18.2 us
    ppermute x12, starting transfers between devices, share(): lax.ppermute(total, 'x', ring(4, step))  15.6 us
    pallas_call x2, Pallas kernels, update(): call(functools.partial(update_kernel, first_panel, panels), 'update', [SM...  11.5 us
    all_to_all x1, starting transfers between devices, per_device(): slots = lax.all_to_all(slots, WIDE, 0, 0)  10.4 us
    pallas_call x3, Pallas kernels, per_device(): call(functools.partial(wait_kernel, panel), f'wait{panel}', obs_specs(pan...  9.58 us
    pallas_call x1, Pallas kernels, per_device(): call(filter_kernel, 'filter', [spec(LENGTH, 128)] + obs_specs(3) + [panel...  8.43 us
    all_to_all x1, starting transfers between devices, per_device(): slab = lax.all_to_all(slab, WIDE, 0, 0)  8.32 us
  transfers between devices with their start and end apart: 30, of which 14 were waited for; matrix products, arithmetic and copies ran while one was open for 5% of the time, Pallas kernels for 23%

profile of v4, /device:TPU:1, one launch (start us, length us, event | category | flops | bytes accessed | tf_op | source)
XLA Modules:
  0.0 211.3 jit_solution(4927912820086065101)
XLA Ops:
  11.3 6.6 %all-to-all-start = ((f32[8,64,128]{2,1,0:T(8,128)}), f32[8,64,128]{2,1,0:T(8,128)S(1)}, u32[]{:S(2)}, u32[]{:S(2)}) async-start(f32[8,64,128]{2,1,0:T(8,128)} %get-tuple-element.72), calls=%async_computation | async-start | bytes 524288 | tf_op jit(solution)/shard_map/all_to_all | solution.py:438
  18.5 2.6 %collective-permute-start.1 = (f32[64,128]{1,0:T(8,128)S(1)}, f32[64,128]{1,0:T(8,128)S(1)}, u32[]{:S(2)}, u32[]{:S(2)}) collective-permute-start(f32[64,128]{1,0:T(8,128)S(1)} %copy-done.28), channel_id=1, source_target_pairs={{0,2},{1,3},{2,0},{3,1},{4,6},{5,7},{6,4},{7,5},{8,10},{9,11},{10,... | collective-permute-start | bytes 98312 | tf_op jit(solution)/shard_map/ppermute | solution.py:452
  27.8 8.2 %all-to-all-start.1 = ((f32[8,272,128]{2,1,0:T(8,128)}), f32[8,272,128]{2,1,0:T(8,128)S(1)}, u32[]{:S(2)}, u32[]{:S(2)}) async-start(f32[8,272,128]{2,1,0:T(8,128)} %bundle.1), calls=%async_computation.1 | async-start | bytes 2228224 | tf_op jit(solution)/shard_map/all_to_all | solution.py:466
  37.3 4.9 %noise.1 = f32[64,16,128]{2,1,0:T(8,128)} custom-call(f32[128,1024]{1,0:T(8,128)} %reshape.57.noise_ref, bf16[1024,1024]{1,0:T(8,128)(2,1)} %constant.129.clone.high_ref, bf16[1024,1024]{1,0:T(8,128)(2,1)} %constant.130.clone.low_ref), custom_call_target="tpu_custom_call" | custom-call | flops 805306368 | bytes 5000000 | tf_op jit(solution)/shard_map/noise/pallas_call | solution.py:468
  45.2 23.8 %all-to-all-done.1.slab_ref.inverse_ref.extra_ref = f32[8,272,128]{2,1,0:T(8,128)S(1)} async-done(((f32[8,272,128]{2,1,0:T(8,128)}), f32[8,272,128]{2,1,0:T(8,128)S(1)}, u32[]{:S(2)}, u32[]{:S(2)}) %all-to-all-start.1) | async-done | bytes 1114144 | tf_op jit(solution)/shard_map/all_to_all | solution.py:466
  69.0 8.3 %all-to-all-start.2 = ((f32[64,16,128]{2,1,0:T(8,128)}), f32[64,16,128]{2,1,0:T(8,128)S(1)}, u32[]{:S(2)}, u32[]{:S(2)}) async-start(f32[64,16,128]{2,1,0:T(8,128)} %noise.1), calls=%async_computation.2 | async-start | bytes 1048576 | tf_op jit(solution)/shard_map/all_to_all | solution.py:490
  78.0 2.7 %collective-permute-start.8 = (f32[8,96,128]{2,1,0:T(8,128)S(1)}, f32[8,96,128]{2,1,0:T(8,128)S(1)}, u32[]{:S(2)}, u32[]{:S(2)}) collective-permute-start(f32[8,96,128]{2,1,0:T(8,128)S(1)} %slice.19.refs_0_.refs_1_), channel_id=1, source_target_pairs={{0,2},{1,3},{2,0},{3,1},{4,6},{5,7},{6,4},{7,5},{8,10},{9,11},{10,... | collective-permute-start | bytes 1179656 | tf_op jit(solution)/shard_map/ppermute | solution.py:489
  90.7 2.9 %collective-permute-done.4.b_ref = f32[24,1024]{1,0:T(8,128)S(1)} collective-permute-done((f32[24,1024]{1,0:T(8,128)S(1)}, f32[24,1024]{1,0:T(8,128)S(1)}, u32[]{:S(2)}, u32[]{:S(2)}) %collective-permute-start.4) | collective-permute-done | bytes 98336 | tf_op jit(solution)/shard_map/ppermute | solution.py:381
  95.5 3.8 %spectrum.1 = (f32[1024,128]{1,0:T(8,128)}, f32[512,128]{1,0:T(8,128)}) custom-call(s32[2]{0:T(128)} %pad_add_fusion.index_ref, f32[1024,32]{1,0:T(8,128)} %copy.15.spectrum_ref, f32[8,272,128]{2,1,0:T(8,128)} %copy-done), custom_call_target="tpu_custom_call" | custom-call | flops 300000000 | bytes 1500000 | tf_op jit(solution)/shard_map/spectrum/pallas_call | solution.py:523
  100.4 2.7 %step1.1 = (f32[24,1024]{1,0:T(8,128)}, f32[24,1024]{1,0:T(8,128)}, f32[32,1024]{1,0:T(8,128)}) custom-call(s32[2]{0:T(128)} %pad_add_fusion.index_ref, f32[4,24,128]{2,1,0:T(8,128)} %get-tuple-element.81.start_ref.refs_5_.refs_6_, f32[24,1024]{1,0:T(8,128)} %copy-done.10, f32[24,1024]{1,0:T(8,128)} %copy-done.18, f32[24,1024]{1,0:T(8,128)} %copy-done.19, ...), custom_call_target="tpu_custom_call" | custom-call | flops 40000000 | bytes 1500000 | tf_op jit(solution)/shard_map/step1/pallas_call | solution.py:539
  107.8 3.2 %collective-permute-start.12 = (f32[24,1024]{1,0:T(8,128)S(1)}, f32[24,1024]{1,0:T(8,128)S(1)}, u32[]{:S(2)}, u32[]{:S(2)}) collective-permute-start(f32[24,1024]{1,0:T(8,128)S(1)} %add.109.a_ref), channel_id=1, source_target_pairs={{0,16},{8,24},{16,0},{24,8},{1,17},{9,25},{17,1},{25,9},{2,18},{10... | collective-permute-start | bytes 294920 | tf_op jit(solution)/shard_map/ppermute | solution.py:381
  111.3 3.5 %wait1.1 = (f32[1024,128]{1,0:T(8,128)}, f32[1,24,128]{2,1,0:T(8,128)}) custom-call(s32[1,4096]{1,0:T(1,128)} %bitcast.22, f32[16,4096]{1,0:T(8,128)} %fusion.3.refs_1_.wave_ref, f32[2,4096]{1,0:T(2,128)} %add_convert_fusion.refs_2_.plane_ref, f32[64,16,128]{2,1,0:T(8,128)} %copy-done.6, f32[24,1024]{1,0:T(8,128)} %get-tuple-element.103.refs_4_, ...), custom_call_target="tpu_custom_call" | custom-call | flops 536870912 | bytes 1500000 | tf_op jit(solution)/shard_map/wait1/pallas_call | solution.py:559
  116.3 2.5 %step2.1 = (f32[24,1024]{1,0:T(8,128)}, f32[24,1024]{1,0:T(8,128)}) custom-call(s32[2]{0:T(128)} %pad_add_fusion.index_ref, f32[1,24,128]{2,1,0:T(8,128)} %get-tuple-element.106.start_ref, f32[24,1024]{1,0:T(8,128)} %copy-done.12, f32[24,1024]{1,0:T(8,128)} %copy-done.22, f32[24,1024]{1,0:T(8,128)} %copy-done.24, f32[24,1024]{1,0:T(8,128)} %copy-done.26, ...), custom_call_target="tpu_custom_call" | custom-call | flops 40000000 | bytes 1500000 | tf_op jit(solution)/shard_map/step2/pallas_call | solution.py:539
  125.7 3.3 %wait2.1 = (f32[1024,128]{1,0:T(8,128)}, f32[1,24,128]{2,1,0:T(8,128)}) custom-call(s32[1,4096]{1,0:T(1,128)} %bitcast.23, f32[16,4096]{1,0:T(8,128)} %fusion.3.refs_1_.wave_ref, f32[2,4096]{1,0:T(2,128)} %add_convert_fusion.refs_2_.plane_ref, f32[1024,128]{1,0:T(8,128)} %get-tuple-element.113.refs_3_, f32[24,1024]{1,0:T(8,128)} %get-tuple-element.103.refs_4_, ...), custom_call_target="tpu_custom_call" | custom-call | flops 536870912 | bytes 1500000 | tf_op jit(solution)/shard_map/wait2/pallas_call | solution.py:559
  130.8 2.6 %step3.1 = (f32[24,1024]{1,0:T(8,128)}, f32[24,1024]{1,0:T(8,128)}, f32[32,1024]{1,0:T(8,128)}) custom-call(s32[2]{0:T(128)} %pad_add_fusion.index_ref, f32[1,24,128]{2,1,0:T(8,128)} %get-tuple-element.117.start_ref, f32[24,1024]{1,0:T(8,128)} %copy-done.11, f32[24,1024]{1,0:T(8,128)} %copy-done.21, f32[24,1024]{1,0:T(8,128)} %copy-done.23, ...), custom_call_target="tpu_custom_call" | custom-call | flops 40000000 | bytes 1500000 | tf_op jit(solution)/shard_map/step3/pallas_call | solution.py:539
  137.6 2.7 %collective-permute-start.20 = (f32[24,1024]{1,0:T(8,128)S(1)}, f32[24,1024]{1,0:T(8,128)S(1)}, u32[]{:S(2)}, u32[]{:S(2)}) collective-permute-start(f32[24,1024]{1,0:T(8,128)S(1)} %add.111.a_ref), channel_id=1, source_target_pairs={{0,16},{8,24},{16,0},{24,8},{1,17},{9,25},{17,1},{25,9},{2,18},{10... | collective-permute-start | bytes 294920 | tf_op jit(solution)/shard_map/ppermute | solution.py:381
  140.4 2.8 %wait3.1.pencil_ref = f32[1024,128]{1,0:T(8,128)} custom-call(s32[1,4096]{1,0:T(1,128)} %bitcast.24, f32[16,4096]{1,0:T(8,128)} %fusion.3.refs_1_.wave_ref, f32[2,4096]{1,0:T(2,128)} %add_convert_fusion.refs_2_.plane_ref, f32[1024,128]{1,0:T(8,128)} %get-tuple-element.123.refs_3_, f32[24,1024]{1,0:T(8,128)} %get-tuple-element.103.refs_4_, ...), custom_call_target="tpu_custom_call" | custom-call | flops 536870912 | bytes 1500000 | tf_op jit(solution)/shard_map/wait3/pallas_call | solution.py:559
  145.8 8.4 %filter.1 = f32[64,16,128]{2,1,0:T(8,128)} custom-call(f32[1024,128]{1,0:T(8,128)} %wait3.1.pencil_ref, s32[1,4096]{1,0:T(1,128)} %bitcast.25, f32[16,4096]{1,0:T(8,128)} %fusion.3.refs_1_.wave_ref, f32[2,4096]{1,0:T(2,128)} %add_convert_fusion.refs_2_.plane_ref, f32[24,1024]{1,0:T(8,128)} %copy-done.8, f32[24,1024]{1,0:T(8,128)} %copy-done.13, ...), custom_call_target="tpu_custom_call" | custom-call | flops 2147483648 | bytes 11000000 | tf_op jit(solution)/shard_map/filter/pallas_call | solution.py:579
  154.3 10.4 %all-to-all-start.3 = ((f32[64,16,128]{2,1,0:T(8,128)}), f32[64,16,128]{2,1,0:T(8,128)S(1)}, u32[]{:S(2)}, u32[]{:S(2)}) async-start(f32[64,16,128]{2,1,0:T(8,128)} %filter.1), calls=%async_computation.3 | async-start | bytes 1048576 | tf_op jit(solution)/shard_map/all_to_all | solution.py:595
  164.8 4.5 %update.2.base_ref = f32[32,16,128]{2,1,0:T(8,128)} custom-call(s32[2]{0:T(128)} %pad_add_fusion.index_ref, f32[32,16,128]{2,1,0:T(8,128)} %base_ref.1, f32[8,32,1024]{2,1,0:T(8,128)} %bitcast.21, f32[32,16,4096]{2,1,0:T(8,128)} %refs_2_), custom_call_target="tpu_custom_call" | custom-call | flops 402653184 | bytes 2700000 | tf_op jit(solution)/shard_map/update/pallas_call | solution.py:393
  169.3 18.2 %all-to-all-done.3.slots_ref = f32[64,16,128]{2,1,0:T(8,128)S(1)} async-done(((f32[64,16,128]{2,1,0:T(8,128)}), f32[64,16,128]{2,1,0:T(8,128)S(1)}, u32[]{:S(2)}, u32[]{:S(2)}) %all-to-all-start.3) | async-done | bytes 524320 | tf_op jit(solution)/shard_map/all_to_all | solution.py:595
  188.3 5.1 %close.1 = f32[16,4,2,1024]{3,2,1,0:T(2,128)} custom-call(f32[64,16,128]{2,1,0:T(8,128)} %copy-done.5, bf16[1024,1024]{1,0:T(8,128)(2,1)} %constant.129.clone.high_ref, bf16[1024,1024]{1,0:T(8,128)(2,1)} %constant.130.clone.low_ref), custom_call_target="tpu_custom_call" | custom-call | flops 805306368 | bytes 5500000 | tf_op jit(solution)/shard_map/close/pallas_call | solution.py:598
  193.4 4.3 %all-gather.15.cloned.1.call-done = f32[384,1024]{1,0:T(8,128)} async-done(((f32[48,1024]{1,0:T(8,128)}), f32[384,1024]{1,0:T(8,128)}) %all-gather.15.cloned.1.call-update) | async-done | bytes 1572880 | tf_op jit(solution)/shard_map/all_gather | solution.py:594
  197.7 7.0 %update.3 = f32[32,16,128]{2,1,0:T(8,128)} custom-call(s32[2]{0:T(128)} %pad_add_fusion.index_ref, f32[32,16,128]{2,1,0:T(8,128)} %update.2.base_ref, f32[8,48,1024]{2,1,0:T(8,128)} %bitcast.20, f32[32,16,4096]{2,1,0:T(8,128)} %refs_2_, f32[32,16,4096]{2,1,0:T(8,128)} %refs_2_, f32[32,16,4096]{2,1,0:T(8,128)} %refs_2_), custom_call_target="tpu_custom_call" | custom-call | flops 1207959552 | bytes 8100000 | tf_op jit(solution)/shard_map/update/pallas_call | solution.py:393
  (141 shorter events, 51.9 us)
Async XLA Ops:
  7.2 93.2 %all-gather.9.cloned.1.call-start = ((), (), s32[]{:S(2)}) async-start(), calls=%async_computation.4 | async-start | bytes 1179648 | tf_op jit(solution)/shard_map/all_gather | solution.py:450
  11.3 13.1 %all-to-all-start = ((f32[8,64,128]{2,1,0:T(8,128)}), f32[8,64,128]{2,1,0:T(8,128)S(1)}, u32[]{:S(2)}, u32[]{:S(2)}) async-start(f32[8,64,128]{2,1,0:T(8,128)} %get-tuple-element.72), calls=%async_computation | async-start | bytes 524288 | tf_op jit(solution)/shard_map/all_to_all | solution.py:438
  17.8 97.8 %all-gather.11.cloned.1.call-start = ((), (), s32[]{:S(2)}) async-start(), calls=%async_computation.5 | async-start | bytes 2359296 | tf_op jit(solution)/shard_map/all_gather | solution.py:465
  17.8 5.5 %collective-permute-start = (f32[64,128]{1,0:T(8,128)S(1)}, f32[64,128]{1,0:T(8,128)S(1)}, u32[]{:S(2)}, u32[]{:S(2)}) collective-permute-start(f32[64,128]{1,0:T(8,128)S(1)} %copy-done.28), channel_id=1, source_target_pairs={{0,1},{1,2},{2,3},{3,0},{4,5},{5,6},{6,7},{7,4},{8,9},{9,10},{10,1... | collective-permute-start | bytes 98312 | tf_op jit(solution)/shard_map/ppermute | solution.py:452
  18.5 4.9 %collective-permute-start.1 = (f32[64,128]{1,0:T(8,128)S(1)}, f32[64,128]{1,0:T(8,128)S(1)}, u32[]{:S(2)}, u32[]{:S(2)}) collective-permute-start(f32[64,128]{1,0:T(8,128)S(1)} %copy-done.28), channel_id=1, source_target_pairs={{0,2},{1,3},{2,0},{3,1},{4,6},{5,7},{6,4},{7,5},{8,10},{9,11},{10,... | collective-permute-start | bytes 98312 | tf_op jit(solution)/shard_map/ppermute | solution.py:452
  27.8 41.2 %all-to-all-start.1 = ((f32[8,272,128]{2,1,0:T(8,128)}), f32[8,272,128]{2,1,0:T(8,128)S(1)}, u32[]{:S(2)}, u32[]{:S(2)}) async-start(f32[8,272,128]{2,1,0:T(8,128)} %bundle.1), calls=%async_computation.1 | async-start | bytes 2228224 | tf_op jit(solution)/shard_map/all_to_all | solution.py:466
  69.0 31.4 %all-to-all-start.2 = ((f32[64,16,128]{2,1,0:T(8,128)}), f32[64,16,128]{2,1,0:T(8,128)S(1)}, u32[]{:S(2)}, u32[]{:S(2)}) async-start(f32[64,16,128]{2,1,0:T(8,128)} %noise.1), calls=%async_computation.2 | async-start | bytes 1048576 | tf_op jit(solution)/shard_map/all_to_all | solution.py:490
  77.3 87.4 %all-gather.13.cloned.1.call-start = ((), (), s32[]{:S(2)}) async-start(), calls=%async_computation.6 | async-start | bytes 1179648 | tf_op jit(solution)/shard_map/all_gather | solution.py:556
  77.4 21.9 %collective-permute-start.7 = (f32[8,96,128]{2,1,0:T(8,128)S(1)}, f32[8,96,128]{2,1,0:T(8,128)S(1)}, u32[]{:S(2)}, u32[]{:S(2)}) collective-permute-start(f32[8,96,128]{2,1,0:T(8,128)S(1)} %slice.19.refs_0_.refs_1_), channel_id=1, source_target_pairs={{0,1},{1,2},{2,3},{3,0},{4,5},{5,6},{6,7},{7,4},{8,9},{9,10},{10,1... | collective-permute-start | bytes 1179656 | tf_op jit(solution)/shard_map/ppermute | solution.py:489
  78.0 21.4 %collective-permute-start.8 = (f32[8,96,128]{2,1,0:T(8,128)S(1)}, f32[8,96,128]{2,1,0:T(8,128)S(1)}, u32[]{:S(2)}, u32[]{:S(2)}) collective-permute-start(f32[8,96,128]{2,1,0:T(8,128)S(1)} %slice.19.refs_0_.refs_1_), channel_id=1, source_target_pairs={{0,2},{1,3},{2,0},{3,1},{4,6},{5,7},{6,4},{7,5},{8,10},{9,11},{10,... | collective-permute-start | bytes 1179656 | tf_op jit(solution)/shard_map/ppermute | solution.py:489
  80.7 18.7 %collective-permute-start.9 = (f32[8,96,128]{2,1,0:T(8,128)S(1)}, f32[8,96,128]{2,1,0:T(8,128)S(1)}, u32[]{:S(2)}, u32[]{:S(2)}) collective-permute-start(f32[8,96,128]{2,1,0:T(8,128)S(1)} %slice.19.refs_0_.refs_1_), channel_id=1, source_target_pairs={{0,3},{1,0},{2,1},{3,2},{4,7},{5,4},{6,5},{7,6},{8,11},{9,8},{10,9... | collective-permute-start | bytes 1179656 | tf_op jit(solution)/shard_map/ppermute | solution.py:489
  87.0 6.7 %collective-permute-start.4 = (f32[24,1024]{1,0:T(8,128)S(1)}, f32[24,1024]{1,0:T(8,128)S(1)}, u32[]{:S(2)}, u32[]{:S(2)}) collective-permute-start(f32[24,1024]{1,0:T(8,128)S(1)} %add.108.a_ref), channel_id=1, source_target_pairs={{0,8},{8,16},{16,24},{24,0},{1,9},{9,17},{17,25},{25,1},{2,10},{10... | collective-permute-start | bytes 294920 | tf_op jit(solution)/shard_map/ppermute | solution.py:381
  88.3 11.0 %collective-permute-start.5 = (f32[24,1024]{1,0:T(8,128)S(1)}, f32[24,1024]{1,0:T(8,128)S(1)}, u32[]{:S(2)}, u32[]{:S(2)}) collective-permute-start(f32[24,1024]{1,0:T(8,128)S(1)} %add.108.a_ref), channel_id=1, source_target_pairs={{0,16},{8,24},{16,0},{24,8},{1,17},{9,25},{17,1},{25,9},{2,18},{10... | collective-permute-start | bytes 294920 | tf_op jit(solution)/shard_map/ppermute | solution.py:381
  93.7 5.7 %collective-permute-start.6 = (f32[24,1024]{1,0:T(8,128)S(1)}, f32[24,1024]{1,0:T(8,128)S(1)}, u32[]{:S(2)}, u32[]{:S(2)}) collective-permute-start(f32[24,1024]{1,0:T(8,128)S(1)} %add.108.a_ref), channel_id=1, source_target_pairs={{0,24},{8,0},{16,8},{24,16},{1,25},{9,1},{17,9},{25,17},{2,26},{10... | collective-permute-start | bytes 294920 | tf_op jit(solution)/shard_map/ppermute | solution.py:381
  103.1 94.6 %all-gather.15.cloned.1.call-start = ((), (), s32[]{:S(2)}) async-start(), calls=%async_computation.7 | async-start | bytes 1769472 | tf_op jit(solution)/shard_map/all_gather | solution.py:594
  107.4 7.3 %collective-permute-start.11 = (f32[24,1024]{1,0:T(8,128)S(1)}, f32[24,1024]{1,0:T(8,128)S(1)}, u32[]{:S(2)}, u32[]{:S(2)}) collective-permute-start(f32[24,1024]{1,0:T(8,128)S(1)} %add.109.a_ref), channel_id=1, source_target_pairs={{0,8},{8,16},{16,24},{24,0},{1,9},{9,17},{17,25},{25,1},{2,10},{10... | collective-permute-start | bytes 294920 | tf_op jit(solution)/shard_map/ppermute | solution.py:381
  107.8 7.9 %collective-permute-start.12 = (f32[24,1024]{1,0:T(8,128)S(1)}, f32[24,1024]{1,0:T(8,128)S(1)}, u32[]{:S(2)}, u32[]{:S(2)}) collective-permute-start(f32[24,1024]{1,0:T(8,128)S(1)} %add.109.a_ref), channel_id=1, source_target_pairs={{0,16},{8,24},{16,0},{24,8},{1,17},{9,25},{17,1},{25,9},{2,18},{10... | collective-permute-start | bytes 294920 | tf_op jit(solution)/shard_map/ppermute | solution.py:381
  111.0 4.7 %collective-permute-start.13 = (f32[24,1024]{1,0:T(8,128)S(1)}, f32[24,1024]{1,0:T(8,128)S(1)}, u32[]{:S(2)}, u32[]{:S(2)}) collective-permute-start(f32[24,1024]{1,0:T(8,128)S(1)} %add.109.a_ref), channel_id=1, source_target_pairs={{0,24},{8,0},{16,8},{24,16},{1,25},{9,1},{17,9},{25,17},{2,26},{10... | collective-permute-start | bytes 294920 | tf_op jit(solution)/shard_map/ppermute | solution.py:381
  122.1 7.0 %collective-permute-start.15 = (f32[24,1024]{1,0:T(8,128)S(1)}, f32[24,1024]{1,0:T(8,128)S(1)}, u32[]{:S(2)}, u32[]{:S(2)}) collective-permute-start(f32[24,1024]{1,0:T(8,128)S(1)} %add.110.a_ref), channel_id=1, source_target_pairs={{0,8},{8,16},{16,24},{24,0},{1,9},{9,17},{17,25},{25,1},{2,10},{10... | collective-permute-start | bytes 294920 | tf_op jit(solution)/shard_map/ppermute | solution.py:381
  123.0 7.1 %collective-permute-start.16 = (f32[24,1024]{1,0:T(8,128)S(1)}, f32[24,1024]{1,0:T(8,128)S(1)}, u32[]{:S(2)}, u32[]{:S(2)}) collective-permute-start(f32[24,1024]{1,0:T(8,128)S(1)} %add.110.a_ref), channel_id=1, source_target_pairs={{0,16},{8,24},{16,0},{24,8},{1,17},{9,25},{17,1},{25,9},{2,18},{10... | collective-permute-start | bytes 294920 | tf_op jit(solution)/shard_map/ppermute | solution.py:381
  125.5 4.7 %collective-permute-start.17 = (f32[24,1024]{1,0:T(8,128)S(1)}, f32[24,1024]{1,0:T(8,128)S(1)}, u32[]{:S(2)}, u32[]{:S(2)}) collective-permute-start(f32[24,1024]{1,0:T(8,128)S(1)} %add.110.a_ref), channel_id=1, source_target_pairs={{0,24},{8,0},{16,8},{24,16},{1,25},{9,1},{17,9},{25,17},{2,26},{10... | collective-permute-start | bytes 294920 | tf_op jit(solution)/shard_map/ppermute | solution.py:381
  136.8 6.3 %collective-permute-start.19 = (f32[24,1024]{1,0:T(8,128)S(1)}, f32[24,1024]{1,0:T(8,128)S(1)}, u32[]{:S(2)}, u32[]{:S(2)}) collective-permute-start(f32[24,1024]{1,0:T(8,128)S(1)} %add.111.a_ref), channel_id=1, source_target_pairs={{0,8},{8,16},{16,24},{24,0},{1,9},{9,17},{17,25},{25,1},{2,10},{10... | collective-permute-start | bytes 294920 | tf_op jit(solution)/shard_map/ppermute | solution.py:381
  137.6 7.4 %collective-permute-start.20 = (f32[24,1024]{1,0:T(8,128)S(1)}, f32[24,1024]{1,0:T(8,128)S(1)}, u32[]{:S(2)}, u32[]{:S(2)}) collective-permute-start(f32[24,1024]{1,0:T(8,128)S(1)} %add.111.a_ref), channel_id=1, source_target_pairs={{0,16},{8,24},{16,0},{24,8},{1,17},{9,25},{17,1},{25,9},{2,18},{10... | collective-permute-start | bytes 294920 | tf_op jit(solution)/shard_map/ppermute | solution.py:381
  154.3 33.2 %all-to-all-start.3 = ((f32[64,16,128]{2,1,0:T(8,128)}), f32[64,16,128]{2,1,0:T(8,128)S(1)}, u32[]{:S(2)}, u32[]{:S(2)}) async-start(f32[64,16,128]{2,1,0:T(8,128)} %filter.1), calls=%async_computation.3 | async-start | bytes 1048576 | tf_op jit(solution)/shard_map/all_to_all | solution.py:595
  (38 other events, 183.4 us)
Sparse Core Ops, SparseCore 0:
  11.4 45.8 all-gather.8
  59.0 52.1 all-gather.10
  113.1 35.2 all-gather.12
  150.0 47.6 all-gather.14

commit v5 on v4

--- a/solution.py
+++ b/solution.py
@@ -16,7 +16,7 @@
 COLS = 24
 NN = (((1,), (0,)), ((), ()))
 NT = (((1,), (1,)), ((), ()))
-LIMIT = pltpu.CompilerParams(vmem_limit_bytes=56 * 1024 * 1024)
+LIMIT = pltpu.CompilerParams(vmem_limit_bytes=40 * 1024 * 1024)
 
 
 def halves(table):
@@ -172,13 +172,11 @@
 def step_kernel(panel, index_ref, start_ref, a_ref, b_ref, c_ref, d_ref, factor_ref, *refs):
     inverse_refs, refs = refs[:8], refs[8:]
     unknown = (a_ref[...] + b_ref[...]) + (c_ref[...] + d_ref[...])
-    if panel == 1:
-        refs[2][0:16] = unknown[0:16]
-        refs[2][16:32] = jnp.zeros((16, LENGTH), F32)
     if panel == 3:
-        older_ref, refs = refs[0], refs[1:]
-        refs[2][0:16] = older_ref[0:16]
-        refs[2][16:32] = unknown[0:16]
+        older_refs, refs = refs[:2], refs[2:]
+        refs[2][0:16] = older_refs[0][0:16]
+        refs[2][16:32] = older_refs[1][0:16]
+        refs[2][32:48] = unknown[0:16]
     out_ref, unknown_ref, high_ref, low_ref = refs[0], refs[1], refs[-2], refs[-1]
     unknown_ref[...] = unknown
     work = start_ref[0] - dot_nt(unknown, factor_ref[...].reshape(128, LENGTH))
@@ -300,23 +298,13 @@
     out_ref[...] = total.reshape(out_ref.shape)
 
 
-def update_kernel(
-    first_panel, panels, index_ref, base_ref, unknown_ref, *refs
-):
-    factor_refs, (out_ref, high_ref, low_ref) = refs[:panels], refs[panels:]
+def update_kernel(index_ref, base_ref, unknown_ref, *refs):
+    factor_refs, (out_ref, both_ref) = refs[:4], refs[4:]
     block = pl.program_id(0)
 
-    @pl.when(block == 0)
-    def _():
-        for k in range(panels):
-            high, low = split(unknown_ref[:, 16 * k : 16 * k + 16, :].reshape(128, LENGTH))
-            high_ref[k] = high
-            low_ref[k] = low
-
     def subtract(base, first):
-        for step in range(panels):
-            panel = first_panel + step
-            rows = factor_refs[step][...].reshape(128, LENGTH)
+        for panel in range(4):
+            rows = factor_refs[panel][...].reshape(128, LENGTH)
             if first:
                 own = index_ref[0] * 16
                 row = lax.broadcasted_iota(jnp.int32, (64, LENGTH), 0)
@@ -324,18 +312,21 @@
                 mine = (row // 16 == panel) & (col == own + row % 16)
                 rows = jnp.concatenate([jnp.where(mine, -1.0, 0.0), rows[64:]])
             rows_high, rows_low = split(rows)
-            wide = dot(jnp.concatenate([rows_high, rows_low]), high_ref[step], NT)
-            base = base - (wide[:128] + wide[128:] + dot(rows_high, low_ref[step], NT))
+            wide = dot(rows_high, both_ref[panel], NT)
+            base = base - (wide[:, :128] + wide[:, 128:])
+            base = base - dot(rows_low, both_ref[panel, 0:128], NT)
         out_ref[...] = base.reshape(8, 16, 128)
 
     base = base_ref[...].reshape(128, 128)
 
     @pl.when(block == 0)
     def _():
-        if first_panel == 0:
-            subtract(jnp.concatenate([jnp.zeros((64, 128), F32), base[64:]]), True)
-        else:
-            subtract(base, True)
+        for panel in range(4):
+            rows = unknown_ref[:, 16 * panel : 16 * panel + 16, :].reshape(128, LENGTH)
+            high, low = split(rows)
+            both_ref[panel, 0:128] = high
+            both_ref[panel, 128:256] = low
+        subtract(jnp.concatenate([jnp.zeros((64, 128), F32), base[64:]]), True)
 
     @pl.when(block > 0)
     def _():
@@ -389,30 +380,31 @@
             group[at] = flat.pop(0)
 
 
-def update(first_panel, panels, index, base, factor, unknowns):
+def update(index, base, factor, unknowns):
     return call(
-        functools.partial(update_kernel, first_panel, panels),
+        update_kernel,
         "update",
         [
             SMEM,
             pl.BlockSpec((8, 16, 128), lambda i: (i, 0, 0)),
-            spec(8, 16 * panels, LENGTH),
+            spec(8, 64, LENGTH),
         ]
         + [
-            pl.BlockSpec((8, 16, LENGTH), lambda i, place=first_panel + k: (i, 0, place))
-            for k in range(panels)
+            pl.BlockSpec((8, 16, LENGTH), lambda i, place=k: (i, 0, place))
+            for k in range(4)
         ],
         pl.BlockSpec((8, 16, 128), lambda i: (i, 0, 0)),
         shape_of(32, 16, 128),
-        3 * 2 * 512 * panels * LENGTH * 128,
-        2_700_000 * panels,
-        [pltpu.VMEM((panels, 128, LENGTH), BF16)] * 2,
+        3 * 2 * 512 * 4 * LENGTH * 128,
+        11_000_000,
+        [pltpu.VMEM((4, 256, LENGTH), BF16)],
         grid=4,
-    )(index, base, unknowns, *[factor] * panels)
+    )(index, base, unknowns, *[factor] * 4)
 
 
 SMEM = pl.BlockSpec(memory_space=pltpu.SMEM)
 ANY = pl.BlockSpec(memory_space=pl.ANY)
+NEAR = pl.BlockSpec(memory_space=pltpu.VMEM)
 TABLE = pltpu.VMEM((LENGTH, LENGTH), BF16)
 
 
@@ -503,7 +495,7 @@
     ] * 4
     inverses = [one for one in range(4) for _ in range(2)]
     inverse_scratch = [pltpu.VMEM((8, 128, 128), BF16)] * 2
-    panel_spec = spec(COLS, LENGTH)
+    panel_spec = NEAR
     panel_shape = shape_of(COLS, LENGTH)
     pencil_spec = spec(LENGTH, 128)
 
@@ -536,24 +528,22 @@
     work = sides
     pencil = slab
     for panel in range(1, 4):
-        partial, unknown, *pair = call(
+        partial, unknown, *solved_rows = call(
             functools.partial(step_kernel, panel),
             f"step{panel}",
             [SMEM, side_spec(1 if panel == 1 else 0)]
             + [panel_spec] * 4
             + [factor_spec(panel, panel - 1)]
             + inverse_specs(panel)
-            + [panel_spec] * (panel == 3),
-            [panel_spec] * 2 + [spec(32, LENGTH)] * (panel != 2),
-            [panel_shape] * 2 + [shape_of(32, LENGTH)] * (panel != 2),
+            + [panel_spec] * 2 * (panel == 3),
+            [panel_spec] * 2 + [spec(48, LENGTH)] * (panel == 3),
+            [panel_shape] * 2 + [shape_of(48, LENGTH)] * (panel == 3),
             40_000_000,
             1_500_000,
             inverse_scratch,
-        )(index, work, *parts, factor_rows(panel, panel - 1), *[own[at] for at in inverses], *unknowns[1:2] * (panel == 3))
+        )(index, work, *parts, factor_rows(panel, panel - 1), *[own[at] for at in inverses], *unknowns * (panel == 3))
         unknowns.append(unknown)
         parts = share(partial)
-        if panel == 1:
-            early = lax.all_gather(pair[0], "z")
         later = panel < 3
         box = list(
             call(
@@ -591,10 +581,8 @@
         [TABLE] * 4 + [pltpu.SemaphoreType.DMA((4,))],
     )(pencil, cell_x, waves, planes, *parts, x_high, x_low, back_high, back_low, even, odd)
     late = (parts[0][:16] + parts[1][:16]) + (parts[2][:16] + parts[3][:16])
-    late = lax.all_gather(jnp.concatenate([pair[0], late]), "z")
+    late = lax.all_gather(jnp.concatenate([solved_rows[0], late]), "z")
     slots = lax.all_to_all(slots, WIDE, 0, 0)
-    solved = update(0, 1, index, right_side, factor, early)
-    slots, solved = lax.optimization_barrier((slots, solved))
     correction = call(
         close_kernel,
         "close",
@@ -606,8 +594,8 @@
         [pltpu.VMEM((256, LENGTH), BF16)],
         grid=4,
     )(slots, z_high, z_low)
-    solved, correction = lax.optimization_barrier((solved, correction))
-    solved = update(1, 3, index, solved, factor, late)
+    base, correction = lax.optimization_barrier((right_side, correction))
+    solved = update(index, base, factor, late)
     return (solved, correction)
 
 

time: 214 us -> 211 us (0.986)
  blocking collectives: 0 us -> 32.3 us
  Pallas kernels: 59.6 us -> 30.3 us
  local copies, waits for them, and re-layouts: 6.14 us -> 33.1 us
  waiting for transfers between devices: 59.8 us -> 41.3 us
  starting transfers between devices: 63.6 us -> 55.2 us
  other arithmetic: 7.98 us -> 3.29 us
    all_to_all x0 -> x1, blocking collectives: none -> 32.3 us  [per_device(): slots = lax.all_to_all(slots, WIDE, 0, 0)]
    unnamed x65 -> x69, local copies, waits for them, and re-layouts: 3.3 us -> 28.9 us
    all_to_all x1 -> x0, waiting for transfers between devices: 18.2 us -> none  [per_device(): slots = lax.all_to_all(slots, WIDE, 0, 0)]
    all_to_all x1 -> x0, starting transfers between devices: 10.4 us -> none  [per_device(): slots = lax.all_to_all(slots, WIDE, 0, 0)]
    pallas_call x2 -> x1, Pallas kernels: 11.5 us -> 6.05 us  [update(): call(update_kernel, 'update', [SMEM, pl.BlockSpec((8, 16, 128), lambda i:...]
    pallas_call x3, Pallas kernels: 9.58 us -> 4.2 us  [per_device(): call(functools.partial(wait_kernel, panel), f'wait{panel}', obs_specs(pan...]
    all_gather x2 -> x1, waiting for transfers between devices: 4.33 us -> 0.01 us  [per_device(): late = lax.all_gather(jnp.concatenate([solved_rows[0], late]), 'z')]
    pallas_call x3, Pallas kernels: 7.83 us -> 3.72 us  [per_device(): call(functools.partial(step_kernel, panel), f'step{panel}', [SMEM, side_s...]
  transfers between devices with their start and end apart: 30 -> 28, of which waited for: 14 -> 13; matrix products, arithmetic and copies ran while one was open for 5% -> 3% of each run, Pallas kernels for 23% -> 10%
where the time goes in v5:
time: 211 us; the launch traced here: 210 us
  starting transfers between devices  55.2 us (26%)
  waiting for transfers between devices  41.3 us (20%)
  local copies, waits for them, and re-layouts  33.1 us (16%)
  blocking collectives  32.3 us (15%)
  Pallas kernels  30.3 us (14%)
  between operations  14.1 us (7%)
  other arithmetic  3.29 us (2%)
    all_to_all x1, blocking collectives, per_device(): slots = lax.all_to_all(slots, WIDE, 0, 0)  32.3 us
    unnamed x69, local copies, waits for them, and re-layouts  28.9 us
    all_to_all x1, waiting for transfers between devices, per_device(): quarter = lax.all_to_all(quarter, 'z', 0, 0)  25 us
    ppermute x12, starting transfers between devices, share(): lax.ppermute(total, 'x', ring(4, step))  18.6 us
    ppermute x12, waiting for transfers between devices, share(): lax.ppermute(total, 'x', ring(4, step))  9.5 us
    all_to_all x1, starting transfers between devices, per_device(): slab = lax.all_to_all(slab, WIDE, 0, 0)  8.59 us
    all_to_all x1, starting transfers between devices, per_device(): quarter = lax.all_to_all(quarter, 'z', 0, 0)  8.11 us
    all_to_all x1, starting transfers between devices, per_device(): columns = lax.all_to_all(columns, ('x', 'core'), 0, 0)  6.57 us
  transfers between devices with their start and end apart: 28, of which 13 were waited for; matrix products, arithmetic and copies ran while one was open for 3% of the time, Pallas kernels for 10%

profile of v5, /device:TPU:1, one launch (start us, length us, event | category | flops | bytes accessed | tf_op | source)
XLA Modules:
  0.0 209.5 jit_solution(9392779187468082868)
XLA Ops:
  10.4 3.4 %copy-done = f32[32,16,4096]{2,1,0:T(8,128)S(1)} copy-done((f32[32,16,4096]{2,1,0:T(8,128)S(1)}, f32[32,16,4096]{2,1,0:T(8,128)}, u32[]{:S(2)}) %copy-start) | copy-done | bytes 8388632
  14.6 6.6 %all-to-all-start = ((f32[8,64,128]{2,1,0:T(8,128)}), f32[8,64,128]{2,1,0:T(8,128)S(1)}, u32[]{:S(2)}, u32[]{:S(2)}) async-start(f32[8,64,128]{2,1,0:T(8,128)} %get-tuple-element.69), calls=%async_computation | async-start | bytes 524288 | tf_op jit(solution)/shard_map/all_to_all | solution.py:430
  21.8 2.6 %collective-permute-start.1 = (f32[64,128]{1,0:T(8,128)S(1)}, f32[64,128]{1,0:T(8,128)S(1)}, u32[]{:S(2)}, u32[]{:S(2)}) collective-permute-start(f32[64,128]{1,0:T(8,128)S(1)} %get-tuple-element.70.refs_0_), channel_id=1, source_target_pairs={{0,2},{1,3},{2,0},{3,1},{4,6},{5,7},{6,4},{7,5},{8,10},{9,11},{10,... | collective-permute-start | bytes 98312 | tf_op jit(solution)/shard_map/ppermute | solution.py:444
  29.6 8.1 %all-to-all-start.1 = ((f32[8,272,128]{2,1,0:T(8,128)}), f32[8,272,128]{2,1,0:T(8,128)S(1)}, u32[]{:S(2)}, u32[]{:S(2)}) async-start(f32[8,272,128]{2,1,0:T(8,128)} %copy-done.8), calls=%async_computation.1 | async-start | bytes 2228224 | tf_op jit(solution)/shard_map/all_to_all | solution.py:458
  37.8 2.2 %reshape.57.noise_ref = f32[128,1024]{1,0:T(8,128)} reshape(f32[16,4,2,1024]{3,2,1,0:T(2,128)} %param.16) | data formatting | bytes 1048576 | tf_op jit(solution)/shard_map/reshape | solution.py:469
  42.6 1.9 noise.1
  46.4 25.0 %all-to-all-done.1.slab_ref.inverse_ref.extra_ref = f32[8,272,128]{2,1,0:T(8,128)S(1)} async-done(((f32[8,272,128]{2,1,0:T(8,128)}), f32[8,272,128]{2,1,0:T(8,128)S(1)}, u32[]{:S(2)}, u32[]{:S(2)}) %all-to-all-start.1) | async-done | bytes 1114144 | tf_op jit(solution)/shard_map/all_to_all | solution.py:458
  71.3 8.6 %all-to-all-start.2 = ((f32[64,16,128]{2,1,0:T(8,128)}), f32[64,16,128]{2,1,0:T(8,128)}, u32[]{:S(2)}, u32[]{:S(2)}) async-start(f32[64,16,128]{2,1,0:T(8,128)} %copy-done.12), calls=%async_computation.2 | async-start | bytes 1048576 | tf_op jit(solution)/shard_map/all_to_all | solution.py:482
  80.6 3.0 %collective-permute-start.8 = (f32[8,96,128]{2,1,0:T(8,128)S(1)}, f32[8,96,128]{2,1,0:T(8,128)S(1)}, u32[]{:S(2)}, u32[]{:S(2)}) collective-permute-start(f32[8,96,128]{2,1,0:T(8,128)S(1)} %slice.19.refs_0_.refs_1_), channel_id=1, source_target_pairs={{0,2},{1,3},{2,0},{3,1},{4,6},{5,7},{6,4},{7,5},{8,10},{9,11},{10,... | collective-permute-start | bytes 1179656 | tf_op jit(solution)/shard_map/ppermute | solution.py:481
  88.7 2.4 %collective-permute-start.5 = (f32[24,1024]{1,0:T(8,128)}, f32[24,1024]{1,0:T(8,128)}, u32[]{:S(2)}, u32[]{:S(2)}) collective-permute-start(f32[24,1024]{1,0:T(8,128)} %add.108.a_ref), channel_id=1, source_target_pairs={{0,16},{8,24},{16,0},{24,8},{1,17},{9,25},{17,1},{25,9},{2,18},{10... | collective-permute-start | bytes 294920 | tf_op jit(solution)/shard_map/ppermute | solution.py:372
  91.1 2.7 %collective-permute-done.4.b_ref = f32[24,1024]{1,0:T(8,128)S(1)} collective-permute-done((f32[24,1024]{1,0:T(8,128)}, f32[24,1024]{1,0:T(8,128)S(1)}, u32[]{:S(2)}, u32[]{:S(2)}) %collective-permute-start.4) | collective-permute-done | bytes 98336 | tf_op jit(solution)/shard_map/ppermute | solution.py:372
  97.3 2.4 %spectrum.1 = (f32[1024,128]{1,0:T(8,128)S(1)}, f32[512,128]{1,0:T(8,128)S(1)}) custom-call(s32[2]{0:T(128)S(1)} %copy-done.31, f32[1024,32]{1,0:T(8,128)S(1)} %copy.15.spectrum_ref, f32[8,272,128]{2,1,0:T(8,128)S(1)} %all-to-all-done.1.slab_ref.inverse_ref.extra_ref), custom_call_target="tpu_custom_call" | custom-call | flops 300000000 | bytes 1500000 | tf_op jit(solution)/shard_map/spectrum/pallas_call | solution.py:515
  101.3 1.7 all-to-all-done.2.refs_3_
  110.5 2.5 %collective-permute-start.12 = (f32[24,1024]{1,0:T(8,128)S(1)}, f32[24,1024]{1,0:T(8,128)S(1)}, u32[]{:S(2)}, u32[]{:S(2)}) collective-permute-start(f32[24,1024]{1,0:T(8,128)S(1)} %add.109.a_ref), channel_id=1, source_target_pairs={{0,16},{8,24},{16,0},{24,8},{1,17},{9,25},{17,1},{25,9},{2,18},{10... | collective-permute-start | bytes 294920 | tf_op jit(solution)/shard_map/ppermute | solution.py:372
  114.1 2.4 %wait1.1 = (f32[1024,128]{1,0:T(8,128)S(1)}, f32[1,24,128]{2,1,0:T(8,128)S(1)}) custom-call(s32[1,4096]{1,0:T(1,128)S(1)} %bitcast.20, f32[16,4096]{1,0:T(8,128)S(1)} %fusion.3.refs_1_.wave_ref, f32[2,4096]{1,0:T(2,128)S(1)} %add_convert_fusion.refs_2_.plane_ref, f32[64,16,128]{2,1,0:T(8,128)} %all-to-all-done.2.refs_3_, ...), custom_call_target="tpu_custom_call" | custom-call | flops 536870912 | bytes 1500000 | tf_op jit(solution)/shard_map/wait1/pallas_call | solution.py:549
  123.7 2.2 %collective-permute-start.16 = (f32[24,1024]{1,0:T(8,128)S(1)}, f32[24,1024]{1,0:T(8,128)S(1)}, u32[]{:S(2)}, u32[]{:S(2)}) collective-permute-start(f32[24,1024]{1,0:T(8,128)S(1)} %add.110.a_ref), channel_id=1, source_target_pairs={{0,16},{8,24},{16,0},{24,8},{1,17},{9,25},{17,1},{25,9},{2,18},{10... | collective-permute-start | bytes 294920 | tf_op jit(solution)/shard_map/ppermute | solution.py:372
  128.1 2.4 %collective-permute-done.16.c_ref = f32[24,1024]{1,0:T(8,128)S(1)} collective-permute-done((f32[24,1024]{1,0:T(8,128)S(1)}, f32[24,1024]{1,0:T(8,128)S(1)}, u32[]{:S(2)}, u32[]{:S(2)}) %collective-permute-start.16) | collective-permute-done | bytes 98336 | tf_op jit(solution)/shard_map/ppermute | solution.py:372
  135.4 2.2 %collective-permute-start.20 = (f32[24,1024]{1,0:T(8,128)S(1)}, f32[24,1024]{1,0:T(8,128)S(1)}, u32[]{:S(2)}, u32[]{:S(2)}) collective-permute-start(f32[24,1024]{1,0:T(8,128)S(1)} %add.111.a_ref), channel_id=1, source_target_pairs={{0,16},{8,24},{16,0},{24,8},{1,17},{9,25},{17,1},{25,9},{2,18},{10... | collective-permute-start | bytes 294920 | tf_op jit(solution)/shard_map/ppermute | solution.py:372
  139.2 3.0 %collective-permute-done.20.c_ref = f32[24,1024]{1,0:T(8,128)S(1)} collective-permute-done((f32[24,1024]{1,0:T(8,128)S(1)}, f32[24,1024]{1,0:T(8,128)S(1)}, u32[]{:S(2)}, u32[]{:S(2)}) %collective-permute-start.20) | collective-permute-done | bytes 98336 | tf_op jit(solution)/shard_map/ppermute | solution.py:372
  150.8 5.8 %filter.1 = f32[64,16,128]{2,1,0:T(8,128)S(1)} custom-call(f32[1024,128]{1,0:T(8,128)S(1)} %copy-done.23, s32[1,4096]{1,0:T(1,128)S(1)} %bitcast.23, f32[16,4096]{1,0:T(8,128)S(1)} %fusion.3.refs_1_.wave_ref, f32[2,4096]{1,0:T(2,128)S(1)} %add_convert_fusion.refs_2_.plane_ref, f32[24,1024]{1,0:T(8,128)S(1)} %add.111.a_ref, ...), custom_call_target="tpu_custom_call" | custom-call | flops 2147483648 | bytes 11000000 | tf_op jit(solution)/shard_map/filter/pallas_call | solution.py:569
  156.6 32.3 %all_to_all.20.slots_ref = f32[64,16,128]{2,1,0:T(8,128)S(1)} all-to-all(f32[64,16,128]{2,1,0:T(8,128)S(1)} %filter.1), channel_id=1, replica_groups=mesh['z'=8,'x'=4,'core'=2,'y'=4] {'z','x','core'}, dimensions={0} | all-to-all | bytes 1048576 | tf_op jit(solution)/shard_map/all_to_all | solution.py:585
  188.9 3.1 %close.1 = f32[16,4,2,1024]{3,2,1,0:T(2,128)} custom-call(f32[64,16,128]{2,1,0:T(8,128)S(1)} %all_to_all.20.slots_ref, bf16[1024,1024]{1,0:T(8,128)(2,1)S(1)} %copy-done.5, bf16[1024,1024]{1,0:T(8,128)(2,1)S(1)} %copy-done.7), custom_call_target="tpu_custom_call" | custom-call | flops 805306368 | bytes 5500000 | tf_op jit(solution)/shard_map/close/pallas_call | solution.py:586
  192.0 3.4 %copy-done.1 = f32[32,16,4096]{2,1,0:T(8,128)S(1)} copy-done((f32[32,16,4096]{2,1,0:T(8,128)S(1)}, f32[32,16,4096]{2,1,0:T(8,128)}, u32[]{:S(2)}) %copy-start.1) | copy-done | bytes 8388632
  196.9 6.1 %update.1 = f32[32,16,128]{2,1,0:T(8,128)} custom-call(s32[2]{0:T(128)S(1)} %copy-done.32, f32[32,16,128]{2,1,0:T(8,128)S(1)} %copy-done.19, f32[8,64,1024]{2,1,0:T(8,128)S(1)} %bitcast.19, f32[32,16,4096]{2,1,0:T(8,128)S(1)} %copy-done.1, f32[32,16,4096]{2,1,0:T(8,128)S(1)} %copy-done.1, f32[32,16,4096]{2,1,0:T(8,128)S(1)} %copy-done.1, ...), custom_call_target="tpu_custom_call" | custom-call | flops 1610612736 | bytes 11000000 | tf_op jit(solution)/shard_map/update/pallas_call | solution.py:384
  (140 shorter events, 59.8 us)
Async XLA Ops:
  7.2 95.9 %all-gather.7.cloned.1.call-start = ((), (), s32[]{:S(2)}) async-start(), calls=%async_computation.4 | async-start | bytes 1179648 | tf_op jit(solution)/shard_map/all_gather | solution.py:442
  14.6 13.1 %all-to-all-start = ((f32[8,64,128]{2,1,0:T(8,128)}), f32[8,64,128]{2,1,0:T(8,128)S(1)}, u32[]{:S(2)}, u32[]{:S(2)}) async-start(f32[8,64,128]{2,1,0:T(8,128)} %get-tuple-element.69), calls=%async_computation | async-start | bytes 524288 | tf_op jit(solution)/shard_map/all_to_all | solution.py:430
  21.1 96.5 %all-gather.9.cloned.1.call-start = ((), (), s32[]{:S(2)}) async-start(), calls=%async_computation.5 | async-start | bytes 2359296 | tf_op jit(solution)/shard_map/all_gather | solution.py:457
  21.1 5.3 %collective-permute-start = (f32[64,128]{1,0:T(8,128)S(1)}, f32[64,128]{1,0:T(8,128)S(1)}, u32[]{:S(2)}, u32[]{:S(2)}) collective-permute-start(f32[64,128]{1,0:T(8,128)S(1)} %get-tuple-element.70.refs_0_), channel_id=1, source_target_pairs={{0,1},{1,2},{2,3},{3,0},{4,5},{5,6},{6,7},{7,4},{8,9},{9,10},{10,1... | collective-permute-start | bytes 98312 | tf_op jit(solution)/shard_map/ppermute | solution.py:444
  21.8 4.7 %collective-permute-start.1 = (f32[64,128]{1,0:T(8,128)S(1)}, f32[64,128]{1,0:T(8,128)S(1)}, u32[]{:S(2)}, u32[]{:S(2)}) collective-permute-start(f32[64,128]{1,0:T(8,128)S(1)} %get-tuple-element.70.refs_0_), channel_id=1, source_target_pairs={{0,2},{1,3},{2,0},{3,1},{4,6},{5,7},{6,4},{7,5},{8,10},{9,11},{10,... | collective-permute-start | bytes 98312 | tf_op jit(solution)/shard_map/ppermute | solution.py:444
  24.4 3.1 %collective-permute-start.2 = (f32[64,128]{1,0:T(8,128)S(1)}, f32[64,128]{1,0:T(8,128)S(1)}, u32[]{:S(2)}, u32[]{:S(2)}) collective-permute-start(f32[64,128]{1,0:T(8,128)S(1)} %get-tuple-element.70.refs_0_), channel_id=1, source_target_pairs={{0,3},{1,0},{2,1},{3,2},{4,7},{5,4},{6,5},{7,6},{8,11},{9,8},{10,9... | collective-permute-start | bytes 98312 | tf_op jit(solution)/shard_map/ppermute | solution.py:444
  29.6 41.8 %all-to-all-start.1 = ((f32[8,272,128]{2,1,0:T(8,128)}), f32[8,272,128]{2,1,0:T(8,128)S(1)}, u32[]{:S(2)}, u32[]{:S(2)}) async-start(f32[8,272,128]{2,1,0:T(8,128)} %copy-done.8), calls=%async_computation.1 | async-start | bytes 2228224 | tf_op jit(solution)/shard_map/all_to_all | solution.py:458
  71.3 31.7 %all-to-all-start.2 = ((f32[64,16,128]{2,1,0:T(8,128)}), f32[64,16,128]{2,1,0:T(8,128)}, u32[]{:S(2)}, u32[]{:S(2)}) async-start(f32[64,16,128]{2,1,0:T(8,128)} %copy-done.12), calls=%async_computation.2 | async-start | bytes 1048576 | tf_op jit(solution)/shard_map/all_to_all | solution.py:482
  79.9 112.0 %all-gather.11.cloned.1.call-start = ((), (), s32[]{:S(2)}) async-start(), calls=%async_computation.6 | async-start | bytes 2359296 | tf_op jit(solution)/shard_map/all_gather | solution.py:584
  80.0 21.3 %collective-permute-start.7 = (f32[8,96,128]{2,1,0:T(8,128)S(1)}, f32[8,96,128]{2,1,0:T(8,128)S(1)}, u32[]{:S(2)}, u32[]{:S(2)}) collective-permute-start(f32[8,96,128]{2,1,0:T(8,128)S(1)} %slice.19.refs_0_.refs_1_), channel_id=1, source_target_pairs={{0,1},{1,2},{2,3},{3,0},{4,5},{5,6},{6,7},{7,4},{8,9},{9,10},{10,1... | collective-permute-start | bytes 1179656 | tf_op jit(solution)/shard_map/ppermute | solution.py:481
  80.6 20.7 %collective-permute-start.8 = (f32[8,96,128]{2,1,0:T(8,128)S(1)}, f32[8,96,128]{2,1,0:T(8,128)S(1)}, u32[]{:S(2)}, u32[]{:S(2)}) collective-permute-start(f32[8,96,128]{2,1,0:T(8,128)S(1)} %slice.19.refs_0_.refs_1_), channel_id=1, source_target_pairs={{0,2},{1,3},{2,0},{3,1},{4,6},{5,7},{6,4},{7,5},{8,10},{9,11},{10,... | collective-permute-start | bytes 1179656 | tf_op jit(solution)/shard_map/ppermute | solution.py:481
  83.6 17.7 %collective-permute-start.9 = (f32[8,96,128]{2,1,0:T(8,128)S(1)}, f32[8,96,128]{2,1,0:T(8,128)S(1)}, u32[]{:S(2)}, u32[]{:S(2)}) collective-permute-start(f32[8,96,128]{2,1,0:T(8,128)S(1)} %slice.19.refs_0_.refs_1_), channel_id=1, source_target_pairs={{0,3},{1,0},{2,1},{3,2},{4,7},{5,4},{6,5},{7,6},{8,11},{9,8},{10,9... | collective-permute-start | bytes 1179656 | tf_op jit(solution)/shard_map/ppermute | solution.py:481
  87.4 6.3 %collective-permute-start.4 = (f32[24,1024]{1,0:T(8,128)}, f32[24,1024]{1,0:T(8,128)S(1)}, u32[]{:S(2)}, u32[]{:S(2)}) collective-permute-start(f32[24,1024]{1,0:T(8,128)} %add.108.a_ref), channel_id=1, source_target_pairs={{0,8},{8,16},{16,24},{24,0},{1,9},{9,17},{17,25},{25,1},{2,10},{10... | collective-permute-start | bytes 294920 | tf_op jit(solution)/shard_map/ppermute | solution.py:372
  88.7 12.6 %collective-permute-start.5 = (f32[24,1024]{1,0:T(8,128)}, f32[24,1024]{1,0:T(8,128)}, u32[]{:S(2)}, u32[]{:S(2)}) collective-permute-start(f32[24,1024]{1,0:T(8,128)} %add.108.a_ref), channel_id=1, source_target_pairs={{0,16},{8,24},{16,0},{24,8},{1,17},{9,25},{17,1},{25,9},{2,18},{10... | collective-permute-start | bytes 294920 | tf_op jit(solution)/shard_map/ppermute | solution.py:372
  94.4 6.8 %collective-permute-start.6 = (f32[24,1024]{1,0:T(8,128)}, f32[24,1024]{1,0:T(8,128)}, u32[]{:S(2)}, u32[]{:S(2)}) collective-permute-start(f32[24,1024]{1,0:T(8,128)} %add.108.a_ref), channel_id=1, source_target_pairs={{0,24},{8,0},{16,8},{24,16},{1,25},{9,1},{17,9},{25,17},{2,26},{10... | collective-permute-start | bytes 294920 | tf_op jit(solution)/shard_map/ppermute | solution.py:372
  109.2 7.2 %collective-permute-start.11 = (f32[24,1024]{1,0:T(8,128)S(1)}, f32[24,1024]{1,0:T(8,128)S(1)}, u32[]{:S(2)}, u32[]{:S(2)}) collective-permute-start(f32[24,1024]{1,0:T(8,128)S(1)} %add.109.a_ref), channel_id=1, source_target_pairs={{0,8},{8,16},{16,24},{24,0},{1,9},{9,17},{17,25},{25,1},{2,10},{10... | collective-permute-start | bytes 294920 | tf_op jit(solution)/shard_map/ppermute | solution.py:372
  110.5 7.1 %collective-permute-start.12 = (f32[24,1024]{1,0:T(8,128)S(1)}, f32[24,1024]{1,0:T(8,128)S(1)}, u32[]{:S(2)}, u32[]{:S(2)}) collective-permute-start(f32[24,1024]{1,0:T(8,128)S(1)} %add.109.a_ref), channel_id=1, source_target_pairs={{0,16},{8,24},{16,0},{24,8},{1,17},{9,25},{17,1},{25,9},{2,18},{10... | collective-permute-start | bytes 294920 | tf_op jit(solution)/shard_map/ppermute | solution.py:372
  113.0 4.7 %collective-permute-start.13 = (f32[24,1024]{1,0:T(8,128)S(1)}, f32[24,1024]{1,0:T(8,128)S(1)}, u32[]{:S(2)}, u32[]{:S(2)}) collective-permute-start(f32[24,1024]{1,0:T(8,128)S(1)} %add.109.a_ref), channel_id=1, source_target_pairs={{0,24},{8,0},{16,8},{24,16},{1,25},{9,1},{17,9},{25,17},{2,26},{10... | collective-permute-start | bytes 294920 | tf_op jit(solution)/shard_map/ppermute | solution.py:372
  122.5 5.5 %collective-permute-start.15 = (f32[24,1024]{1,0:T(8,128)S(1)}, f32[24,1024]{1,0:T(8,128)S(1)}, u32[]{:S(2)}, u32[]{:S(2)}) collective-permute-start(f32[24,1024]{1,0:T(8,128)S(1)} %add.110.a_ref), channel_id=1, source_target_pairs={{0,8},{8,16},{16,24},{24,0},{1,9},{9,17},{17,25},{25,1},{2,10},{10... | collective-permute-start | bytes 294920 | tf_op jit(solution)/shard_map/ppermute | solution.py:372
  123.7 6.8 %collective-permute-start.16 = (f32[24,1024]{1,0:T(8,128)S(1)}, f32[24,1024]{1,0:T(8,128)S(1)}, u32[]{:S(2)}, u32[]{:S(2)}) collective-permute-start(f32[24,1024]{1,0:T(8,128)S(1)} %add.110.a_ref), channel_id=1, source_target_pairs={{0,16},{8,24},{16,0},{24,8},{1,17},{9,25},{17,1},{25,9},{2,18},{10... | collective-permute-start | bytes 294920 | tf_op jit(solution)/shard_map/ppermute | solution.py:372
  125.8 4.8 %collective-permute-start.17 = (f32[24,1024]{1,0:T(8,128)S(1)}, f32[24,1024]{1,0:T(8,128)S(1)}, u32[]{:S(2)}, u32[]{:S(2)}) collective-permute-start(f32[24,1024]{1,0:T(8,128)S(1)} %add.110.a_ref), channel_id=1, source_target_pairs={{0,24},{8,0},{16,8},{24,16},{1,25},{9,1},{17,9},{25,17},{2,26},{10... | collective-permute-start | bytes 294920 | tf_op jit(solution)/shard_map/ppermute | solution.py:372
  133.9 5.3 %collective-permute-start.19 = (f32[24,1024]{1,0:T(8,128)S(1)}, f32[24,1024]{1,0:T(8,128)S(1)}, u32[]{:S(2)}, u32[]{:S(2)}) collective-permute-start(f32[24,1024]{1,0:T(8,128)S(1)} %add.111.a_ref), channel_id=1, source_target_pairs={{0,8},{8,16},{16,24},{24,0},{1,9},{9,17},{17,25},{25,1},{2,10},{10... | collective-permute-start | bytes 294920 | tf_op jit(solution)/shard_map/ppermute | solution.py:372
  135.4 6.8 %collective-permute-start.20 = (f32[24,1024]{1,0:T(8,128)S(1)}, f32[24,1024]{1,0:T(8,128)S(1)}, u32[]{:S(2)}, u32[]{:S(2)}) collective-permute-start(f32[24,1024]{1,0:T(8,128)S(1)} %add.111.a_ref), channel_id=1, source_target_pairs={{0,16},{8,24},{16,0},{24,8},{1,17},{9,25},{17,1},{25,9},{2,18},{10... | collective-permute-start | bytes 294920 | tf_op jit(solution)/shard_map/ppermute | solution.py:372
  137.5 4.7 %collective-permute-start.21 = (f32[24,1024]{1,0:T(8,128)S(1)}, f32[24,1024]{1,0:T(8,128)S(1)}, u32[]{:S(2)}, u32[]{:S(2)}) collective-permute-start(f32[24,1024]{1,0:T(8,128)S(1)} %add.111.a_ref), channel_id=1, source_target_pairs={{0,24},{8,0},{16,8},{24,16},{1,25},{9,1},{17,9},{25,17},{2,26},{10... | collective-permute-start | bytes 294920 | tf_op jit(solution)/shard_map/ppermute | solution.py:372
  (38 other events, 188.1 us)
Sparse Core Ops, SparseCore 0:
  14.7 46.9 all-gather.6
  63.4 50.6 all-gather.8
  143.1 46.7 all-gather.10

commit v6 on v5

--- a/solution.py
+++ b/solution.py
@@ -16,7 +16,6 @@
 COLS = 24
 NN = (((1,), (0,)), ((), ()))
 NT = (((1,), (1,)), ((), ()))
-LIMIT = pltpu.CompilerParams(vmem_limit_bytes=40 * 1024 * 1024)
 
 
 def halves(table):
@@ -349,7 +348,9 @@
     return jax.ShapeDtypeStruct(shape, F32)
 
 
-def call(body, name, in_specs, out_specs, out_shape, flops, moved, scratch=(), grid=1):
+def call(
+    body, name, in_specs, out_specs, out_shape, flops, moved, scratch=(), grid=1, room=40
+):
     return pl.pallas_call(
         body,
         grid=(grid,),
@@ -357,7 +358,7 @@
         out_specs=out_specs,
         out_shape=out_shape,
         scratch_shapes=scratch,
-        compiler_params=LIMIT,
+        compiler_params=pltpu.CompilerParams(vmem_limit_bytes=room * 1024 * 1024),
         cost_estimate=cost(flops, moved),
         name=name,
     )
@@ -399,6 +400,7 @@
         11_000_000,
         [pltpu.VMEM((4, 256, LENGTH), BF16)],
         grid=4,
+        room=56,
     )(index, base, unknowns, *[factor] * 4)
 
 
@@ -541,6 +543,7 @@
             40_000_000,
             1_500_000,
             inverse_scratch,
+            room=56 if panel == 1 else 40,
         )(index, work, *parts, factor_rows(panel, panel - 1), *[own[at] for at in inverses], *unknowns * (panel == 3))
         unknowns.append(unknown)
         parts = share(partial)
@@ -579,6 +582,7 @@
         8 * 2 * 128 * LENGTH * LENGTH,
         11_000_000,
         [TABLE] * 4 + [pltpu.SemaphoreType.DMA((4,))],
+        room=56,
     )(pencil, cell_x, waves, planes, *parts, x_high, x_low, back_high, back_low, even, odd)
     late = (parts[0][:16] + parts[1][:16]) + (parts[2][:16] + parts[3][:16])
     late = lax.all_gather(jnp.concatenate([solved_rows[0], late]), "z")

time: 211 us -> 207 us (0.981)
  local copies, waits for them, and re-layouts: 33.1 us -> 18.8 us
  Pallas kernels: 30.3 us -> 36.5 us
    unnamed x69 -> x79, local copies, waits for them, and re-layouts: 28.9 us -> 14.6 us
    pallas_call x1, Pallas kernels: 5.78 us -> 8.77 us  [per_device(): call(filter_kernel, 'filter', [spec(LENGTH, 128)] + obs_specs(3) + [panel...]
    all_gather x1, waiting for transfers between devices: 0.01 us -> 2.68 us  [per_device(): late = lax.all_gather(jnp.concatenate([solved_rows[0], late]), 'z')]
    pallas_call x1, Pallas kernels: 6.05 us -> 8.24 us  [update(): call(update_kernel, 'update', [SMEM, pl.BlockSpec((8, 16, 128), lambda i:...]
  transfers between devices with their start and end apart: 28 -> 28, of which waited for: 13 -> 15; matrix products, arithmetic and copies ran while one was open for 3% -> 3% of each run, Pallas kernels for 10% -> 12%
where the time goes in v6:
time: 207 us; the launch traced here: 205 us
  starting transfers between devices  55.3 us (27%)
  waiting for transfers between devices  43.4 us (21%)
  Pallas kernels  36.5 us (18%)
  blocking collectives  32.8 us (16%)
  local copies, waits for them, and re-layouts  18.8 us (9%)
  between operations  14.2 us (7%)
  other arithmetic  3.55 us (2%)
    all_to_all x1, blocking collectives, per_device(): slots = lax.all_to_all(slots, WIDE, 0, 0)  32.8 us
    all_to_all x1, waiting for transfers between devices, per_device(): quarter = lax.all_to_all(quarter, 'z', 0, 0)  24.9 us
    ppermute x12, starting transfers between devices, share(): lax.ppermute(total, 'x', ring(4, step))  18.7 us
    unnamed x79, local copies, waits for them, and re-layouts  14.6 us
    pallas_call x1, Pallas kernels, per_device(): call(filter_kernel, 'filter', [spec(LENGTH, 128)] + obs_specs(3) + [panel...  8.77 us
    all_to_all x1, starting transfers between devices, per_device(): slab = lax.all_to_all(slab, WIDE, 0, 0)  8.56 us
    pallas_call x1, Pallas kernels, update(): call(update_kernel, 'update', [SMEM, pl.BlockSpec((8, 16, 128), lambda i:...  8.24 us
    all_to_all x1, starting transfers between devices, per_device(): quarter = lax.all_to_all(quarter, 'z', 0, 0)  8.11 us
  transfers between devices with their start and end apart: 28, of which 15 were waited for; matrix products, arithmetic and copies ran while one was open for 3% of the time, Pallas kernels for 12%

profile of v6, /device:TPU:1, one launch (start us, length us, event | category | flops | bytes accessed | tf_op | source)
XLA Modules:
  0.0 204.5 jit_solution(15796659485748560525)
XLA Ops:
  10.4 3.4 %copy-done = f32[32,16,4096]{2,1,0:T(8,128)S(1)} copy-done((f32[32,16,4096]{2,1,0:T(8,128)S(1)}, f32[32,16,4096]{2,1,0:T(8,128)}, u32[]{:S(2)}) %copy-start) | copy-done | bytes 8388632
  14.5 6.6 %all-to-all-start = ((f32[8,64,128]{2,1,0:T(8,128)}), f32[8,64,128]{2,1,0:T(8,128)S(1)}, u32[]{:S(2)}, u32[]{:S(2)}) async-start(f32[8,64,128]{2,1,0:T(8,128)} %get-tuple-element.69), calls=%async_computation | async-start | bytes 524288 | tf_op jit(solution)/shard_map/all_to_all | solution.py:432
  21.7 2.6 %collective-permute-start.1 = (f32[64,128]{1,0:T(8,128)S(1)}, f32[64,128]{1,0:T(8,128)S(1)}, u32[]{:S(2)}, u32[]{:S(2)}) collective-permute-start(f32[64,128]{1,0:T(8,128)S(1)} %get-tuple-element.70.refs_0_), channel_id=1, source_target_pairs={{0,2},{1,3},{2,0},{3,1},{4,6},{5,7},{6,4},{7,5},{8,10},{9,11},{10,... | collective-permute-start | bytes 98312 | tf_op jit(solution)/shard_map/ppermute | solution.py:446
  29.5 8.1 %all-to-all-start.1 = ((f32[8,272,128]{2,1,0:T(8,128)}), f32[8,272,128]{2,1,0:T(8,128)S(1)}, u32[]{:S(2)}, u32[]{:S(2)}) async-start(f32[8,272,128]{2,1,0:T(8,128)} %copy-done.15), calls=%async_computation.1 | async-start | bytes 2228224 | tf_op jit(solution)/shard_map/all_to_all | solution.py:460
  37.8 2.2 %reshape.57.noise_ref = f32[128,1024]{1,0:T(8,128)} reshape(f32[16,4,2,1024]{3,2,1,0:T(2,128)} %param.16) | data formatting | bytes 1048576 | tf_op jit(solution)/shard_map/reshape | solution.py:471
  46.4 24.9 %all-to-all-done.1.slab_ref.inverse_ref.extra_ref = f32[8,272,128]{2,1,0:T(8,128)S(1)} async-done(((f32[8,272,128]{2,1,0:T(8,128)}), f32[8,272,128]{2,1,0:T(8,128)S(1)}, u32[]{:S(2)}, u32[]{:S(2)}) %all-to-all-start.1) | async-done | bytes 1114144 | tf_op jit(solution)/shard_map/all_to_all | solution.py:460
  71.3 8.6 %all-to-all-start.2 = ((f32[64,16,128]{2,1,0:T(8,128)}), f32[64,16,128]{2,1,0:T(8,128)}, u32[]{:S(2)}, u32[]{:S(2)}) async-start(f32[64,16,128]{2,1,0:T(8,128)} %copy-done.18), calls=%async_computation.2 | async-start | bytes 1048576 | tf_op jit(solution)/shard_map/all_to_all | solution.py:484
  80.6 3.0 %collective-permute-start.8 = (f32[8,96,128]{2,1,0:T(8,128)S(1)}, f32[8,96,128]{2,1,0:T(8,128)S(1)}, u32[]{:S(2)}, u32[]{:S(2)}) collective-permute-start(f32[8,96,128]{2,1,0:T(8,128)S(1)} %slice.19.refs_0_.refs_1_), channel_id=1, source_target_pairs={{0,2},{1,3},{2,0},{3,1},{4,6},{5,7},{6,4},{7,5},{8,10},{9,11},{10,... | collective-permute-start | bytes 1179656 | tf_op jit(solution)/shard_map/ppermute | solution.py:483
  88.7 2.4 %collective-permute-start.5 = (f32[24,1024]{1,0:T(8,128)}, f32[24,1024]{1,0:T(8,128)}, u32[]{:S(2)}, u32[]{:S(2)}) collective-permute-start(f32[24,1024]{1,0:T(8,128)} %add.108.a_ref), channel_id=1, source_target_pairs={{0,16},{8,24},{16,0},{24,8},{1,17},{9,25},{17,1},{25,9},{2,18},{10... | collective-permute-start | bytes 294920 | tf_op jit(solution)/shard_map/ppermute | solution.py:373
  91.1 2.8 %collective-permute-done.4.b_ref = f32[24,1024]{1,0:T(8,128)S(1)} collective-permute-done((f32[24,1024]{1,0:T(8,128)}, f32[24,1024]{1,0:T(8,128)S(1)}, u32[]{:S(2)}, u32[]{:S(2)}) %collective-permute-start.4) | collective-permute-done | bytes 98336 | tf_op jit(solution)/shard_map/ppermute | solution.py:373
  96.2 2.4 %spectrum.1 = (f32[1024,128]{1,0:T(8,128)S(1)}, f32[512,128]{1,0:T(8,128)S(1)}) custom-call(s32[2]{0:T(128)S(1)} %pad_add_fusion.index_ref, f32[1024,32]{1,0:T(8,128)S(1)} %copy.15.spectrum_ref, f32[8,272,128]{2,1,0:T(8,128)S(1)} %all-to-all-done.1.slab_ref.inverse_ref.extra_ref), custom_call_target="tpu_custom_call" | custom-call | flops 300000000 | bytes 1500000 | tf_op jit(solution)/shard_map/spectrum/pallas_call | solution.py:517
  100.8 2.1 %all-to-all-done.2.refs_3_ = f32[64,16,128]{2,1,0:T(8,128)} async-done(((f32[64,16,128]{2,1,0:T(8,128)}), f32[64,16,128]{2,1,0:T(8,128)}, u32[]{:S(2)}, u32[]{:S(2)}) %all-to-all-start.2) | async-done | bytes 524320 | tf_op jit(solution)/shard_map/all_to_all | solution.py:484
  103.0 2.6 %step1.1 = (f32[24,1024]{1,0:T(8,128)}, f32[24,1024]{1,0:T(8,128)}) custom-call(s32[2]{0:T(128)} %copy-done.31, f32[4,24,128]{2,1,0:T(8,128)} %copy-done.26, f32[24,1024]{1,0:T(8,128)} %add.108.a_ref, f32[24,1024]{1,0:T(8,128)} %copy-done.37, f32[24,1024]{1,0:T(8,128)} %collective-permute-done.5.c_ref, f32[24,1024]{1,0:T(8,128)} %collective-permute-done.6.d_ref, ...), custom_call_target="tpu_custom_call" | custom-call | flops 40000000 | bytes 1500000 | tf_op jit(solution)/shard_map/step1/pallas_call | solution.py:533
  110.0 2.4 %collective-permute-start.12 = (f32[24,1024]{1,0:T(8,128)S(1)}, f32[24,1024]{1,0:T(8,128)S(1)}, u32[]{:S(2)}, u32[]{:S(2)}) collective-permute-start(f32[24,1024]{1,0:T(8,128)S(1)} %add.109.a_ref), channel_id=1, source_target_pairs={{0,16},{8,24},{16,0},{24,8},{1,17},{9,25},{17,1},{25,9},{2,18},{10... | collective-permute-start | bytes 294920 | tf_op jit(solution)/shard_map/ppermute | solution.py:373
  114.4 2.4 %wait1.1 = (f32[1024,128]{1,0:T(8,128)S(1)}, f32[1,24,128]{2,1,0:T(8,128)S(1)}) custom-call(s32[1,4096]{1,0:T(1,128)S(1)} %bitcast.19, f32[16,4096]{1,0:T(8,128)S(1)} %fusion.3.refs_1_.wave_ref, f32[2,4096]{1,0:T(2,128)S(1)} %add_convert_fusion.refs_2_.plane_ref, f32[64,16,128]{2,1,0:T(8,128)} %all-to-all-done.2.refs_3_, f32[24,1024]{1,0:T(8,128)S(1)} %copy-done.21, ...), custom_call_target="tpu_custom_call" | custom-call | flops 536870912 | bytes 1500000 | tf_op jit(solution)/shard_map/wait1/pallas_call | solution.py:552
  123.1 2.2 %collective-permute-start.16 = (f32[24,1024]{1,0:T(8,128)S(1)}, f32[24,1024]{1,0:T(8,128)S(1)}, u32[]{:S(2)}, u32[]{:S(2)}) collective-permute-start(f32[24,1024]{1,0:T(8,128)S(1)} %add.110.a_ref), channel_id=1, source_target_pairs={{0,16},{8,24},{16,0},{24,8},{1,17},{9,25},{17,1},{25,9},{2,18},{10... | collective-permute-start | bytes 294920 | tf_op jit(solution)/shard_map/ppermute | solution.py:373
  127.6 2.4 %collective-permute-done.16.c_ref = f32[24,1024]{1,0:T(8,128)S(1)} collective-permute-done((f32[24,1024]{1,0:T(8,128)S(1)}, f32[24,1024]{1,0:T(8,128)S(1)}, u32[]{:S(2)}, u32[]{:S(2)}) %collective-permute-start.16) | collective-permute-done | bytes 98336 | tf_op jit(solution)/shard_map/ppermute | solution.py:373
  134.8 2.2 %collective-permute-start.20 = (f32[24,1024]{1,0:T(8,128)S(1)}, f32[24,1024]{1,0:T(8,128)S(1)}, u32[]{:S(2)}, u32[]{:S(2)}) collective-permute-start(f32[24,1024]{1,0:T(8,128)S(1)} %add.111.a_ref), channel_id=1, source_target_pairs={{0,16},{8,24},{16,0},{24,8},{1,17},{9,25},{17,1},{25,9},{2,18},{10... | collective-permute-start | bytes 294920 | tf_op jit(solution)/shard_map/ppermute | solution.py:373
  139.4 2.2 %collective-permute-done.20.c_ref = f32[24,1024]{1,0:T(8,128)S(1)} collective-permute-done((f32[24,1024]{1,0:T(8,128)S(1)}, f32[24,1024]{1,0:T(8,128)S(1)}, u32[]{:S(2)}, u32[]{:S(2)}) %collective-permute-start.20) | collective-permute-done | bytes 98336 | tf_op jit(solution)/shard_map/ppermute | solution.py:373
  142.4 8.8 %filter.1 = f32[64,16,128]{2,1,0:T(8,128)} custom-call(f32[1024,128]{1,0:T(8,128)} %copy-done.25, s32[1,4096]{1,0:T(1,128)} %bitcast.22, f32[16,4096]{1,0:T(8,128)} %copy-done.17, f32[2,4096]{1,0:T(2,128)} %copy-done.23, f32[24,1024]{1,0:T(8,128)} %copy-done.33, f32[24,1024]{1,0:T(8,128)} %copy-done.34, f32[24,1024]{1,0:T(8,128)} %copy-done.35, ...), custom_call_target="tpu_custom_call" | custom-call | flops 2147483648 | bytes 11000000 | tf_op jit(solution)/shard_map/filter/pallas_call | solution.py:572
  151.2 32.8 %all_to_all.20.slots_ref = f32[64,16,128]{2,1,0:T(8,128)S(1)} all-to-all(f32[64,16,128]{2,1,0:T(8,128)} %filter.1), channel_id=1, replica_groups=mesh['z'=8,'x'=4,'core'=2,'y'=4] {'z','x','core'}, dimensions={0} | all-to-all | bytes 1048576 | tf_op jit(solution)/shard_map/all_to_all | solution.py:589
  184.0 3.1 %close.1 = f32[16,4,2,1024]{3,2,1,0:T(2,128)} custom-call(f32[64,16,128]{2,1,0:T(8,128)S(1)} %all_to_all.20.slots_ref, bf16[1024,1024]{1,0:T(8,128)(2,1)S(1)} %copy-done.12, bf16[1024,1024]{1,0:T(8,128)(2,1)S(1)} %copy-done.14), custom_call_target="tpu_custom_call" | custom-call | flops 805306368 | bytes 5500000 | tf_op jit(solution)/shard_map/close/pallas_call | solution.py:590
  187.1 2.7 %all-gather.11.cloned.1.call-done = f32[512,1024]{1,0:T(8,128)} async-done(((f32[64,1024]{1,0:T(8,128)}), f32[512,1024]{1,0:T(8,128)}) %all-gather.11.cloned.1.call-update) | async-done | bytes 2097168 | tf_op jit(solution)/shard_map/all_gather | solution.py:588
  189.8 8.2 %update.1 = f32[32,16,128]{2,1,0:T(8,128)} custom-call(s32[2]{0:T(128)} %copy-done.31, f32[32,16,128]{2,1,0:T(8,128)} %base_ref, f32[8,64,1024]{2,1,0:T(8,128)} %bitcast.24, f32[32,16,4096]{2,1,0:T(8,128)} %refs_3_, f32[32,16,4096]{2,1,0:T(8,128)} %refs_3_, f32[32,16,4096]{2,1,0:T(8,128)} %refs_3_, f32[32,16,4096]{2,1,0:T(8,128)} %refs_3_), custom_call_target="tpu_custom_call" | custom-call | flops 1610612736 | bytes 11000000 | tf_op jit(solution)/shard_map/update/pallas_call | solution.py:385
  (150 shorter events, 49.4 us)
Async XLA Ops:
  7.2 95.8 %all-gather.7.cloned.1.call-start = ((), (), s32[]{:S(2)}) async-start(), calls=%async_computation.4 | async-start | bytes 1179648 | tf_op jit(solution)/shard_map/all_gather | solution.py:444
  14.5 13.1 %all-to-all-start = ((f32[8,64,128]{2,1,0:T(8,128)}), f32[8,64,128]{2,1,0:T(8,128)S(1)}, u32[]{:S(2)}, u32[]{:S(2)}) async-start(f32[8,64,128]{2,1,0:T(8,128)} %get-tuple-element.69), calls=%async_computation | async-start | bytes 524288 | tf_op jit(solution)/shard_map/all_to_all | solution.py:432
  21.1 95.9 %all-gather.9.cloned.1.call-start = ((), (), s32[]{:S(2)}) async-start(), calls=%async_computation.5 | async-start | bytes 2359296 | tf_op jit(solution)/shard_map/all_gather | solution.py:459
  21.1 5.3 %collective-permute-start = (f32[64,128]{1,0:T(8,128)S(1)}, f32[64,128]{1,0:T(8,128)S(1)}, u32[]{:S(2)}, u32[]{:S(2)}) collective-permute-start(f32[64,128]{1,0:T(8,128)S(1)} %get-tuple-element.70.refs_0_), channel_id=1, source_target_pairs={{0,1},{1,2},{2,3},{3,0},{4,5},{5,6},{6,7},{7,4},{8,9},{9,10},{10,1... | collective-permute-start | bytes 98312 | tf_op jit(solution)/shard_map/ppermute | solution.py:446
  21.7 4.7 %collective-permute-start.1 = (f32[64,128]{1,0:T(8,128)S(1)}, f32[64,128]{1,0:T(8,128)S(1)}, u32[]{:S(2)}, u32[]{:S(2)}) collective-permute-start(f32[64,128]{1,0:T(8,128)S(1)} %get-tuple-element.70.refs_0_), channel_id=1, source_target_pairs={{0,2},{1,3},{2,0},{3,1},{4,6},{5,7},{6,4},{7,5},{8,10},{9,11},{10,... | collective-permute-start | bytes 98312 | tf_op jit(solution)/shard_map/ppermute | solution.py:446
  24.4 3.1 %collective-permute-start.2 = (f32[64,128]{1,0:T(8,128)S(1)}, f32[64,128]{1,0:T(8,128)S(1)}, u32[]{:S(2)}, u32[]{:S(2)}) collective-permute-start(f32[64,128]{1,0:T(8,128)S(1)} %get-tuple-element.70.refs_0_), channel_id=1, source_target_pairs={{0,3},{1,0},{2,1},{3,2},{4,7},{5,4},{6,5},{7,6},{8,11},{9,8},{10,9... | collective-permute-start | bytes 98312 | tf_op jit(solution)/shard_map/ppermute | solution.py:446
  29.5 41.8 %all-to-all-start.1 = ((f32[8,272,128]{2,1,0:T(8,128)}), f32[8,272,128]{2,1,0:T(8,128)S(1)}, u32[]{:S(2)}, u32[]{:S(2)}) async-start(f32[8,272,128]{2,1,0:T(8,128)} %copy-done.15), calls=%async_computation.1 | async-start | bytes 2228224 | tf_op jit(solution)/shard_map/all_to_all | solution.py:460
  71.3 31.6 %all-to-all-start.2 = ((f32[64,16,128]{2,1,0:T(8,128)}), f32[64,16,128]{2,1,0:T(8,128)}, u32[]{:S(2)}, u32[]{:S(2)}) async-start(f32[64,16,128]{2,1,0:T(8,128)} %copy-done.18), calls=%async_computation.2 | async-start | bytes 1048576 | tf_op jit(solution)/shard_map/all_to_all | solution.py:484
  79.9 109.9 %all-gather.11.cloned.1.call-start = ((), (), s32[]{:S(2)}) async-start(), calls=%async_computation.6 | async-start | bytes 2359296 | tf_op jit(solution)/shard_map/all_gather | solution.py:588
  80.0 20.1 %collective-permute-start.7 = (f32[8,96,128]{2,1,0:T(8,128)S(1)}, f32[8,96,128]{2,1,0:T(8,128)S(1)}, u32[]{:S(2)}, u32[]{:S(2)}) collective-permute-start(f32[8,96,128]{2,1,0:T(8,128)S(1)} %slice.19.refs_0_.refs_1_), channel_id=1, source_target_pairs={{0,1},{1,2},{2,3},{3,0},{4,5},{5,6},{6,7},{7,4},{8,9},{9,10},{10,1... | collective-permute-start | bytes 1179656 | tf_op jit(solution)/shard_map/ppermute | solution.py:483
  80.6 20.2 %collective-permute-start.8 = (f32[8,96,128]{2,1,0:T(8,128)S(1)}, f32[8,96,128]{2,1,0:T(8,128)S(1)}, u32[]{:S(2)}, u32[]{:S(2)}) collective-permute-start(f32[8,96,128]{2,1,0:T(8,128)S(1)} %slice.19.refs_0_.refs_1_), channel_id=1, source_target_pairs={{0,2},{1,3},{2,0},{3,1},{4,6},{5,7},{6,4},{7,5},{8,10},{9,11},{10,... | collective-permute-start | bytes 1179656 | tf_op jit(solution)/shard_map/ppermute | solution.py:483
  83.6 17.2 %collective-permute-start.9 = (f32[8,96,128]{2,1,0:T(8,128)S(1)}, f32[8,96,128]{2,1,0:T(8,128)S(1)}, u32[]{:S(2)}, u32[]{:S(2)}) collective-permute-start(f32[8,96,128]{2,1,0:T(8,128)S(1)} %slice.19.refs_0_.refs_1_), channel_id=1, source_target_pairs={{0,3},{1,0},{2,1},{3,2},{4,7},{5,4},{6,5},{7,6},{8,11},{9,8},{10,9... | collective-permute-start | bytes 1179656 | tf_op jit(solution)/shard_map/ppermute | solution.py:483
  87.4 6.4 %collective-permute-start.4 = (f32[24,1024]{1,0:T(8,128)}, f32[24,1024]{1,0:T(8,128)S(1)}, u32[]{:S(2)}, u32[]{:S(2)}) collective-permute-start(f32[24,1024]{1,0:T(8,128)} %add.108.a_ref), channel_id=1, source_target_pairs={{0,8},{8,16},{16,24},{24,0},{1,9},{9,17},{17,25},{25,1},{2,10},{10... | collective-permute-start | bytes 294920 | tf_op jit(solution)/shard_map/ppermute | solution.py:373
  88.7 11.4 %collective-permute-start.5 = (f32[24,1024]{1,0:T(8,128)}, f32[24,1024]{1,0:T(8,128)}, u32[]{:S(2)}, u32[]{:S(2)}) collective-permute-start(f32[24,1024]{1,0:T(8,128)} %add.108.a_ref), channel_id=1, source_target_pairs={{0,16},{8,24},{16,0},{24,8},{1,17},{9,25},{17,1},{25,9},{2,18},{10... | collective-permute-start | bytes 294920 | tf_op jit(solution)/shard_map/ppermute | solution.py:373
  93.9 6.2 %collective-permute-start.6 = (f32[24,1024]{1,0:T(8,128)}, f32[24,1024]{1,0:T(8,128)}, u32[]{:S(2)}, u32[]{:S(2)}) collective-permute-start(f32[24,1024]{1,0:T(8,128)} %add.108.a_ref), channel_id=1, source_target_pairs={{0,24},{8,0},{16,8},{24,16},{1,25},{9,1},{17,9},{25,17},{2,26},{10... | collective-permute-start | bytes 294920 | tf_op jit(solution)/shard_map/ppermute | solution.py:373
  108.7 8.1 %collective-permute-start.11 = (f32[24,1024]{1,0:T(8,128)S(1)}, f32[24,1024]{1,0:T(8,128)S(1)}, u32[]{:S(2)}, u32[]{:S(2)}) collective-permute-start(f32[24,1024]{1,0:T(8,128)S(1)} %add.109.a_ref), channel_id=1, source_target_pairs={{0,8},{8,16},{16,24},{24,0},{1,9},{9,17},{17,25},{25,1},{2,10},{10... | collective-permute-start | bytes 294920 | tf_op jit(solution)/shard_map/ppermute | solution.py:373
  110.0 7.0 %collective-permute-start.12 = (f32[24,1024]{1,0:T(8,128)S(1)}, f32[24,1024]{1,0:T(8,128)S(1)}, u32[]{:S(2)}, u32[]{:S(2)}) collective-permute-start(f32[24,1024]{1,0:T(8,128)S(1)} %add.109.a_ref), channel_id=1, source_target_pairs={{0,16},{8,24},{16,0},{24,8},{1,17},{9,25},{17,1},{25,9},{2,18},{10... | collective-permute-start | bytes 294920 | tf_op jit(solution)/shard_map/ppermute | solution.py:373
  112.3 4.7 %collective-permute-start.13 = (f32[24,1024]{1,0:T(8,128)S(1)}, f32[24,1024]{1,0:T(8,128)S(1)}, u32[]{:S(2)}, u32[]{:S(2)}) collective-permute-start(f32[24,1024]{1,0:T(8,128)S(1)} %add.109.a_ref), channel_id=1, source_target_pairs={{0,24},{8,0},{16,8},{24,16},{1,25},{9,1},{17,9},{25,17},{2,26},{10... | collective-permute-start | bytes 294920 | tf_op jit(solution)/shard_map/ppermute | solution.py:373
  121.9 5.6 %collective-permute-start.15 = (f32[24,1024]{1,0:T(8,128)S(1)}, f32[24,1024]{1,0:T(8,128)S(1)}, u32[]{:S(2)}, u32[]{:S(2)}) collective-permute-start(f32[24,1024]{1,0:T(8,128)S(1)} %add.110.a_ref), channel_id=1, source_target_pairs={{0,8},{8,16},{16,24},{24,0},{1,9},{9,17},{17,25},{25,1},{2,10},{10... | collective-permute-start | bytes 294920 | tf_op jit(solution)/shard_map/ppermute | solution.py:373
  123.1 6.8 %collective-permute-start.16 = (f32[24,1024]{1,0:T(8,128)S(1)}, f32[24,1024]{1,0:T(8,128)S(1)}, u32[]{:S(2)}, u32[]{:S(2)}) collective-permute-start(f32[24,1024]{1,0:T(8,128)S(1)} %add.110.a_ref), channel_id=1, source_target_pairs={{0,16},{8,24},{16,0},{24,8},{1,17},{9,25},{17,1},{25,9},{2,18},{10... | collective-permute-start | bytes 294920 | tf_op jit(solution)/shard_map/ppermute | solution.py:373
  125.3 4.7 %collective-permute-start.17 = (f32[24,1024]{1,0:T(8,128)S(1)}, f32[24,1024]{1,0:T(8,128)S(1)}, u32[]{:S(2)}, u32[]{:S(2)}) collective-permute-start(f32[24,1024]{1,0:T(8,128)S(1)} %add.110.a_ref), channel_id=1, source_target_pairs={{0,24},{8,0},{16,8},{24,16},{1,25},{9,1},{17,9},{25,17},{2,26},{10... | collective-permute-start | bytes 294920 | tf_op jit(solution)/shard_map/ppermute | solution.py:373
  133.3 6.1 %collective-permute-start.19 = (f32[24,1024]{1,0:T(8,128)S(1)}, f32[24,1024]{1,0:T(8,128)S(1)}, u32[]{:S(2)}, u32[]{:S(2)}) collective-permute-start(f32[24,1024]{1,0:T(8,128)S(1)} %add.111.a_ref), channel_id=1, source_target_pairs={{0,8},{8,16},{16,24},{24,0},{1,9},{9,17},{17,25},{25,1},{2,10},{10... | collective-permute-start | bytes 294920 | tf_op jit(solution)/shard_map/ppermute | solution.py:373
  134.8 6.8 %collective-permute-start.20 = (f32[24,1024]{1,0:T(8,128)S(1)}, f32[24,1024]{1,0:T(8,128)S(1)}, u32[]{:S(2)}, u32[]{:S(2)}) collective-permute-start(f32[24,1024]{1,0:T(8,128)S(1)} %add.111.a_ref), channel_id=1, source_target_pairs={{0,16},{8,24},{16,0},{24,8},{1,17},{9,25},{17,1},{25,9},{2,18},{10... | collective-permute-start | bytes 294920 | tf_op jit(solution)/shard_map/ppermute | solution.py:373
  136.9 4.7 %collective-permute-start.21 = (f32[24,1024]{1,0:T(8,128)S(1)}, f32[24,1024]{1,0:T(8,128)S(1)}, u32[]{:S(2)}, u32[]{:S(2)}) collective-permute-start(f32[24,1024]{1,0:T(8,128)S(1)} %add.111.a_ref), channel_id=1, source_target_pairs={{0,24},{8,0},{16,8},{24,16},{1,25},{9,1},{17,9},{25,17},{2,26},{10... | collective-permute-start | bytes 294920 | tf_op jit(solution)/shard_map/ppermute | solution.py:373
  (43 other events, 628.3 us)
Sparse Core Ops, SparseCore 0:
  14.7 47.0 all-gather.6
  63.6 50.7 all-gather.8
  142.5 47.2 all-gather.10

commit v7 on v6

--- a/solution.py
+++ b/solution.py
@@ -523,9 +523,9 @@
         300_000_000,
         1_500_000,
     )(index, spectrum.reshape(LENGTH, 32), quarter)
-    box = [even, odd, slab]
-    tie((parts, (0, 1, 2, 3)), (own, (0, 1, 2, 3)), (box, (0, 1, 2)))
-    even, odd, slab = box
+    box = [even, odd]
+    tie((parts, (0, 1, 2, 3)), (own, (0, 1, 2, 3)), (box, (0, 1)))
+    even, odd = box
     unknowns = []
     work = sides
     pencil = slab
@@ -545,6 +545,10 @@
             inverse_scratch,
             room=56 if panel == 1 else 40,
         )(index, work, *parts, factor_rows(panel, panel - 1), *[own[at] for at in inverses], *unknowns * (panel == 3))
+        if panel == 1:
+            box = [partial, pencil]
+            tie((box, (0, 1)))
+            partial, pencil = box
         unknowns.append(unknown)
         parts = share(partial)
         later = panel < 3

time: 207 us -> 212 us (1.024)
  local copies, waits for them, and re-layouts: 18.8 us -> 24.4 us
    unnamed x79 -> x93, local copies, waits for them, and re-layouts: 14.6 us -> 20.2 us
    ppermute x12, starting transfers between devices: 18.7 us -> 16 us  [share(): lax.ppermute(total, 'x', ring(4, step))]
    all_to_all x1, waiting for transfers between devices: 2.13 us -> 0.01 us  [per_device(): slab = lax.all_to_all(slab, WIDE, 0, 0)]
  transfers between devices with their start and end apart: 28 -> 28, of which waited for: 15 -> 14; matrix products, arithmetic and copies ran while one was open for 3% -> 3% of each run, Pallas kernels for 12% -> 12%
where the time goes in v7:
time: 212 us; the launch traced here: 209 us
  starting transfers between devices  53.3 us (25%)
  waiting for transfers between devices  43.7 us (21%)
  Pallas kernels  36.5 us (17%)
  blocking collectives  33.4 us (16%)
  local copies, waits for them, and re-layouts  24.4 us (12%)
  between operations  14.2 us (7%)
  other arithmetic  3.65 us (2%)
    all_to_all x1, blocking collectives, per_device(): slots = lax.all_to_all(slots, WIDE, 0, 0)  33.4 us
    all_to_all x1, waiting for transfers between devices, per_device(): quarter = lax.all_to_all(quarter, 'z', 0, 0)  24.3 us
    unnamed x93, local copies, waits for them, and re-layouts  20.2 us
    ppermute x12, starting transfers between devices, share(): lax.ppermute(total, 'x', ring(4, step))  16 us
    ppermute x12, waiting for transfers between devices, share(): lax.ppermute(total, 'x', ring(4, step))  9.65 us
    pallas_call x1, Pallas kernels, per_device(): call(filter_kernel, 'filter', [spec(LENGTH, 128)] + obs_specs(3) + [panel...  8.79 us
    all_to_all x1, starting transfers between devices, per_device(): slab = lax.all_to_all(slab, WIDE, 0, 0)  8.54 us
    pallas_call x1, Pallas kernels, update(): call(update_kernel, 'update', [SMEM, pl.BlockSpec((8, 16, 128), lambda i:...  8.23 us
  transfers between devices with their start and end apart: 28, of which 14 were waited for; matrix products, arithmetic and copies ran while one was open for 3% of the time, Pallas kernels for 12%

profile of v7, /device:TPU:1, one launch (start us, length us, event | category | flops | bytes accessed | tf_op | source)
XLA Modules:
  0.0 209.1 jit_solution(4685145759865024220)
XLA Ops:
  10.4 3.4 %copy-done = f32[32,16,4096]{2,1,0:T(8,128)S(1)} copy-done((f32[32,16,4096]{2,1,0:T(8,128)S(1)}, f32[32,16,4096]{2,1,0:T(8,128)}, u32[]{:S(2)}) %copy-start) | copy-done | bytes 8388632
  14.5 6.6 %all-to-all-start = ((f32[8,64,128]{2,1,0:T(8,128)}), f32[8,64,128]{2,1,0:T(8,128)S(1)}, u32[]{:S(2)}, u32[]{:S(2)}) async-start(f32[8,64,128]{2,1,0:T(8,128)} %get-tuple-element.70), calls=%async_computation | async-start | bytes 524288 | tf_op jit(solution)/shard_map/all_to_all | solution.py:432
  21.7 2.6 %collective-permute-start.1 = (f32[64,128]{1,0:T(8,128)S(1)}, f32[64,128]{1,0:T(8,128)S(1)}, u32[]{:S(2)}, u32[]{:S(2)}) collective-permute-start(f32[64,128]{1,0:T(8,128)S(1)} %get-tuple-element.71.refs_0_), channel_id=1, source_target_pairs={{0,2},{1,3},{2,0},{3,1},{4,6},{5,7},{6,4},{7,5},{8,10},{9,11},{10,... | collective-permute-start | bytes 98312 | tf_op jit(solution)/shard_map/ppermute | solution.py:446
  29.5 8.1 %all-to-all-start.1 = ((f32[8,272,128]{2,1,0:T(8,128)}), f32[8,272,128]{2,1,0:T(8,128)S(1)}, u32[]{:S(2)}, u32[]{:S(2)}) async-start(f32[8,272,128]{2,1,0:T(8,128)} %copy-done.15), calls=%async_computation.1 | async-start | bytes 2228224 | tf_op jit(solution)/shard_map/all_to_all | solution.py:460
  37.7 2.2 %reshape.57.noise_ref = f32[128,1024]{1,0:T(8,128)} reshape(f32[16,4,2,1024]{3,2,1,0:T(2,128)} %param.16) | data formatting | bytes 1048576 | tf_op jit(solution)/shard_map/reshape | solution.py:471
  42.6 1.9 noise.1
  45.3 1.7 fusion.3.refs_1_.wave_ref
  47.1 24.3 %all-to-all-done.1.slab_ref.inverse_ref.extra_ref = f32[8,272,128]{2,1,0:T(8,128)S(1)} async-done(((f32[8,272,128]{2,1,0:T(8,128)}), f32[8,272,128]{2,1,0:T(8,128)S(1)}, u32[]{:S(2)}, u32[]{:S(2)}) %all-to-all-start.1) | async-done | bytes 1114144 | tf_op jit(solution)/shard_map/all_to_all | solution.py:460
  71.3 8.5 %all-to-all-start.2 = ((f32[64,16,128]{2,1,0:T(8,128)}), f32[64,16,128]{2,1,0:T(8,128)}, u32[]{:S(2)}, u32[]{:S(2)}) async-start(f32[64,16,128]{2,1,0:T(8,128)} %copy-done.19), calls=%async_computation.2 | async-start | bytes 1048576 | tf_op jit(solution)/shard_map/all_to_all | solution.py:484
  80.6 3.0 %collective-permute-start.8 = (f32[8,96,128]{2,1,0:T(8,128)S(1)}, f32[8,96,128]{2,1,0:T(8,128)S(1)}, u32[]{:S(2)}, u32[]{:S(2)}) collective-permute-start(f32[8,96,128]{2,1,0:T(8,128)S(1)} %slice.19.refs_0_.refs_1_), channel_id=1, source_target_pairs={{0,2},{1,3},{2,0},{3,1},{4,6},{5,7},{6,4},{7,5},{8,10},{9,11},{10,... | collective-permute-start | bytes 1179656 | tf_op jit(solution)/shard_map/ppermute | solution.py:483
  88.0 2.4 %collective-permute-start.5 = (f32[24,1024]{1,0:T(8,128)S(1)}, f32[24,1024]{1,0:T(8,128)}, u32[]{:S(2)}, u32[]{:S(2)}) collective-permute-start(f32[24,1024]{1,0:T(8,128)S(1)} %add.108.a_ref), channel_id=1, source_target_pairs={{0,16},{8,24},{16,0},{24,8},{1,17},{9,25},{17,1},{25,9},{2,18},{10... | collective-permute-start | bytes 294920 | tf_op jit(solution)/shard_map/ppermute | solution.py:373
  90.4 2.7 %collective-permute-done.4.b_ref = f32[24,1024]{1,0:T(8,128)S(1)} collective-permute-done((f32[24,1024]{1,0:T(8,128)S(1)}, f32[24,1024]{1,0:T(8,128)S(1)}, u32[]{:S(2)}, u32[]{:S(2)}) %collective-permute-start.4) | collective-permute-done | bytes 98336 | tf_op jit(solution)/shard_map/ppermute | solution.py:373
  95.3 2.4 %spectrum.1 = (f32[1024,128]{1,0:T(8,128)S(1)}, f32[512,128]{1,0:T(8,128)S(1)}) custom-call(s32[2]{0:T(128)S(1)} %pad_add_fusion.index_ref, f32[1024,32]{1,0:T(8,128)S(1)} %copy.15.spectrum_ref, f32[8,272,128]{2,1,0:T(8,128)S(1)} %all-to-all-done.1.slab_ref.inverse_ref.extra_ref), custom_call_target="tpu_custom_call" | custom-call | flops 300000000 | bytes 1500000 | tf_op jit(solution)/shard_map/spectrum/pallas_call | solution.py:517
  101.7 2.6 %step1.1 = (f32[24,1024]{1,0:T(8,128)}, f32[24,1024]{1,0:T(8,128)}) custom-call(s32[2]{0:T(128)} %copy-done.37, f32[4,24,128]{2,1,0:T(8,128)} %copy-done.28, f32[24,1024]{1,0:T(8,128)} %copy-done.40, f32[24,1024]{1,0:T(8,128)} %copy-done.44, f32[24,1024]{1,0:T(8,128)} %collective-permute-done.5.c_ref, f32[24,1024]{1,0:T(8,128)} %collective-permute-done.6.d_ref, ...), custom_call_target="tpu_custom_call" | custom-call | flops 40000000 | bytes 1500000 | tf_op jit(solution)/shard_map/step1/pallas_call | solution.py:533
  109.2 2.4 %collective-permute-start.12 = (f32[24,1024]{1,0:T(8,128)S(1)}, f32[24,1024]{1,0:T(8,128)S(1)}, u32[]{:S(2)}, u32[]{:S(2)}) collective-permute-start(f32[24,1024]{1,0:T(8,128)S(1)} %add.109.a_ref), channel_id=1, source_target_pairs={{0,16},{8,24},{16,0},{24,8},{1,17},{9,25},{17,1},{25,9},{2,18},{10... | collective-permute-start | bytes 294920 | tf_op jit(solution)/shard_map/ppermute | solution.py:373
  114.7 2.4 %wait1.1 = (f32[1024,128]{1,0:T(8,128)S(1)}, f32[1,24,128]{2,1,0:T(8,128)S(1)}) custom-call(s32[1,4096]{1,0:T(1,128)S(1)} %bitcast.19, f32[16,4096]{1,0:T(8,128)S(1)} %copy-done.17, f32[2,4096]{1,0:T(2,128)S(1)} %add_convert_fusion.refs_2_.plane_ref, f32[64,16,128]{2,1,0:T(8,128)} %all-to-all-done.2.refs_3_, f32[24,1024]{1,0:T(8,128)S(1)} %copy-done.22, ...), custom_call_target="tpu_custom_call" | custom-call | flops 536870912 | bytes 1500000 | tf_op jit(solution)/shard_map/wait1/pallas_call | solution.py:556
  129.8 3.6 %collective-permute-done.15.b_ref = f32[24,1024]{1,0:T(8,128)S(1)} collective-permute-done((f32[24,1024]{1,0:T(8,128)S(1)}, f32[24,1024]{1,0:T(8,128)S(1)}, u32[]{:S(2)}, u32[]{:S(2)}) %collective-permute-start.15) | collective-permute-done | bytes 98336 | tf_op jit(solution)/shard_map/ppermute | solution.py:373
  137.3 3.3 %collective-permute-start.20 = (f32[24,1024]{1,0:T(8,128)S(1)}, f32[24,1024]{1,0:T(8,128)S(1)}, u32[]{:S(2)}, u32[]{:S(2)}) collective-permute-start(f32[24,1024]{1,0:T(8,128)S(1)} %add.111.a_ref), channel_id=1, source_target_pairs={{0,16},{8,24},{16,0},{24,8},{1,17},{9,25},{17,1},{25,9},{2,18},{10... | collective-permute-start | bytes 294920 | tf_op jit(solution)/shard_map/ppermute | solution.py:373
  142.5 2.8 %collective-permute-done.20.c_ref = f32[24,1024]{1,0:T(8,128)S(1)} collective-permute-done((f32[24,1024]{1,0:T(8,128)S(1)}, f32[24,1024]{1,0:T(8,128)S(1)}, u32[]{:S(2)}, u32[]{:S(2)}) %collective-permute-start.20) | collective-permute-done | bytes 98336 | tf_op jit(solution)/shard_map/ppermute | solution.py:373
  146.1 8.8 %filter.1 = f32[64,16,128]{2,1,0:T(8,128)} custom-call(f32[1024,128]{1,0:T(8,128)} %copy-done.27, s32[1,4096]{1,0:T(1,128)} %bitcast.22, f32[16,4096]{1,0:T(8,128)} %fusion.3.refs_1_.wave_ref, f32[2,4096]{1,0:T(2,128)} %copy-done.23, f32[24,1024]{1,0:T(8,128)} %copy-done.39, f32[24,1024]{1,0:T(8,128)} %copy-done.41, f32[24,1024]{1,0:T(8,128)} %copy-done.42, ...), custom_call_target="tpu_custom_call" | custom-call | flops 2147483648 | bytes 11000000 | tf_op jit(solution)/shard_map/filter/pallas_call | solution.py:576
  154.9 33.4 %all_to_all.20.slots_ref = f32[64,16,128]{2,1,0:T(8,128)S(1)} all-to-all(f32[64,16,128]{2,1,0:T(8,128)} %filter.1), channel_id=1, replica_groups=mesh['z'=8,'x'=4,'core'=2,'y'=4] {'z','x','core'}, dimensions={0} | all-to-all | bytes 1048576 | tf_op jit(solution)/shard_map/all_to_all | solution.py:593
  188.3 3.1 %close.1 = f32[16,4,2,1024]{3,2,1,0:T(2,128)} custom-call(f32[64,16,128]{2,1,0:T(8,128)S(1)} %all_to_all.20.slots_ref, bf16[1024,1024]{1,0:T(8,128)(2,1)S(1)} %copy-done.12, bf16[1024,1024]{1,0:T(8,128)(2,1)S(1)} %copy-done.14), custom_call_target="tpu_custom_call" | custom-call | flops 805306368 | bytes 5500000 | tf_op jit(solution)/shard_map/close/pallas_call | solution.py:594
  191.4 2.9 %all-gather.11.cloned.1.call-done = f32[512,1024]{1,0:T(8,128)} async-done(((f32[64,1024]{1,0:T(8,128)}), f32[512,1024]{1,0:T(8,128)}) %all-gather.11.cloned.1.call-update) | async-done | bytes 2097168 | tf_op jit(solution)/shard_map/all_gather | solution.py:592
  194.3 8.2 %update.1 = f32[32,16,128]{2,1,0:T(8,128)} custom-call(s32[2]{0:T(128)} %copy-done.37, f32[32,16,128]{2,1,0:T(8,128)} %base_ref, f32[8,64,1024]{2,1,0:T(8,128)} %bitcast.24, f32[32,16,4096]{2,1,0:T(8,128)} %refs_3_, f32[32,16,4096]{2,1,0:T(8,128)} %refs_3_, f32[32,16,4096]{2,1,0:T(8,128)} %refs_3_, f32[32,16,4096]{2,1,0:T(8,128)} %refs_3_), custom_call_target="tpu_custom_call" | custom-call | flops 1610612736 | bytes 11000000 | tf_op jit(solution)/shard_map/update/pallas_call | solution.py:385
  (164 shorter events, 51.6 us)
Async XLA Ops:
  7.2 93.6 %all-gather.7.cloned.1.call-start = ((), (), s32[]{:S(2)}) async-start(), calls=%async_computation.4 | async-start | bytes 1179648 | tf_op jit(solution)/shard_map/all_gather | solution.py:444
  14.5 13.1 %all-to-all-start = ((f32[8,64,128]{2,1,0:T(8,128)}), f32[8,64,128]{2,1,0:T(8,128)S(1)}, u32[]{:S(2)}, u32[]{:S(2)}) async-start(f32[8,64,128]{2,1,0:T(8,128)} %get-tuple-element.70), calls=%async_computation | async-start | bytes 524288 | tf_op jit(solution)/shard_map/all_to_all | solution.py:432
  21.1 98.0 %all-gather.9.cloned.1.call-start = ((), (), s32[]{:S(2)}) async-start(), calls=%async_computation.5 | async-start | bytes 2359296 | tf_op jit(solution)/shard_map/all_gather | solution.py:459
  21.1 5.3 %collective-permute-start = (f32[64,128]{1,0:T(8,128)S(1)}, f32[64,128]{1,0:T(8,128)S(1)}, u32[]{:S(2)}, u32[]{:S(2)}) collective-permute-start(f32[64,128]{1,0:T(8,128)S(1)} %get-tuple-element.71.refs_0_), channel_id=1, source_target_pairs={{0,1},{1,2},{2,3},{3,0},{4,5},{5,6},{6,7},{7,4},{8,9},{9,10},{10,1... | collective-permute-start | bytes 98312 | tf_op jit(solution)/shard_map/ppermute | solution.py:446
  21.7 4.7 %collective-permute-start.1 = (f32[64,128]{1,0:T(8,128)S(1)}, f32[64,128]{1,0:T(8,128)S(1)}, u32[]{:S(2)}, u32[]{:S(2)}) collective-permute-start(f32[64,128]{1,0:T(8,128)S(1)} %get-tuple-element.71.refs_0_), channel_id=1, source_target_pairs={{0,2},{1,3},{2,0},{3,1},{4,6},{5,7},{6,4},{7,5},{8,10},{9,11},{10,... | collective-permute-start | bytes 98312 | tf_op jit(solution)/shard_map/ppermute | solution.py:446
  24.3 3.1 %collective-permute-start.2 = (f32[64,128]{1,0:T(8,128)S(1)}, f32[64,128]{1,0:T(8,128)S(1)}, u32[]{:S(2)}, u32[]{:S(2)}) collective-permute-start(f32[64,128]{1,0:T(8,128)S(1)} %get-tuple-element.71.refs_0_), channel_id=1, source_target_pairs={{0,3},{1,0},{2,1},{3,2},{4,7},{5,4},{6,5},{7,6},{8,11},{9,8},{10,9... | collective-permute-start | bytes 98312 | tf_op jit(solution)/shard_map/ppermute | solution.py:446
  29.5 41.8 %all-to-all-start.1 = ((f32[8,272,128]{2,1,0:T(8,128)}), f32[8,272,128]{2,1,0:T(8,128)S(1)}, u32[]{:S(2)}, u32[]{:S(2)}) async-start(f32[8,272,128]{2,1,0:T(8,128)} %copy-done.15), calls=%async_computation.1 | async-start | bytes 2228224 | tf_op jit(solution)/shard_map/all_to_all | solution.py:460
  71.3 33.0 %all-to-all-start.2 = ((f32[64,16,128]{2,1,0:T(8,128)}), f32[64,16,128]{2,1,0:T(8,128)}, u32[]{:S(2)}, u32[]{:S(2)}) async-start(f32[64,16,128]{2,1,0:T(8,128)} %copy-done.19), calls=%async_computation.2 | async-start | bytes 1048576 | tf_op jit(solution)/shard_map/all_to_all | solution.py:484
  79.9 114.4 %all-gather.11.cloned.1.call-start = ((), (), s32[]{:S(2)}) async-start(), calls=%async_computation.6 | async-start | bytes 2359296 | tf_op jit(solution)/shard_map/all_gather | solution.py:592
  80.0 19.2 %collective-permute-start.7 = (f32[8,96,128]{2,1,0:T(8,128)S(1)}, f32[8,96,128]{2,1,0:T(8,128)S(1)}, u32[]{:S(2)}, u32[]{:S(2)}) collective-permute-start(f32[8,96,128]{2,1,0:T(8,128)S(1)} %slice.19.refs_0_.refs_1_), channel_id=1, source_target_pairs={{0,1},{1,2},{2,3},{3,0},{4,5},{5,6},{6,7},{7,4},{8,9},{9,10},{10,1... | collective-permute-start | bytes 1179656 | tf_op jit(solution)/shard_map/ppermute | solution.py:483
  80.6 20.2 %collective-permute-start.8 = (f32[8,96,128]{2,1,0:T(8,128)S(1)}, f32[8,96,128]{2,1,0:T(8,128)S(1)}, u32[]{:S(2)}, u32[]{:S(2)}) collective-permute-start(f32[8,96,128]{2,1,0:T(8,128)S(1)} %slice.19.refs_0_.refs_1_), channel_id=1, source_target_pairs={{0,2},{1,3},{2,0},{3,1},{4,6},{5,7},{6,4},{7,5},{8,10},{9,11},{10,... | collective-permute-start | bytes 1179656 | tf_op jit(solution)/shard_map/ppermute | solution.py:483
  83.5 17.2 %collective-permute-start.9 = (f32[8,96,128]{2,1,0:T(8,128)S(1)}, f32[8,96,128]{2,1,0:T(8,128)S(1)}, u32[]{:S(2)}, u32[]{:S(2)}) collective-permute-start(f32[8,96,128]{2,1,0:T(8,128)S(1)} %slice.19.refs_0_.refs_1_), channel_id=1, source_target_pairs={{0,3},{1,0},{2,1},{3,2},{4,7},{5,4},{6,5},{7,6},{8,11},{9,8},{10,9... | collective-permute-start | bytes 1179656 | tf_op jit(solution)/shard_map/ppermute | solution.py:483
  86.8 6.4 %collective-permute-start.4 = (f32[24,1024]{1,0:T(8,128)S(1)}, f32[24,1024]{1,0:T(8,128)S(1)}, u32[]{:S(2)}, u32[]{:S(2)}) collective-permute-start(f32[24,1024]{1,0:T(8,128)S(1)} %add.108.a_ref), channel_id=1, source_target_pairs={{0,8},{8,16},{16,24},{24,0},{1,9},{9,17},{17,25},{25,1},{2,10},{10... | collective-permute-start | bytes 294920 | tf_op jit(solution)/shard_map/ppermute | solution.py:373
  88.0 11.2 %collective-permute-start.5 = (f32[24,1024]{1,0:T(8,128)S(1)}, f32[24,1024]{1,0:T(8,128)}, u32[]{:S(2)}, u32[]{:S(2)}) collective-permute-start(f32[24,1024]{1,0:T(8,128)S(1)} %add.108.a_ref), channel_id=1, source_target_pairs={{0,16},{8,24},{16,0},{24,8},{1,17},{9,25},{17,1},{25,9},{2,18},{10... | collective-permute-start | bytes 294920 | tf_op jit(solution)/shard_map/ppermute | solution.py:373
  93.2 6.0 %collective-permute-start.6 = (f32[24,1024]{1,0:T(8,128)S(1)}, f32[24,1024]{1,0:T(8,128)}, u32[]{:S(2)}, u32[]{:S(2)}) collective-permute-start(f32[24,1024]{1,0:T(8,128)S(1)} %add.108.a_ref), channel_id=1, source_target_pairs={{0,24},{8,0},{16,8},{24,16},{1,25},{9,1},{17,9},{25,17},{2,26},{10... | collective-permute-start | bytes 294920 | tf_op jit(solution)/shard_map/ppermute | solution.py:373
  107.8 10.1 %collective-permute-start.11 = (f32[24,1024]{1,0:T(8,128)S(1)}, f32[24,1024]{1,0:T(8,128)S(1)}, u32[]{:S(2)}, u32[]{:S(2)}) collective-permute-start(f32[24,1024]{1,0:T(8,128)S(1)} %add.109.a_ref), channel_id=1, source_target_pairs={{0,8},{8,16},{16,24},{24,0},{1,9},{9,17},{17,25},{25,1},{2,10},{10... | collective-permute-start | bytes 294920 | tf_op jit(solution)/shard_map/ppermute | solution.py:373
  109.2 8.6 %collective-permute-start.12 = (f32[24,1024]{1,0:T(8,128)S(1)}, f32[24,1024]{1,0:T(8,128)S(1)}, u32[]{:S(2)}, u32[]{:S(2)}) collective-permute-start(f32[24,1024]{1,0:T(8,128)S(1)} %add.109.a_ref), channel_id=1, source_target_pairs={{0,16},{8,24},{16,0},{24,8},{1,17},{9,25},{17,1},{25,9},{2,18},{10... | collective-permute-start | bytes 294920 | tf_op jit(solution)/shard_map/ppermute | solution.py:373
  111.6 6.9 %collective-permute-start.13 = (f32[24,1024]{1,0:T(8,128)S(1)}, f32[24,1024]{1,0:T(8,128)S(1)}, u32[]{:S(2)}, u32[]{:S(2)}) collective-permute-start(f32[24,1024]{1,0:T(8,128)S(1)} %add.109.a_ref), channel_id=1, source_target_pairs={{0,24},{8,0},{16,8},{24,16},{1,25},{9,1},{17,9},{25,17},{2,26},{10... | collective-permute-start | bytes 294920 | tf_op jit(solution)/shard_map/ppermute | solution.py:373
  125.8 7.6 %collective-permute-start.15 = (f32[24,1024]{1,0:T(8,128)S(1)}, f32[24,1024]{1,0:T(8,128)S(1)}, u32[]{:S(2)}, u32[]{:S(2)}) collective-permute-start(f32[24,1024]{1,0:T(8,128)S(1)} %add.110.a_ref), channel_id=1, source_target_pairs={{0,8},{8,16},{16,24},{24,0},{1,9},{9,17},{17,25},{25,1},{2,10},{10... | collective-permute-start | bytes 294920 | tf_op jit(solution)/shard_map/ppermute | solution.py:373
  126.2 7.2 %collective-permute-start.16 = (f32[24,1024]{1,0:T(8,128)S(1)}, f32[24,1024]{1,0:T(8,128)S(1)}, u32[]{:S(2)}, u32[]{:S(2)}) collective-permute-start(f32[24,1024]{1,0:T(8,128)S(1)} %add.110.a_ref), channel_id=1, source_target_pairs={{0,16},{8,24},{16,0},{24,8},{1,17},{9,25},{17,1},{25,9},{2,18},{10... | collective-permute-start | bytes 294920 | tf_op jit(solution)/shard_map/ppermute | solution.py:373
  127.0 6.6 %collective-permute-start.17 = (f32[24,1024]{1,0:T(8,128)S(1)}, f32[24,1024]{1,0:T(8,128)S(1)}, u32[]{:S(2)}, u32[]{:S(2)}) collective-permute-start(f32[24,1024]{1,0:T(8,128)S(1)} %add.110.a_ref), channel_id=1, source_target_pairs={{0,24},{8,0},{16,8},{24,16},{1,25},{9,1},{17,9},{25,17},{2,26},{10... | collective-permute-start | bytes 294920 | tf_op jit(solution)/shard_map/ppermute | solution.py:373
  137.2 5.3 %collective-permute-start.19 = (f32[24,1024]{1,0:T(8,128)S(1)}, f32[24,1024]{1,0:T(8,128)S(1)}, u32[]{:S(2)}, u32[]{:S(2)}) collective-permute-start(f32[24,1024]{1,0:T(8,128)S(1)} %add.111.a_ref), channel_id=1, source_target_pairs={{0,8},{8,16},{16,24},{24,0},{1,9},{9,17},{17,25},{25,1},{2,10},{10... | collective-permute-start | bytes 294920 | tf_op jit(solution)/shard_map/ppermute | solution.py:373
  137.3 7.9 %collective-permute-start.20 = (f32[24,1024]{1,0:T(8,128)S(1)}, f32[24,1024]{1,0:T(8,128)S(1)}, u32[]{:S(2)}, u32[]{:S(2)}) collective-permute-start(f32[24,1024]{1,0:T(8,128)S(1)} %add.111.a_ref), channel_id=1, source_target_pairs={{0,16},{8,24},{16,0},{24,8},{1,17},{9,25},{17,1},{25,9},{2,18},{10... | collective-permute-start | bytes 294920 | tf_op jit(solution)/shard_map/ppermute | solution.py:373
  140.6 4.7 %collective-permute-start.21 = (f32[24,1024]{1,0:T(8,128)S(1)}, f32[24,1024]{1,0:T(8,128)S(1)}, u32[]{:S(2)}, u32[]{:S(2)}) collective-permute-start(f32[24,1024]{1,0:T(8,128)S(1)} %add.111.a_ref), channel_id=1, source_target_pairs={{0,24},{8,0},{16,8},{24,16},{1,25},{9,1},{17,9},{25,17},{2,26},{10... | collective-permute-start | bytes 294920 | tf_op jit(solution)/shard_map/ppermute | solution.py:373
  (50 other events, 584.9 us)
Sparse Core Ops, SparseCore 0:
  14.7 47.0 all-gather.6
  63.5 50.5 all-gather.8
  146.2 48.0 all-gather.10
